TPU v7x, 32 devices: a whole 2x2x4 slice. The times are simulated.
32 devices in a mesh: rows: 16 (over z, y, core), chan: 2 (over x).
Axes of the slice: x: 2, y: 2, z: 4, core: 2. Of those that a mesh axis runs over, the one named last changes fastest.
Arguments:
- frame_one: bfloat16 [4096, 256], P('rows', 'chan'), may hold values from -6 to 6
- frame_two: bfloat16 [128, 480, 256], P('rows', None, 'chan'), may hold values from -6 to 6
Outputs:
- pyramid: bfloat16 [16, 5040, 4096], P(None, 'chan', 'rows')
All inputs are finite; a program needn't handle non-finite values.
Results may differ from a plain program's by a relative error of at most 0.0016.
Values may be sent and summed in bfloat16 or wider, within the bound.
No kernel may reach another device: no remote copies, remote signals or barrier semaphores. Data moves between devices by JAX's collectives and lax.ppermute only.
A program may use at most 128 MiB of HBM per device.

v0:
```python
import functools

import jax
import jax.numpy as jnp
from jax import lax
from jax.experimental import pallas as pl
from jax.experimental.pallas import tpu as pltpu
from jax.sharding import PartitionSpec as P

LANES = 128
PARAMS = {'LAG': 2, 'F0': 10, 'F1': 0, 'PS0': 1, 'JA': 3, 'JB': 1, 'C0POS': 2, 'GATE': 30, 'F3': 10, 'F2': 22, 'NL': 0, 'PE4': 0, 'CP2': 1, 'P4': 0, 'P3': 1, 'X00': 10, 'X01': 10, 'C0': 10, 'X10': 10, 'X11': 10, 'C1': 10, 'X20': 10, 'X21': 10, 'C2': 10, 'X30': 10, 'X31': 10, 'C3': 10, 'X40': 10, 'X41': 10, 'C4': 10}


def G(name):
    return PARAMS.get(name, 0)


VMEM_BYTES = 28 * 1024 * 1024


def pool_strip(strip):
    full = strip.astype(jnp.float32)
    rows_n, cols_n, chans = full.shape
    level_one = full.reshape(rows_n // 2, 2, cols_n // 2, 2, chans).mean(axis=(1, 3))
    level_two = level_one.reshape(rows_n // 4, 2, cols_n // 4, 2, chans).mean(axis=(1, 3))
    joined = jnp.concatenate(
        [full.reshape(-1, chans), level_one.reshape(-1, chans), level_two.reshape(-1, chans)],
        axis=0,
    )
    return joined.astype(jnp.bfloat16)


def gather_local(frame_one, frame_two):
    groups = lax.axis_size("chan")
    queries = lax.all_gather(frame_one, "chan", axis=0, tiled=False)
    channels = queries.shape[0] * queries.shape[2]
    factor = 1.0 / jnp.sqrt(jnp.float32(channels))
    pooled = pool_strip(frame_two)
    share = pooled.shape[0] // groups
    traded = lax.all_to_all(
        pooled.reshape(groups, share, pooled.shape[1]), "chan", split_axis=0, concat_axis=0, tiled=True
    )
    gathered = lax.all_gather(traded, "rows", axis=0, tiled=False)
    values = jnp.einsum("skpc,kqc->spq", gathered, queries, preferred_element_type=jnp.float32)
    return (values * factor).astype(jnp.bfloat16)


def pooled_levels(half, sums, sums_two):
    rows_n, cols_n, _ = half.shape
    means = []
    for row in range(rows_n // 2):
        sums[row] = half[2 * row].astype(jnp.float32) + half[2 * row + 1].astype(jnp.float32)
        left = sums[row, pl.ds(0, cols_n // 2, stride=2), :]
        right = sums[row, pl.ds(1, cols_n // 2, stride=2), :]
        means.append((left + right) * 0.25)
    means_two = []
    for row in range(rows_n // 4):
        sums_two[row] = means[2 * row] + means[2 * row + 1]
        left = sums_two[row, pl.ds(0, cols_n // 4, stride=2), :]
        right = sums_two[row, pl.ds(1, cols_n // 4, stride=2), :]
        means_two.append((left + right) * 0.25)
    return jnp.concatenate(means + means_two, axis=0)


def strips_in(refs):
    return [ref.at[index] for ref in refs for index in range(ref.shape[0])]


def extra_kernel(pieces, results, flip, meta, *refs):
    halves = strips_in(refs[:pieces])
    extra, sums, sums_two = refs[-2 - results], *refs[-2:]
    count, cols_n = extra.shape[1], halves[0].shape[1]
    upper = meta[0] == (1 if flip else 0)

    @pl.when(upper)
    def _():
        for index, half in enumerate(halves):
            extra[index] = pooled_levels(half, sums, sums_two).astype(extra.dtype)

    @pl.when(jnp.logical_not(upper))
    def _():
        for index, half in enumerate(halves):
            parts, left, row = [], count, 0
            while left > 0:
                parts.append(half[row].astype(jnp.float32)[: min(left, cols_n)])
                left, row = left - cols_n, row + 1
            extra[index] = jnp.concatenate(parts, axis=0).astype(extra.dtype)


def chunks(segments, step):
    todo, runs = list(segments), []
    while todo:
        run, room = [], step
        while todo and room > 0:
            ref, first, last = todo.pop(0)
            take = min(room, last - first)
            run.append((ref, first, first + take))
            room -= take
            if first + take < last:
                todo.insert(0, (ref, first + take, last))
        runs.append(run)
    return runs


def joined(run):
    parts = [ref[first:last].astype(jnp.float32) for ref, first, last in run]
    return parts[0] if len(parts) == 1 else jnp.concatenate(parts, axis=0)


def corr_kernel(factor, pieces, wide, slots, landing, pins, meta, *refs):
    own, other = strips_in(refs[: pieces[0]]), strips_in(refs[pieces[0] : sum(pieces[:2])])
    refs = refs[sum(pieces[:2]) :]
    came_own, came_other = strips_in(refs[: pieces[2]]), strips_in(refs[pieces[2] : pieces[2] + pieces[3]])
    queries, *refs = refs[pieces[2] + pieces[3] :]
    landed = refs.pop(0) if landing else None
    out, *refs = refs[1 + pins :]
    pair = refs.pop(0) if wide else None
    done, values, sums, sums_two, sems, land_sems = refs
    rows_n, cols_n, _ = own[0].shape
    count, width = came_own[0].shape[0], done.shape[2]
    raw = rows_n * cols_n
    ones = (rows_n // 2) * (cols_n // 2)

    copies = []
    for index, slot in enumerate(landing):
        copies.append(pltpu.make_async_copy(landed.at[index], out.at[meta[slot]], land_sems.at[index]))
        copies[-1].start()

    def times(left):
        return jnp.dot(left, queries[...], preferred_element_type=jnp.float32) * factor

    def store(index, at, part):
        done[index, at : at + part.shape[0]] = part[:, :width].astype(done.dtype)
        if wide:
            pair[index, at : at + part.shape[0]] = part[:, width:].astype(done.dtype)

    for index in range(len(own)):

        def raw_row(row):
            return jnp.concatenate([own[index][row], other[index][row]], axis=1)

        def came_rows():
            return jnp.concatenate([came_own[index][...], came_other[index][...]], axis=1)

        @pl.when(meta[0] == 0)
        def _():
            for row in range(rows_n):
                store(index, row * cols_n, times(raw_row(row)))
            store(index, raw, times(came_rows()))

        @pl.when(meta[0] != 0)
        def _():
            for row in range(count // cols_n, rows_n):
                values[row * cols_n : (row + 1) * cols_n] = times(raw_row(row))
            values[raw : raw + count] = times(came_rows())
            levels = [pooled_levels(half[index], sums, sums_two).astype(done.dtype) for half in (own, other)]
            lower = raw + count
            values[lower : lower + count] = times(jnp.concatenate(levels, axis=1))
            segments = [
                (values, count, raw),
                (values, raw, raw + ones),
                (values, lower, lower + ones),
                (values, raw + ones, raw + count),
                (values, lower + ones, lower + count),
            ]
            step = cols_n // 2
            for at, run in enumerate(chunks(segments, step)):
                store(index, at * step, joined(run))

        copies.append(pltpu.make_async_copy(done.at[index], out.at[meta[slots[index]]], sems.at[index]))
        copies[-1].start()
    for copy in copies:
        copy.wait()


def gate_kernel(*refs):
    pass


def first_open_row(total, raw):
    return (2 * raw - total) // 16 * 16


def raw_kernel(factor, arrays, wide, landing, leaving, slots, meta, *refs):
    own, other = strips_in(refs[:arrays]), strips_in(refs[arrays : 2 * arrays])
    queries, *refs = refs[2 * arrays :]
    landed = refs.pop(0) if landing else None
    leavers, refs = refs[: len(leaving)], refs[len(leaving) :]
    _, out, done, *refs = refs
    pair = refs.pop(0) if wide else None
    values, sums, sums_two, land_sems, sems = refs
    rows_n, cols_n, _ = own[0].shape
    count, width = done.shape[1] - rows_n * cols_n, done.shape[2]
    raw = rows_n * cols_n
    ones = (rows_n // 2) * (cols_n // 2)

    copies = []
    for index, slot in enumerate(landing):
        copies.append(pltpu.make_async_copy(landed.at[index], out.at[meta[slot]], land_sems.at[index]))
        copies[-1].start()
    total, cut = done.shape[1], first_open_row(done.shape[1], rows_n * cols_n)
    slots = list(slots)

    def leave(strip, whole):
        rows = pl.ds(0, total if whole else cut)
        number = len(copies) - len(landing)
        copies.append(pltpu.make_async_copy(strip.at[rows], out.at[meta[slots.pop(0)], rows], sems.at[number]))
        copies[-1].start()

    for strips, whole in zip(leavers, leaving):
        for index in range(strips.shape[0] if whole is not None else 0):
            leave(strips.at[index], whole)

    def times(left):
        return jnp.dot(left, queries[...], preferred_element_type=jnp.float32) * factor

    def store(index, at, part):
        done[index, at : at + part.shape[0]] = part[:, :width].astype(done.dtype)
        if wide:
            pair[index, at : at + part.shape[0]] = part[:, width:].astype(done.dtype)

    for index, halves in enumerate(zip(own, other)):

        def raw_row(row):
            return jnp.concatenate([half[row] for half in halves], axis=1)

        @pl.when(meta[0] == 0)
        def _():
            for row in range(rows_n):
                store(index, row * cols_n, times(raw_row(row)))
            store(index, raw, jnp.zeros((count, values.shape[1]), jnp.float32))

        @pl.when(meta[0] != 0)
        def _():
            for row in range(count // cols_n, rows_n):
                values[row * cols_n : (row + 1) * cols_n] = times(raw_row(row))
            levels = [pooled_levels(half, sums, sums_two).astype(done.dtype) for half in halves]
            values[raw : raw + count] = times(jnp.concatenate(levels, axis=1))
            segments = [
                (values, count, raw),
                (values, raw, raw + ones),
                (values, raw, raw + ones),
                (values, raw + ones, raw + count),
                (values, raw + ones, raw + count),
            ]
            step = cols_n // 2
            for at, run in enumerate(chunks(segments, step)):
                store(index, at * step, joined(run))

        if slots:
            leave(done.at[index], False)
    for copy in copies:
        copy.wait()


def came_kernel(factor, arrays, wide, late, pins, slots, late_whole, meta, *refs):
    own, other = strips_in(refs[:arrays]), strips_in(refs[arrays : 2 * arrays])
    queries, *refs = refs[2 * arrays :]
    late_rows = refs.pop(0) if late else None
    refs = refs[2 + late + pins :]
    out, done, *refs = refs
    late_done = refs.pop(0) if late else None
    pair = refs.pop(0) if wide else None
    values, sems = refs
    count, width = own[0].shape[0], done.shape[2]
    raw = done.shape[1] - count
    ones = count * 4 // 5
    copies = []

    def leave(strip, whole=False):
        if slots:
            cut = 0 if whole else first_open_row(raw + count, raw)
            rows = pl.ds(cut, raw + count - cut)
            slot = meta[slots[len(copies)]]
            copies.append(pltpu.make_async_copy(strip.at[rows], out.at[slot, rows], sems.at[len(copies)]))
            copies[-1].start()

    def merge(strip, part):
        @pl.when(meta[0] == 0)
        def _():
            strip[raw : raw + count] = part.astype(done.dtype)

        @pl.when(meta[0] != 0)
        def _():
            values[...] = part
            at = raw - count
            for first, last, into in ((0, ones, at), (ones, count, at + 2 * ones)):
                start = into // 16 * 16
                end = -(-(into + last - first) // 16) * 16
                parts = [values[first:last]]
                if start < into:
                    parts.insert(0, strip[start : start + 16].astype(jnp.float32)[: into - start])
                over = end - (into + last - first)
                if over:
                    parts.append(strip[end - 16 : end].astype(jnp.float32)[16 - over :])
                strip[start:end] = jnp.concatenate(parts, axis=0).astype(done.dtype)

    if late:
        for index in range(late_done.shape[0]):
            merge(late_done.at[index], late_rows[index].astype(jnp.float32))
            leave(late_done.at[index], late_whole)
    for index, halves in enumerate(zip(own, other)):
        left = jnp.concatenate([half[...] for half in halves], axis=1)
        part = jnp.dot(left, queries[...], preferred_element_type=jnp.float32) * factor
        if wide:
            pair[index] = part[:, width:].astype(done.dtype)
        merge(done.at[index], part[:, :width])
        leave(done.at[index])
    for copy in copies:
        copy.wait()


def ring_local(frame_one, frame_two):
    rows_axis = lax.axis_size("rows")
    rows_n, cols_n, chans = frame_two.shape
    queries_n = frame_one.shape[0]
    half_rows = rows_n // 2
    raw = half_rows * cols_n
    count = (half_rows // 2) * (cols_n // 2) + (half_rows // 4) * (cols_n // 4)
    factor = float(1.0 / (2 * chans) ** 0.5)
    me, side = lax.axis_index("rows"), lax.axis_index("chan")

    chips = rows_axis // 2
    columns, half_way = chips // 2, chips // 2
    order = [2 * z for z in range(columns)] + [2 * z + 1 for z in reversed(range(columns))]
    ring = [(2 * order[p], 2 * order[(p + 1) % chips]) for p in range(chips)]
    ring += [(2 * order[p] + 1, 2 * order[p - 1] + 1) for p in range(chips)]
    swap = [(r, r ^ 1) for r in range(rows_axis)]
    across = [(0, 1), (1, 0)]

    core, column, line = me % 2, me // 4, (me // 2) % 2
    place = jnp.where(line == 0, column, chips - 1 - column)
    steps = jnp.arange(half_way + 1, dtype=jnp.int32)

    def strips_of(c):
        p = (place + jnp.where(c == 0, -steps, steps)) % chips
        chip = jnp.where(p < columns, 2 * p, 2 * (chips - 1 - p) + 1)
        return [2 * chip + c, 2 * chip + 1 - c]

    meta = jnp.concatenate([side[None], *strips_of(core), *strips_of(1 - core)]).astype(jnp.int32)

    def slots_of(d, other_core):
        first = 1 + (2 * other_core) * (half_way + 1) + d
        return (first,) if d in (0, half_way) else (first, first + half_way + 1)

    in_vmem = pl.BlockSpec(memory_space=pltpu.VMEM)
    anywhere = pl.BlockSpec(memory_space=pl.ANY)
    scalars = pl.BlockSpec(memory_space=pltpu.SMEM)
    out_type = jax.ShapeDtypeStruct((rows_axis, raw + count, queries_n), frame_two.dtype)
    pooling = [
        pltpu.VMEM((half_rows // 2, cols_n, chans), jnp.float32),
        pltpu.VMEM((half_rows // 4, cols_n // 2, chans), jnp.float32),
    ]
    params = pltpu.CompilerParams(vmem_limit_bytes=VMEM_BYTES)
    def modelled(us):
        return pl.CostEstimate(flops=int(us * 10**9) + 1000, bytes_accessed=1000, transcendentals=0)


    def make_extra(out, halves, cost=0, pins=(), flip=False, carry=False, passed=None):
        strips = sum(half.shape[0] for half in halves)
        handed = () if out is None else (out,)
        carried = tuple(halves) if carry else ()
        aliases = {1 + len(halves): 1} if handed else {}
        aliases.update({1 + index: 2 + index for index in range(len(carried))})
        if passed is not None:
            pins, carried = (passed, *pins), (passed,)
            aliases[1 + len(halves) + len(handed)] = 2
        return pl.pallas_call(
            functools.partial(extra_kernel, len(halves), 2 + len(carried), flip),
            out_shape=(jax.ShapeDtypeStruct((strips, count, chans), frame_two.dtype), out_type)
            + tuple(jax.ShapeDtypeStruct(half.shape, half.dtype) for half in carried),
            in_specs=[scalars] + [in_vmem] * len(halves) + [anywhere] * len(handed + pins),
            out_specs=(in_vmem, anywhere) + (in_vmem if carry else anywhere,) * len(carried),
            scratch_shapes=pooling,
            input_output_aliases=aliases,
            compiler_params=params,
            cost_estimate=modelled(cost),
            name="extra",
        )(meta, *halves, *handed, *pins)

    def correlate(out, slots, own, other, came_own, came_other, landing=(), landed=None, cost=0, pins=()):
        parts = (own, other, came_own, came_other)
        strips = sum(piece.shape[0] for piece in own)
        operands = [*own, *other, *came_own, *came_other, queries_wide]
        pair_type = jax.ShapeDtypeStruct((strips, raw + count, queries_n), frame_two.dtype)
        return pl.pallas_call(
            functools.partial(corr_kernel, factor, tuple(len(part) for part in parts), True, slots, landing, len(pins)),
            out_shape=(out_type, pair_type),
            in_specs=[scalars] + [in_vmem] * len(operands) + [anywhere] * (1 + bool(landing) + len(pins)),
            out_specs=(anywhere, in_vmem),
            scratch_shapes=[
                pltpu.VMEM((strips, raw + count, queries_n), frame_two.dtype),
                pltpu.VMEM((raw + 2 * count, 2 * queries_n), jnp.float32),
                *pooling,
                pltpu.SemaphoreType.DMA((strips,)),
                pltpu.SemaphoreType.DMA((max(1, len(landing)),)),
            ],
            input_output_aliases={1 + len(operands) + bool(landing): 0},
            compiler_params=params,
            cost_estimate=modelled(cost),
            name="correlate",
        )(meta, *operands, *([landed] if landing else []), out, *pins)

    def product_type(strips, pixels):
        return jax.ShapeDtypeStruct((strips, pixels, queries_n), frame_two.dtype)

    def raw_rows(out, own, other, wide, landing=(), landed=None, cost=0, leavers=(), leaving=(), slots=(), pins=()):
        operands = [*own, *other, queries_wide if wide else queries]
        strips = sum(half.shape[0] for half in own)
        passive = ([landed] if landing else []) + list(leavers)
        pins = tuple(pins)
        return pl.pallas_call(
            functools.partial(raw_kernel, factor, len(own), wide, landing, leaving, slots),
            out_shape=(out_type,) + (product_type(strips, raw + count),) * (1 + wide),
            in_specs=[scalars] + [in_vmem] * len(operands) + [anywhere] * (1 + len(passive)),
            out_specs=(anywhere,) + (in_vmem,) * (1 + wide),
            scratch_shapes=[
                pltpu.VMEM((raw + count, queries_n * (1 + wide)), jnp.float32),
                *pooling,
                pltpu.SemaphoreType.DMA((max(1, len(landing)),)),
                pltpu.SemaphoreType.DMA((max(1, len(slots)),)),
            ],
            input_output_aliases={1 + len(operands) + len(passive): 0},
            compiler_params=params,
            cost_estimate=modelled(cost),
            name="raw_rows",
        )(meta, *operands, *passive, out)

    def came_rows(out, done, slots, own, other, wide, late=(), cost=0, pins=()):
        operands = [*own, *other, queries_wide if wide else queries, *late[:1]]
        first = 1 + len(operands)
        inout = [out, done, *late[1:]]
        extra_types = (product_type(done.shape[0], count),) if wide else ()
        return pl.pallas_call(
            functools.partial(came_kernel, factor, len(own), wide, len(late) // 2, len(pins), slots, not G("NL")),
            out_shape=tuple(jax.ShapeDtypeStruct(array.shape, array.dtype) for array in inout) + extra_types,
            in_specs=[scalars] + [in_vmem] * len(operands) + [anywhere] + [in_vmem] * (len(inout) - 1) + [anywhere] * len(pins),
            out_specs=(anywhere,) + (in_vmem,) * (len(inout) - 1 + wide),
            scratch_shapes=[
                pltpu.VMEM((count, queries_n), jnp.float32),
                pltpu.SemaphoreType.DMA((max(1, len(slots)),)),
            ],
            input_output_aliases={first + index: index for index in range(len(inout))},
            compiler_params=params,
            cost_estimate=modelled(cost),
            name="came_rows",
        )(meta, *operands, *inout, *pins)

    def gate(out, pins, cost):
        handed = (out, *pins)
        return pl.pallas_call(
            gate_kernel,
            out_shape=tuple(jax.ShapeDtypeStruct(array.shape, array.dtype) for array in handed),
            in_specs=[anywhere] * len(handed),
            out_specs=(anywhere,) * len(handed),
            input_output_aliases={index: index for index in range(len(handed))},
            compiler_params=params,
            cost_estimate=modelled(cost),
            name="gate",
        )(*handed)

    mine = lax.dynamic_slice_in_dim(frame_two, side * half_rows, half_rows, axis=0)[None]
    theirs = lax.dynamic_slice_in_dim(frame_two, (1 - side) * half_rows, half_rows, axis=0)[None]
    if G("XQ"):
        sent = jnp.concatenate([theirs.reshape(raw, chans), frame_one], axis=0)
        got = lax.ppermute(sent, "chan", across)
        partner, queries_other = got[:raw].reshape(theirs.shape), got[raw:]
    else:
        partner = lax.ppermute(theirs, "chan", across)
        queries_other = lax.ppermute(frame_one, "chan", across)
    def all_queries(mine, theirs):
        own_core = jnp.concatenate([mine.T, theirs.T], axis=0)
        return own_core, jnp.concatenate([own_core, lax.ppermute(own_core, "rows", swap)], axis=1)

    if not G("QC"): queries, queries_wide = all_queries(frame_one, queries_other)

    def permute_rows(pairs, pieces):
        return [lax.ppermute(piece, "rows", pairs) for piece in pieces]

    def whole(pieces):
        return pieces if len(pieces) == 1 else [jnp.concatenate(pieces, axis=0)]

    came = {0: ([mine], [partner])}
    moving = [[half, *permute_rows(swap, [half])] for half in (mine, partner)]
    join = [G("JA"), G("JB")]
    for d in range(1, half_way + 1):
        if d == half_way:
            moving = [[pieces[0][:1]] for pieces in moving]
        if d == half_way - 1 and G("BSPL"):
            moving[1] = [moving[1][0][:1], moving[1][0][1:]]
        moving = [whole(pieces) if d == join[part] else pieces for part, pieces in enumerate(moving)]
        if d == 1:
            ring_first = moving[1][-1]
        moving = [permute_rows(ring, pieces) for pieces in moving]
        came[d] = tuple(moving)
    across_came = {}

    def do_extra(out, d, part, pin=None):
        pins = () if pin is None else tuple(across_came[pin]) if isinstance(pin, tuple) else (pin,)
        across_came[d, 1 - part] = []
        groups = [[piece] for piece in came[d][part]] if part and d == half_way - 1 else [came[d][part]]
        for pieces in groups:
            extra, out = make_extra(out, pieces, G(f"X{d}{part}"), pins)
            across_came[d, 1 - part].append(lax.ppermute(extra, "chan", across))
            pins = ()
        return out

    lag = G("LAG")
    waiting = []

    def landing(now):
        if waiting and waiting[0][0] <= now:
            return waiting.pop(0)[1:]
        return (), None

    def product(out, d, pins=(), now=None):
        out, pair = correlate(out, slots_of(d, 0), *came[d], across_came[d, 0], across_came[d, 1], *landing(d if now is None else now), G(f"C{d}"), pins)
        waiting.append((d + lag, slots_of(d, 1), permute_rows(swap, [pair])[0]))
        return out

    if G("QC"):
        extra, out, sent = make_extra(None, came[0][0], G("X00"), ({1: partner, 2: ring_first}[G("PINX")],) if G("PINX") else (), passed=frame_one)
        across_came[0, 1] = [lax.ppermute(extra, "chan", across)]
        queries, queries_wide = all_queries(frame_one, lax.ppermute(sent, "chan", across))
    else:
        out = do_extra(None, 0, 0, partner if G("PINX") else None)
    lacking, out = make_extra(out, [theirs], G("X01"), tuple(across_came[0, 1]) if G("PIN01") else (), flip=True)
    across_came[0, 0] = [lacking]
    near, far = half_way - 1, half_way

    def swap_one(piece):
        return permute_rows(swap, [piece])[0]

    def near_raw(out):
        return raw_rows(out, *came[near], True, *landing(near), G("F3"))

    swapped = []

    def far_extra(out, part, pins):
        extra, out, piece = make_extra(out, came[far][part], G(f"X4{part}"), pins, carry=True)
        came[far][part][0] = piece
        across_came[far, 1 - part] = [lax.ppermute(extra, "chan", across)]
        swapped.append(swap_one(piece))
        return out

    out = do_extra(out, 1, 0)
    out = do_extra(out, 2, 0, (1, 1))
    out = do_extra(out, 1, 1, (2, 1))
    out = product(out, 0)
    for d in range(3, far):
        out = do_extra(out, d, 0, (d - 2, 0))
        out = product(out, d - 2)
        out = do_extra(out, d - 1, 1, (d, 1))
    if G("CP2") == 0: out = product(out, near - 1, now=near)
    out = far_extra(out, 0, tuple(across_came[near - 1, 0]) if G("P4") else ())
    if G("CP2") == 1: out = product(out, near - 1, now=near)
    out = do_extra(out, near, 1, (far, 1) if G("P3") else None)
    out, near_done, near_pair = near_raw(out)
    out = far_extra(out, 1, (swapped[0],) if G("PS0") == 1 else ())
    near_late = swap_one(near_pair)
    pins = (tuple(across_came[far, 1]) if G("PE4") == 1 else ()) + ((swapped[0],) if G("PS0") == 2 else ())

    slots = slots_of(near, 1) + slots_of(far, 0) + slots_of(far, 1)

    out, near_done, near_rows = came_rows(out, near_done, (), across_came[near, 0], across_came[near, 1], True, cost=G("F2"), pins=pins)
    near_rows = swap_one(near_rows)
    out, far_done = raw_rows(
        out,
        [came[far][0][0], swapped[0]],
        [came[far][1][0], swapped[1]],
        False,
        *landing(far),
        G("F0"),
        (near_done, near_late),
        (True, False if G("NL") else None),
        slots_of(near, 0) + (slots if G("NL") else slots[len(slots_of(near, 1)) :]),
    )
    out, own, other = gate(out, [across_came[far, 0][0], across_came[far, 1][0]], G("GATE"))
    return came_rows(out, far_done, slots, [own, swap_one(own)], [other, swap_one(other)], False, (near_rows, near_late), G("F1"))[0]


def solution(mesh):
    rows_axis, groups = mesh.shape["rows"], mesh.shape["chan"]

    def local(frame_one, frame_two):
        rows_n, cols_n, chans = frame_two.shape
        ring = groups == 2 and rows_axis % 8 == 0 and rows_axis >= 16 and rows_n % 8 == 0 and cols_n % 32 == 0 and chans % LANES == 0
        return (ring_local if ring else gather_local)(frame_one, frame_two)

    in_specs = (P("rows", "chan"), P("rows", None, "chan"))
    out_specs = P(None, "chan", "rows")
    return jax.shard_map(local, mesh=mesh, in_specs=in_specs, out_specs=out_specs, check_vma=False)
```

profile of v0, /device:TPU:0, one launch (start us, length us, event | category | flops | bytes accessed | tf_op | source)
XLA Modules:
  0.0 95.8 jit_solution(12096028948613992267)
XLA Ops:
  0.0 1.2 %dynamic-slice_bitcast_fusion = (bf16[1,4,480,128]{3,2,1,0:T(8,128)(2,1)S(1)}, bf16[1,4,480,128]{3,2,1,0:T(8,128)(2,1)S(1)}) fusion(bf16[8,480,128]{2,1,0:T(8,128)(2,1)} %param.3, s32[]{:T(128)S(6)} %select_n.72, s32[]{:T(128)S(6)} %select_n.71), kind=kLoop, calls=%fused_computation.2 | loop fusion | bytes 1966088 | tf_op jit(solution)/shard_map/broadcast_in_dim | solution.py:463
  1.8 2.6 %collective-permute-start = (bf16[1,4,480,128]{3,2,1,0:T(8,128)(2,1)S(1)}, bf16[1,4,480,128]{3,2,1,0:T(8,128)(2,1)S(1)}, u32[]{:S(2)}, u32[]{:S(2)}) collective-permute-start(bf16[1,4,480,128]{3,2,1,0:T(8,128)(2,1)S(1)} %get-tuple-element.86.refs_0_), channel_id=1, source_target_pairs={{0,8},{8,16},{16,24},{24,28},{28,20},{20,12},{12,4},{4,0},{2,6},{1... | collective-permute-start | bytes 1474568 | tf_op jit(solution)/shard_map/ppermute | solution.py:478
  4.4 1.5 %collective-permute-start.7 = (bf16[1,4,480,128]{3,2,1,0:T(8,128)(2,1)S(1)}, bf16[1,4,480,128]{3,2,1,0:T(8,128)(2,1)S(1)}, u32[]{:S(2)}, u32[]{:S(2)}) collective-permute-start(bf16[1,4,480,128]{3,2,1,0:T(8,128)(2,1)S(1)} %get-tuple-element.85.refs_0_), channel_id=1, source_target_pairs={{0,1},{1,0},{2,3},{3,2},{4,5},{5,4},{6,7},{7,6},{8,9},{9,8},{10,11... | collective-permute-start | bytes 1474568 | tf_op jit(solution)/shard_map/ppermute | solution.py:469
  5.9 0.9 copy.27
  8.2 1.6 %collective-permute-start.3 = (bf16[1,4,480,128]{3,2,1,0:T(8,128)(2,1)S(1)}, bf16[1,4,480,128]{3,2,1,0:T(8,128)(2,1)S(1)}, u32[]{:S(2)}, u32[]{:S(2)}) collective-permute-start(bf16[1,4,480,128]{3,2,1,0:T(8,128)(2,1)S(1)} %collective-permute-done.2), channel_id=1, source_target_pairs={{0,8},{8,16},{16,24},{24,28},{28,20},{20,12},{12,4},{4,0},{2,6},{1... | collective-permute-start | bytes 1474568 | tf_op jit(solution)/shard_map/ppermute | solution.py:478
  10.5 0.7 collective-permute-done.refs_0_
  11.2 2.1 %collective-permute-start.1 = (bf16[1,4,480,128]{3,2,1,0:T(8,128)(2,1)S(1)}, bf16[1,4,480,128]{3,2,1,0:T(8,128)(2,1)S(1)}, u32[]{:S(2)}, u32[]{:S(2)}) collective-permute-start(bf16[1,4,480,128]{3,2,1,0:T(8,128)(2,1)S(1)} %collective-permute-done.refs_0_), channel_id=1, source_target_pairs={{0,8},{8,16},{16,24},{24,28},{28,20},{20,12},{12,4},{4,0},{2,6},{1... | collective-permute-start | bytes 1474568 | tf_op jit(solution)/shard_map/ppermute | solution.py:478
  13.2 5.1 %collective-permute-done.7.refs_1_ = bf16[1,4,480,128]{3,2,1,0:T(8,128)(2,1)S(1)} collective-permute-done((bf16[1,4,480,128]{3,2,1,0:T(8,128)(2,1)S(1)}, bf16[1,4,480,128]{3,2,1,0:T(8,128)(2,1)S(1)}, u32[]{:S(2)}, u32[]{:S(2)}) %collective-permute-start.7) | collective-permute-done | bytes 491552 | tf_op jit(solution)/shard_map/ppermute | solution.py:469
  18.7 0.8 extra.12
  19.5 1.5 %collective-permute-start.11 = (bf16[2,600,128]{2,1,0:T(8,128)(2,1)S(1)}, bf16[2,600,128]{2,1,0:T(8,128)(2,1)S(1)}, u32[]{:S(2)}, u32[]{:S(2)}) collective-permute-start(bf16[2,600,128]{2,1,0:T(8,128)(2,1)S(1)} %get-tuple-element.48), channel_id=1, source_target_pairs={{0,1},{1,0},{2,3},{3,2},{4,5},{5,4},{6,7},{7,6},{8,9},{9,8},{10,11... | collective-permute-start | bytes 921608 | tf_op jit(solution)/shard_map/ppermute | solution.py:504
  21.2 1.6 %collective-permute-start.9 = (bf16[2,4,480,128]{3,2,1,0:T(8,128)(2,1)S(1)}, bf16[2,4,480,128]{3,2,1,0:T(8,128)(2,1)S(1)}, u32[]{:S(2)}, u32[]{:S(2)}) collective-permute-start(bf16[2,4,480,128]{3,2,1,0:T(8,128)(2,1)S(1)} %pad_maximum_fusion.1), channel_id=1, source_target_pairs={{0,8},{8,16},{16,24},{24,28},{28,20},{20,12},{12,4},{4,0},{2,6},{1... | collective-permute-start | bytes 2949128 | tf_op jit(solution)/shard_map/ppermute | solution.py:478
  22.9 6.2 %collective-permute-done.11.refs_3_.refs_4_ = bf16[2,600,128]{2,1,0:T(8,128)(2,1)S(1)} collective-permute-done((bf16[2,600,128]{2,1,0:T(8,128)(2,1)S(1)}, bf16[2,600,128]{2,1,0:T(8,128)(2,1)S(1)}, u32[]{:S(2)}, u32[]{:S(2)}) %collective-permute-start.11) | collective-permute-done | bytes 307232 | tf_op jit(solution)/shard_map/ppermute | solution.py:504
  29.0 0.8 extra.13
  29.8 1.3 %collective-permute-start.12 = (bf16[2,600,128]{2,1,0:T(8,128)(2,1)S(1)}, bf16[2,600,128]{2,1,0:T(8,128)(2,1)S(1)}, u32[]{:S(2)}, u32[]{:S(2)}) collective-permute-start(bf16[2,600,128]{2,1,0:T(8,128)(2,1)S(1)} %get-tuple-element.50), channel_id=1, source_target_pairs={{0,1},{1,0},{2,3},{3,2},{4,5},{5,4},{6,7},{7,6},{8,9},{9,8},{10,11... | collective-permute-start | bytes 921608 | tf_op jit(solution)/shard_map/ppermute | solution.py:504
  31.1 0.8 collective-permute-start.16
  32.0 1.6 %collective-permute-start.5 = (bf16[2,4,480,128]{3,2,1,0:T(8,128)(2,1)S(1)}, bf16[2,4,480,128]{3,2,1,0:T(8,128)(2,1)S(1)}, u32[]{:S(2)}, u32[]{:S(2)}) collective-permute-start(bf16[2,4,480,128]{3,2,1,0:T(8,128)(2,1)S(1)} %pad_maximum_fusion), channel_id=1, source_target_pairs={{0,8},{8,16},{16,24},{24,28},{28,20},{20,12},{12,4},{4,0},{2,6},{1... | collective-permute-start | bytes 2949128 | tf_op jit(solution)/shard_map/ppermute | solution.py:478
  33.7 6.4 %collective-permute-done.12.refs_2_.refs_4_ = bf16[2,600,128]{2,1,0:T(8,128)(2,1)S(1)} collective-permute-done((bf16[2,600,128]{2,1,0:T(8,128)(2,1)S(1)}, bf16[2,600,128]{2,1,0:T(8,128)(2,1)S(1)}, u32[]{:S(2)}, u32[]{:S(2)}) %collective-permute-start.12) | collective-permute-done | bytes 307232 | tf_op jit(solution)/shard_map/ppermute | solution.py:504
  40.1 0.8 extra.14
  40.9 1.1 %collective-permute-start.13 = (bf16[2,600,128]{2,1,0:T(8,128)(2,1)S(1)}, bf16[2,600,128]{2,1,0:T(8,128)(2,1)S(1)}, u32[]{:S(2)}, u32[]{:S(2)}) collective-permute-start(bf16[2,600,128]{2,1,0:T(8,128)(2,1)S(1)} %get-tuple-element.51), channel_id=1, source_target_pairs={{0,1},{1,0},{2,3},{3,2},{4,5},{5,4},{6,7},{7,6},{8,9},{9,8},{10,11... | collective-permute-start | bytes 921608 | tf_op jit(solution)/shard_map/ppermute | solution.py:504
  42.0 0.8 collective-permute-done.16.refs_3_
  42.8 2.5 %correlate.3 = (bf16[16,2520,256]{2,1,0:T(8,128)(2,1)}, bf16[1,2520,256]{2,1,0:T(8,128)(2,1)S(1)}) custom-call(s32[21]{0:T(128)S(1)} %concatenate.15.meta, bf16[1,4,480,128]{3,2,1,0:T(8,128)(2,1)S(1)} %get-tuple-element.86.refs_0_, bf16[1,4,480,128]{3,2,1,0:T(8,128)(2,1)S(1)} %collective-permute-done.7.refs_1_, ...), custom_call_target="tpu_custom_call", output_to_operand_aliasing={{0}: (6, {})} | custom-call | flops 10000001024 | bytes 1000 | tf_op jit(solution)/shard_map/correlate/pallas_call | solution.py:386
  45.3 1.2 %collective-permute-start.10 = (bf16[2,4,480,128]{3,2,1,0:T(8,128)(2,1)S(1)}, bf16[2,4,480,128]{3,2,1,0:T(8,128)(2,1)S(1)}, u32[]{:S(2)}, u32[]{:S(2)}) collective-permute-start(bf16[2,4,480,128]{3,2,1,0:T(8,128)(2,1)S(1)} %collective-permute-done.9.refs_0_.refs_2_), channel_id=1, source_target_pairs={{0,8},{8,16},{16,24},{24,28},{28,20},{20,12},{12,4},{4,0},{2,6},{1... | collective-permute-start | bytes 2949128 | tf_op jit(solution)/shard_map/ppermute | solution.py:478
  46.5 1.9 %collective-permute-done.13.refs_2_.refs_3_ = bf16[2,600,128]{2,1,0:T(8,128)(2,1)S(1)} collective-permute-done((bf16[2,600,128]{2,1,0:T(8,128)(2,1)S(1)}, bf16[2,600,128]{2,1,0:T(8,128)(2,1)S(1)}, u32[]{:S(2)}, u32[]{:S(2)}) %collective-permute-start.13) | collective-permute-done | bytes 307232 | tf_op jit(solution)/shard_map/ppermute | solution.py:504
  48.7 0.8 extra.15
  49.5 1.3 %collective-permute-start.17 = (bf16[2,600,128]{2,1,0:T(8,128)(2,1)S(1)}, bf16[2,600,128]{2,1,0:T(8,128)(2,1)S(1)}, u32[]{:S(2)}, u32[]{:S(2)}) collective-permute-start(bf16[2,600,128]{2,1,0:T(8,128)(2,1)S(1)} %get-tuple-element.58), channel_id=1, source_target_pairs={{0,1},{1,0},{2,3},{3,2},{4,5},{5,4},{6,7},{7,6},{8,9},{9,8},{10,11... | collective-permute-start | bytes 921608 | tf_op jit(solution)/shard_map/ppermute | solution.py:504
  50.8 1.6 %collective-permute-start.6 = (bf16[1,4,480,128]{3,2,1,0:T(8,128)(2,1)S(1)}, bf16[1,4,480,128]{3,2,1,0:T(8,128)(2,1)S(1)}, u32[]{:S(2)}, u32[]{:S(2)}) collective-permute-start(bf16[1,4,480,128]{3,2,1,0:T(8,128)(2,1)S(1)} %slice.8), channel_id=1, source_target_pairs={{0,8},{8,16},{16,24},{24,28},{28,20},{20,12},{12,4},{4,0},{2,6},{1... | collective-permute-start | bytes 1474568 | tf_op jit(solution)/shard_map/ppermute | solution.py:478
  52.5 3.3 %correlate.4 = (bf16[16,2520,256]{2,1,0:T(8,128)(2,1)}, bf16[2,2520,256]{2,1,0:T(8,128)(2,1)S(1)}) custom-call(s32[21]{0:T(128)S(1)} %concatenate.15.meta, bf16[1,4,480,128]{3,2,1,0:T(8,128)(2,1)S(1)} %collective-permute-done.refs_0_, bf16[1,4,480,128]{3,2,1,0:T(8,128)(2,1)S(1)} %collective-permute-done.3.refs_1_, ...), custom_call_target="tpu_custom_call", output_to_operand_aliasing={{0}: (7, {})} | custom-call | flops 10000001024 | bytes 1000 | tf_op jit(solution)/shard_map/correlate/pallas_call | solution.py:386
  55.9 2.1 %collective-permute-done.17.refs_2_.refs_1_ = bf16[2,600,128]{2,1,0:T(8,128)(2,1)S(1)} collective-permute-done((bf16[2,600,128]{2,1,0:T(8,128)(2,1)S(1)}, bf16[2,600,128]{2,1,0:T(8,128)(2,1)S(1)}, u32[]{:S(2)}, u32[]{:S(2)}) %collective-permute-start.17) | collective-permute-done | bytes 307232 | tf_op jit(solution)/shard_map/ppermute | solution.py:504
  58.0 1.5 %collective-permute-done.10.refs_0_.refs_2_ = bf16[2,4,480,128]{3,2,1,0:T(8,128)(2,1)S(1)} collective-permute-done((bf16[2,4,480,128]{3,2,1,0:T(8,128)(2,1)S(1)}, bf16[2,4,480,128]{3,2,1,0:T(8,128)(2,1)S(1)}, u32[]{:S(2)}, u32[]{:S(2)}) %collective-permute-start.10) | collective-permute-done | bytes 983072 | tf_op jit(solution)/shard_map/ppermute | solution.py:478
  59.5 0.8 extra.16
  60.2 1.1 %collective-permute-start.22 = (bf16[2,600,128]{2,1,0:T(8,128)(2,1)S(1)}, bf16[2,600,128]{2,1,0:T(8,128)(2,1)S(1)}, u32[]{:S(2)}, u32[]{:S(2)}) collective-permute-start(bf16[2,600,128]{2,1,0:T(8,128)(2,1)S(1)} %get-tuple-element.62), channel_id=1, source_target_pairs={{0,1},{1,0},{2,3},{3,2},{4,5},{5,4},{6,7},{7,6},{8,9},{9,8},{10,11... | collective-permute-start | bytes 921608 | tf_op jit(solution)/shard_map/ppermute | solution.py:504
  61.3 1.6 %collective-permute-start.19 = (bf16[2,4,480,128]{3,2,1,0:T(8,128)(2,1)S(1)}, bf16[2,4,480,128]{3,2,1,0:T(8,128)(2,1)S(1)}, u32[]{:S(2)}, u32[]{:S(2)}) collective-permute-start(bf16[2,4,480,128]{3,2,1,0:T(8,128)(2,1)S(1)} %collective-permute-done.10.refs_0_.refs_2_), channel_id=1, source_target_pairs={{0,8},{8,16},{16,24},{24,28},{28,20},{20,12},{12,4},{4,0},{2,6},{1... | collective-permute-start | bytes 2949128 | tf_op jit(solution)/shard_map/ppermute | solution.py:478
  62.9 1.8 %collective-permute-done.6.refs_0_ = bf16[1,4,480,128]{3,2,1,0:T(8,128)(2,1)S(1)} collective-permute-done((bf16[1,4,480,128]{3,2,1,0:T(8,128)(2,1)S(1)}, bf16[1,4,480,128]{3,2,1,0:T(8,128)(2,1)S(1)}, u32[]{:S(2)}, u32[]{:S(2)}) %collective-permute-start.6) | collective-permute-done | bytes 491552 | tf_op jit(solution)/shard_map/ppermute | solution.py:478
  64.7 0.7 extra.17
  65.4 1.2 %collective-permute-start.24 = (bf16[1,600,128]{2,1,0:T(8,128)(2,1)S(1)}, bf16[1,600,128]{2,1,0:T(8,128)(2,1)S(1)}, u32[]{:S(2)}, u32[]{:S(2)}) collective-permute-start(bf16[1,600,128]{2,1,0:T(8,128)(2,1)S(1)} %get-tuple-element.66), channel_id=1, source_target_pairs={{0,1},{1,0},{2,3},{3,2},{4,5},{5,4},{6,7},{7,6},{8,9},{9,8},{10,11... | collective-permute-start | bytes 460808 | tf_op jit(solution)/shard_map/ppermute | solution.py:542
  66.6 3.8 %collective-permute-done.22.refs_3_ = bf16[2,600,128]{2,1,0:T(8,128)(2,1)S(1)} collective-permute-done((bf16[2,600,128]{2,1,0:T(8,128)(2,1)S(1)}, bf16[2,600,128]{2,1,0:T(8,128)(2,1)S(1)}, u32[]{:S(2)}, u32[]{:S(2)}) %collective-permute-start.22) | collective-permute-done | bytes 307232 | tf_op jit(solution)/shard_map/ppermute | solution.py:504
  70.4 3.5 %correlate.5 = (bf16[16,2520,256]{2,1,0:T(8,128)(2,1)}, bf16[2,2520,256]{2,1,0:T(8,128)(2,1)S(1)}) custom-call(s32[21]{0:T(128)S(1)} %concatenate.15.meta, bf16[1,4,480,128]{3,2,1,0:T(8,128)(2,1)S(1)} %collective-permute-done.1.refs_0_, bf16[1,4,480,128]{3,2,1,0:T(8,128)(2,1)S(1)} %collective-permute-done.4.refs_1_, ...), custom_call_target="tpu_custom_call", output_to_operand_aliasing={{0}: (8, {})} | custom-call | flops 10000001024 | bytes 1000 | tf_op jit(solution)/shard_map/correlate/pallas_call | solution.py:386
  74.5 0.9 collective-permute-done.19.refs_0_.refs_1_
  75.5 1.6 %collective-permute-start.20 = (bf16[1,4,480,128]{3,2,1,0:T(8,128)(2,1)S(1)}, bf16[1,4,480,128]{3,2,1,0:T(8,128)(2,1)S(1)}, u32[]{:S(2)}, u32[]{:S(2)}) collective-permute-start(bf16[1,4,480,128]{3,2,1,0:T(8,128)(2,1)S(1)} %slice.9), channel_id=1, source_target_pairs={{0,8},{8,16},{16,24},{24,28},{28,20},{20,12},{12,4},{4,0},{2,6},{1... | collective-permute-start | bytes 1474568 | tf_op jit(solution)/shard_map/ppermute | solution.py:478
  77.1 0.8 extra.18
  77.9 0.9 collective-permute-start.27
  78.8 2.0 %raw_rows.2 = (bf16[16,2520,256]{2,1,0:T(8,128)(2,1)}, bf16[2,2520,256]{2,1,0:T(8,128)(2,1)S(1)}, bf16[2,2520,256]{2,1,0:T(8,128)(2,1)S(1)}) custom-call(s32[21]{0:T(128)S(1)} %concatenate.15.meta, bf16[2,4,480,128]{3,2,1,0:T(8,128)(2,1)S(1)} %collective-permute-done.5.refs_0_, ...), custom_call_target="tpu_custom_call", output_to_operand_aliasing={{0}: (5, {})} | custom-call | flops 10000001024 | bytes 1000 | tf_op jit(solution)/shard_map/raw_rows/pallas_call | solution.py:412
  81.0 3.4 %collective-permute-done.20.refs_0_ = bf16[1,4,480,128]{3,2,1,0:T(8,128)(2,1)S(1)} collective-permute-done((bf16[1,4,480,128]{3,2,1,0:T(8,128)(2,1)S(1)}, bf16[1,4,480,128]{3,2,1,0:T(8,128)(2,1)S(1)}, u32[]{:S(2)}, u32[]{:S(2)}) %collective-permute-start.20) | collective-permute-done | bytes 491552 | tf_op jit(solution)/shard_map/ppermute | solution.py:478
  85.1 1.0 %collective-permute-start.29 = (bf16[1,600,128]{2,1,0:T(8,128)(2,1)S(1)}, bf16[1,600,128]{2,1,0:T(8,128)(2,1)S(1)}, u32[]{:S(2)}, u32[]{:S(2)}) collective-permute-start(bf16[1,600,128]{2,1,0:T(8,128)(2,1)S(1)} %get-tuple-element.78), channel_id=1, source_target_pairs={{0,1},{1,0},{2,3},{3,2},{4,5},{5,4},{6,7},{7,6},{8,9},{9,8},{10,11... | collective-permute-start | bytes 460808 | tf_op jit(solution)/shard_map/ppermute | solution.py:542
  86.1 1.3 %came_rows.2 = (bf16[16,2520,256]{2,1,0:T(8,128)(2,1)}, bf16[2,2520,256]{2,1,0:T(8,128)(2,1)S(1)}, bf16[2,600,256]{2,1,0:T(8,128)(2,1)S(1)}) custom-call(s32[21]{0:T(128)S(1)} %concatenate.15.meta, bf16[2,600,128]{2,1,0:T(8,128)(2,1)S(1)} %collective-permute-done.27.refs_0_, ...), custom_call_target="tpu_custom_call", output_to_operand_aliasing={{0}: (4, {}), {1}: (5, {})} | custom-call | flops 22000001024 | bytes 1000 | tf_op jit(solution)/shard_map/came_rows/pallas_call | solution.py:434
  87.6 3.3 %raw_rows.3 = (bf16[16,2520,256]{2,1,0:T(8,128)(2,1)}, bf16[2,2520,256]{2,1,0:T(8,128)(2,1)S(1)}) custom-call(s32[21]{0:T(128)S(1)} %concatenate.15.meta, bf16[1,4,480,128]{3,2,1,0:T(8,128)(2,1)S(1)} %get-tuple-element.60.refs_0_, bf16[1,4,480,128]{3,2,1,0:T(8,128)(2,1)S(1)} %collective-permute-done.18.refs_2_.refs_1_, ...), custom_call_target="tpu_custom_call", output_to_operand_aliasing={{0}: (9, {})} | custom-call | flops 10000001024 | bytes 1000 | tf_op jit(solution)/shard_map/raw_rows/pallas_call | solution.py:412
  92.0 0.9 collective-permute-done.30.refs_1_
  93.1 2.5 %came_rows.3 = (bf16[16,2520,256]{2,1,0:T(8,128)(2,1)}, bf16[2,2520,256]{2,1,0:T(8,128)(2,1)S(1)}, bf16[2,2520,256]{2,1,0:T(8,128)(2,1)S(1)}) custom-call(s32[21]{0:T(128)S(1)} %concatenate.15.meta, bf16[1,600,128]{2,1,0:T(8,128)(2,1)S(1)} %get-tuple-element.79.refs_0_, ...), custom_call_target="tpu_custom_call", output_to_operand_aliasing={{0}: (7, {}), {1}: (8, {}), {2}: (9, {})} | custom-call | flops 1000 | bytes 1000 | tf_op jit(solution)/shard_map/came_rows/pallas_call | solution.py:434
  (47 shorter events, 6.5 us)
Async XLA Ops:
  1.2 7.0 %collective-permute-start.2 = (bf16[1,4,480,128]{3,2,1,0:T(8,128)(2,1)S(1)}, bf16[1,4,480,128]{3,2,1,0:T(8,128)(2,1)S(1)}, u32[]{:S(2)}, u32[]{:S(2)}) collective-permute-start(bf16[1,4,480,128]{3,2,1,0:T(8,128)(2,1)S(1)} %get-tuple-element.86.refs_0_), channel_id=1, source_target_pairs={{0,2},{2,0},{4,6},{6,4},{8,10},{10,8},{12,14},{14,12},{16,18},{18,... | collective-permute-start | bytes 1474568 | tf_op jit(solution)/shard_map/ppermute | solution.py:478
  1.8 9.4 %collective-permute-start = (bf16[1,4,480,128]{3,2,1,0:T(8,128)(2,1)S(1)}, bf16[1,4,480,128]{3,2,1,0:T(8,128)(2,1)S(1)}, u32[]{:S(2)}, u32[]{:S(2)}) collective-permute-start(bf16[1,4,480,128]{3,2,1,0:T(8,128)(2,1)S(1)} %get-tuple-element.86.refs_0_), channel_id=1, source_target_pairs={{0,8},{8,16},{16,24},{24,28},{28,20},{20,12},{12,4},{4,0},{2,6},{1... | collective-permute-start | bytes 1474568 | tf_op jit(solution)/shard_map/ppermute | solution.py:478
  4.4 13.9 %collective-permute-start.7 = (bf16[1,4,480,128]{3,2,1,0:T(8,128)(2,1)S(1)}, bf16[1,4,480,128]{3,2,1,0:T(8,128)(2,1)S(1)}, u32[]{:S(2)}, u32[]{:S(2)}) collective-permute-start(bf16[1,4,480,128]{3,2,1,0:T(8,128)(2,1)S(1)} %get-tuple-element.85.refs_0_), channel_id=1, source_target_pairs={{0,1},{1,0},{2,3},{3,2},{4,5},{5,4},{6,7},{7,6},{8,9},{9,8},{10,11... | collective-permute-start | bytes 1474568 | tf_op jit(solution)/shard_map/ppermute | solution.py:469
  6.8 14.2 %collective-permute-start.14 = (bf16[256,128]{0,1:T(8,128)(2,1)S(1)}, bf16[256,128]{0,1:T(8,128)(2,1)S(1)}, u32[]{:S(2)}, u32[]{:S(2)}) collective-permute-start(bf16[256,128]{0,1:T(8,128)(2,1)S(1)} %copy.27), channel_id=1, source_target_pairs={{0,1},{1,0},{2,3},{3,2},{4,5},{5,4},{6,7},{7,6},{8,9},{9,8},{10,11... | collective-permute-start | bytes 196616 | tf_op jit(solution)/shard_map/ppermute | solution.py:470
  8.2 10.1 %collective-permute-start.3 = (bf16[1,4,480,128]{3,2,1,0:T(8,128)(2,1)S(1)}, bf16[1,4,480,128]{3,2,1,0:T(8,128)(2,1)S(1)}, u32[]{:S(2)}, u32[]{:S(2)}) collective-permute-start(bf16[1,4,480,128]{3,2,1,0:T(8,128)(2,1)S(1)} %collective-permute-done.2), channel_id=1, source_target_pairs={{0,8},{8,16},{16,24},{24,28},{28,20},{20,12},{12,4},{4,0},{2,6},{1... | collective-permute-start | bytes 1474568 | tf_op jit(solution)/shard_map/ppermute | solution.py:478
  11.2 11.7 %collective-permute-start.1 = (bf16[1,4,480,128]{3,2,1,0:T(8,128)(2,1)S(1)}, bf16[1,4,480,128]{3,2,1,0:T(8,128)(2,1)S(1)}, u32[]{:S(2)}, u32[]{:S(2)}) collective-permute-start(bf16[1,4,480,128]{3,2,1,0:T(8,128)(2,1)S(1)} %collective-permute-done.refs_0_), channel_id=1, source_target_pairs={{0,8},{8,16},{16,24},{24,28},{28,20},{20,12},{12,4},{4,0},{2,6},{1... | collective-permute-start | bytes 1474568 | tf_op jit(solution)/shard_map/ppermute | solution.py:478
  18.3 2.8 %collective-permute-start.8 = (bf16[1,4,480,128]{3,2,1,0:T(8,128)(2,1)S(1)}, bf16[1,4,480,128]{3,2,1,0:T(8,128)(2,1)S(1)}, u32[]{:S(2)}, u32[]{:S(2)}) collective-permute-start(bf16[1,4,480,128]{3,2,1,0:T(8,128)(2,1)S(1)} %collective-permute-done.7.refs_1_), channel_id=1, source_target_pairs={{0,2},{2,0},{4,6},{6,4},{8,10},{10,8},{12,14},{14,12},{16,18},{18,... | collective-permute-start | bytes 1474568 | tf_op jit(solution)/shard_map/ppermute | solution.py:478
  18.3 10.7 %collective-permute-start.4 = (bf16[1,4,480,128]{3,2,1,0:T(8,128)(2,1)S(1)}, bf16[1,4,480,128]{3,2,1,0:T(8,128)(2,1)S(1)}, u32[]{:S(2)}, u32[]{:S(2)}) collective-permute-start(bf16[1,4,480,128]{3,2,1,0:T(8,128)(2,1)S(1)} %collective-permute-done.3.refs_1_), channel_id=1, source_target_pairs={{0,8},{8,16},{16,24},{24,28},{28,20},{20,12},{12,4},{4,0},{2,6},{1... | collective-permute-start | bytes 1474568 | tf_op jit(solution)/shard_map/ppermute | solution.py:478
  19.5 9.6 %collective-permute-start.11 = (bf16[2,600,128]{2,1,0:T(8,128)(2,1)S(1)}, bf16[2,600,128]{2,1,0:T(8,128)(2,1)S(1)}, u32[]{:S(2)}, u32[]{:S(2)}) collective-permute-start(bf16[2,600,128]{2,1,0:T(8,128)(2,1)S(1)} %get-tuple-element.48), channel_id=1, source_target_pairs={{0,1},{1,0},{2,3},{3,2},{4,5},{5,4},{6,7},{7,6},{8,9},{9,8},{10,11... | collective-permute-start | bytes 921608 | tf_op jit(solution)/shard_map/ppermute | solution.py:504
  21.0 10.9 %collective-permute-start.15 = (bf16[256,256]{1,0:T(8,128)(2,1)S(1)}, bf16[256,256]{1,0:T(8,128)(2,1)S(1)}, u32[]{:S(2)}, u32[]{:S(2)}) collective-permute-start(bf16[256,256]{1,0:T(8,128)(2,1)S(1)} %pad_maximum_fusion.3.refs_4_), channel_id=1, source_target_pairs={{0,2},{2,0},{4,6},{6,4},{8,10},{10,8},{12,14},{14,12},{16,18},{18,... | collective-permute-start | bytes 393224 | tf_op jit(solution)/shard_map/ppermute | solution.py:473
  21.2 18.9 %collective-permute-start.9 = (bf16[2,4,480,128]{3,2,1,0:T(8,128)(2,1)S(1)}, bf16[2,4,480,128]{3,2,1,0:T(8,128)(2,1)S(1)}, u32[]{:S(2)}, u32[]{:S(2)}) collective-permute-start(bf16[2,4,480,128]{3,2,1,0:T(8,128)(2,1)S(1)} %pad_maximum_fusion.1), channel_id=1, source_target_pairs={{0,8},{8,16},{16,24},{24,28},{28,20},{20,12},{12,4},{4,0},{2,6},{1... | collective-permute-start | bytes 2949128 | tf_op jit(solution)/shard_map/ppermute | solution.py:478
  29.8 10.3 %collective-permute-start.12 = (bf16[2,600,128]{2,1,0:T(8,128)(2,1)S(1)}, bf16[2,600,128]{2,1,0:T(8,128)(2,1)S(1)}, u32[]{:S(2)}, u32[]{:S(2)}) collective-permute-start(bf16[2,600,128]{2,1,0:T(8,128)(2,1)S(1)} %get-tuple-element.50), channel_id=1, source_target_pairs={{0,1},{1,0},{2,3},{3,2},{4,5},{5,4},{6,7},{7,6},{8,9},{9,8},{10,11... | collective-permute-start | bytes 921608 | tf_op jit(solution)/shard_map/ppermute | solution.py:504
  31.1 11.7 %collective-permute-start.16 = (bf16[1,600,128]{2,1,0:T(8,128)(2,1)S(1)}, bf16[1,600,128]{2,1,0:T(8,128)(2,1)S(1)}, u32[]{:S(2)}, u32[]{:S(2)}) collective-permute-start(bf16[1,600,128]{2,1,0:T(8,128)(2,1)S(1)} %get-tuple-element.53), channel_id=1, source_target_pairs={{0,1},{1,0},{2,3},{3,2},{4,5},{5,4},{6,7},{7,6},{8,9},{9,8},{10,11... | collective-permute-start | bytes 460808 | tf_op jit(solution)/shard_map/ppermute | solution.py:504
  32.0 16.7 %collective-permute-start.5 = (bf16[2,4,480,128]{3,2,1,0:T(8,128)(2,1)S(1)}, bf16[2,4,480,128]{3,2,1,0:T(8,128)(2,1)S(1)}, u32[]{:S(2)}, u32[]{:S(2)}) collective-permute-start(bf16[2,4,480,128]{3,2,1,0:T(8,128)(2,1)S(1)} %pad_maximum_fusion), channel_id=1, source_target_pairs={{0,8},{8,16},{16,24},{24,28},{28,20},{20,12},{12,4},{4,0},{2,6},{1... | collective-permute-start | bytes 2949128 | tf_op jit(solution)/shard_map/ppermute | solution.py:478
  40.9 7.6 %collective-permute-start.13 = (bf16[2,600,128]{2,1,0:T(8,128)(2,1)S(1)}, bf16[2,600,128]{2,1,0:T(8,128)(2,1)S(1)}, u32[]{:S(2)}, u32[]{:S(2)}) collective-permute-start(bf16[2,600,128]{2,1,0:T(8,128)(2,1)S(1)} %get-tuple-element.51), channel_id=1, source_target_pairs={{0,1},{1,0},{2,3},{3,2},{4,5},{5,4},{6,7},{7,6},{8,9},{9,8},{10,11... | collective-permute-start | bytes 921608 | tf_op jit(solution)/shard_map/ppermute | solution.py:504
  45.2 25.2 %collective-permute-start.23 = (bf16[1,2520,256]{2,1,0:T(8,128)(2,1)S(1)}, bf16[1,2520,256]{2,1,0:T(8,128)(2,1)S(1)}, u32[]{:S(2)}, u32[]{:S(2)}) collective-permute-start(bf16[1,2520,256]{2,1,0:T(8,128)(2,1)S(1)} %get-tuple-element.63), channel_id=1, source_target_pairs={{0,2},{2,0},{4,6},{6,4},{8,10},{10,8},{12,14},{14,12},{16,18},{18,... | collective-permute-start | bytes 3870728 | tf_op jit(solution)/shard_map/ppermute | solution.py:478
  45.3 14.1 %collective-permute-start.10 = (bf16[2,4,480,128]{3,2,1,0:T(8,128)(2,1)S(1)}, bf16[2,4,480,128]{3,2,1,0:T(8,128)(2,1)S(1)}, u32[]{:S(2)}, u32[]{:S(2)}) collective-permute-start(bf16[2,4,480,128]{3,2,1,0:T(8,128)(2,1)S(1)} %collective-permute-done.9.refs_0_.refs_2_), channel_id=1, source_target_pairs={{0,8},{8,16},{16,24},{24,28},{28,20},{20,12},{12,4},{4,0},{2,6},{1... | collective-permute-start | bytes 2949128 | tf_op jit(solution)/shard_map/ppermute | solution.py:478
  49.5 8.5 %collective-permute-start.17 = (bf16[2,600,128]{2,1,0:T(8,128)(2,1)S(1)}, bf16[2,600,128]{2,1,0:T(8,128)(2,1)S(1)}, u32[]{:S(2)}, u32[]{:S(2)}) collective-permute-start(bf16[2,600,128]{2,1,0:T(8,128)(2,1)S(1)} %get-tuple-element.58), channel_id=1, source_target_pairs={{0,1},{1,0},{2,3},{3,2},{4,5},{5,4},{6,7},{7,6},{8,9},{9,8},{10,11... | collective-permute-start | bytes 921608 | tf_op jit(solution)/shard_map/ppermute | solution.py:504
  50.8 13.9 %collective-permute-start.6 = (bf16[1,4,480,128]{3,2,1,0:T(8,128)(2,1)S(1)}, bf16[1,4,480,128]{3,2,1,0:T(8,128)(2,1)S(1)}, u32[]{:S(2)}, u32[]{:S(2)}) collective-permute-start(bf16[1,4,480,128]{3,2,1,0:T(8,128)(2,1)S(1)} %slice.8), channel_id=1, source_target_pairs={{0,8},{8,16},{16,24},{24,28},{28,20},{20,12},{12,4},{4,0},{2,6},{1... | collective-permute-start | bytes 1474568 | tf_op jit(solution)/shard_map/ppermute | solution.py:478
  55.8 23.0 %collective-permute-start.21 = (bf16[2,2520,256]{2,1,0:T(8,128)(2,1)S(1)}, bf16[2,2520,256]{2,1,0:T(8,128)(2,1)S(1)}, u32[]{:S(2)}, u32[]{:S(2)}) collective-permute-start(bf16[2,2520,256]{2,1,0:T(8,128)(2,1)S(1)} %get-tuple-element.61), channel_id=1, source_target_pairs={{0,2},{2,0},{4,6},{6,4},{8,10},{10,8},{12,14},{14,12},{16,18},{18,... | collective-permute-start | bytes 7741448 | tf_op jit(solution)/shard_map/ppermute | solution.py:478
  60.2 10.2 %collective-permute-start.22 = (bf16[2,600,128]{2,1,0:T(8,128)(2,1)S(1)}, bf16[2,600,128]{2,1,0:T(8,128)(2,1)S(1)}, u32[]{:S(2)}, u32[]{:S(2)}) collective-permute-start(bf16[2,600,128]{2,1,0:T(8,128)(2,1)S(1)} %get-tuple-element.62), channel_id=1, source_target_pairs={{0,1},{1,0},{2,3},{3,2},{4,5},{5,4},{6,7},{7,6},{8,9},{9,8},{10,11... | collective-permute-start | bytes 921608 | tf_op jit(solution)/shard_map/ppermute | solution.py:504
  61.3 14.1 %collective-permute-start.19 = (bf16[2,4,480,128]{3,2,1,0:T(8,128)(2,1)S(1)}, bf16[2,4,480,128]{3,2,1,0:T(8,128)(2,1)S(1)}, u32[]{:S(2)}, u32[]{:S(2)}) collective-permute-start(bf16[2,4,480,128]{3,2,1,0:T(8,128)(2,1)S(1)} %collective-permute-done.10.refs_0_.refs_2_), channel_id=1, source_target_pairs={{0,8},{8,16},{16,24},{24,28},{28,20},{20,12},{12,4},{4,0},{2,6},{1... | collective-permute-start | bytes 2949128 | tf_op jit(solution)/shard_map/ppermute | solution.py:478
  65.4 11.7 %collective-permute-start.24 = (bf16[1,600,128]{2,1,0:T(8,128)(2,1)S(1)}, bf16[1,600,128]{2,1,0:T(8,128)(2,1)S(1)}, u32[]{:S(2)}, u32[]{:S(2)}) collective-permute-start(bf16[1,600,128]{2,1,0:T(8,128)(2,1)S(1)} %get-tuple-element.66), channel_id=1, source_target_pairs={{0,1},{1,0},{2,3},{3,2},{4,5},{5,4},{6,7},{7,6},{8,9},{9,8},{10,11... | collective-permute-start | bytes 460808 | tf_op jit(solution)/shard_map/ppermute | solution.py:542
  70.4 10.5 %collective-permute-start.18 = (bf16[1,4,480,128]{3,2,1,0:T(8,128)(2,1)S(1)}, bf16[1,4,480,128]{3,2,1,0:T(8,128)(2,1)S(1)}, u32[]{:S(2)}, u32[]{:S(2)}) collective-permute-start(bf16[1,4,480,128]{3,2,1,0:T(8,128)(2,1)S(1)} %get-tuple-element.60.refs_0_), channel_id=1, source_target_pairs={{0,2},{2,0},{4,6},{6,4},{8,10},{10,8},{12,14},{14,12},{16,18},{18,... | collective-permute-start | bytes 1474568 | tf_op jit(solution)/shard_map/ppermute | solution.py:478
  74.0 13.7 %collective-permute-start.26 = (bf16[2,2520,256]{2,1,0:T(8,128)(2,1)S(1)}, bf16[2,2520,256]{2,1,0:T(8,128)(2,1)S(1)}, u32[]{:S(2)}, u32[]{:S(2)}) collective-permute-start(bf16[2,2520,256]{2,1,0:T(8,128)(2,1)S(1)} %get-tuple-element.70), channel_id=1, source_target_pairs={{0,2},{2,0},{4,6},{6,4},{8,10},{10,8},{12,14},{14,12},{16,18},{18,... | collective-permute-start | bytes 7741448 | tf_op jit(solution)/shard_map/ppermute | solution.py:478
  75.5 8.9 %collective-permute-start.20 = (bf16[1,4,480,128]{3,2,1,0:T(8,128)(2,1)S(1)}, bf16[1,4,480,128]{3,2,1,0:T(8,128)(2,1)S(1)}, u32[]{:S(2)}, u32[]{:S(2)}) collective-permute-start(bf16[1,4,480,128]{3,2,1,0:T(8,128)(2,1)S(1)} %slice.9), channel_id=1, source_target_pairs={{0,8},{8,16},{16,24},{24,28},{28,20},{20,12},{12,4},{4,0},{2,6},{1... | collective-permute-start | bytes 1474568 | tf_op jit(solution)/shard_map/ppermute | solution.py:478
  77.9 8.2 %collective-permute-start.27 = (bf16[2,600,128]{2,1,0:T(8,128)(2,1)S(1)}, bf16[2,600,128]{2,1,0:T(8,128)(2,1)S(1)}, u32[]{:S(2)}, u32[]{:S(2)}) collective-permute-start(bf16[2,600,128]{2,1,0:T(8,128)(2,1)S(1)} %get-tuple-element.71), channel_id=1, source_target_pairs={{0,1},{1,0},{2,3},{3,2},{4,5},{5,4},{6,7},{7,6},{8,9},{9,8},{10,11... | collective-permute-start | bytes 921608 | tf_op jit(solution)/shard_map/ppermute | solution.py:504
  80.9 6.8 %collective-permute-start.28 = (bf16[2,2520,256]{2,1,0:T(8,128)(2,1)S(1)}, bf16[2,2520,256]{2,1,0:T(8,128)(2,1)S(1)}, u32[]{:S(2)}, u32[]{:S(2)}) collective-permute-start(bf16[2,2520,256]{2,1,0:T(8,128)(2,1)S(1)} %get-tuple-element.75), channel_id=1, source_target_pairs={{0,2},{2,0},{4,6},{6,4},{8,10},{10,8},{12,14},{14,12},{16,18},{18,... | collective-permute-start | bytes 7741448 | tf_op jit(solution)/shard_map/ppermute | solution.py:478
  85.0 2.6 %collective-permute-start.25 = (bf16[1,4,480,128]{3,2,1,0:T(8,128)(2,1)S(1)}, bf16[1,4,480,128]{3,2,1,0:T(8,128)(2,1)S(1)}, u32[]{:S(2)}, u32[]{:S(2)}) collective-permute-start(bf16[1,4,480,128]{3,2,1,0:T(8,128)(2,1)S(1)} %get-tuple-element.69.refs_2_), channel_id=1, source_target_pairs={{0,2},{2,0},{4,6},{6,4},{8,10},{10,8},{12,14},{14,12},{16,18},{18,... | collective-permute-start | bytes 1474568 | tf_op jit(solution)/shard_map/ppermute | solution.py:478
  85.1 6.4 %collective-permute-start.29 = (bf16[1,600,128]{2,1,0:T(8,128)(2,1)S(1)}, bf16[1,600,128]{2,1,0:T(8,128)(2,1)S(1)}, u32[]{:S(2)}, u32[]{:S(2)}) collective-permute-start(bf16[1,600,128]{2,1,0:T(8,128)(2,1)S(1)} %get-tuple-element.78), channel_id=1, source_target_pairs={{0,1},{1,0},{2,3},{3,2},{4,5},{5,4},{6,7},{7,6},{8,9},{9,8},{10,11... | collective-permute-start | bytes 460808 | tf_op jit(solution)/shard_map/ppermute | solution.py:542
  87.4 4.6 %collective-permute-start.32 = (bf16[2,600,256]{2,1,0:T(8,128)(2,1)S(1)}, bf16[2,600,256]{2,1,0:T(8,128)(2,1)S(1)}, u32[]{:S(2)}, u32[]{:S(2)}) collective-permute-start(bf16[2,600,256]{2,1,0:T(8,128)(2,1)S(1)} %get-tuple-element.81), channel_id=1, source_target_pairs={{0,2},{2,0},{4,6},{6,4},{8,10},{10,8},{12,14},{14,12},{16,18},{18,... | collective-permute-start | bytes 1843208 | tf_op jit(solution)/shard_map/ppermute | solution.py:478
  91.5 1.4 %collective-permute-start.30 = (bf16[1,600,128]{2,1,0:T(8,128)(2,1)S(1)}, bf16[1,600,128]{2,1,0:T(8,128)(2,1)S(1)}, u32[]{:S(2)}, u32[]{:S(2)}) collective-permute-start(bf16[1,600,128]{2,1,0:T(8,128)(2,1)S(1)} %get-tuple-element.79.refs_0_), channel_id=1, source_target_pairs={{0,2},{2,0},{4,6},{6,4},{8,10},{10,8},{12,14},{14,12},{16,18},{18,... | collective-permute-start | bytes 460808 | tf_op jit(solution)/shard_map/ppermute | solution.py:478
  91.5 1.6 %collective-permute-start.31 = (bf16[1,600,128]{2,1,0:T(8,128)(2,1)S(1)}, bf16[1,600,128]{2,1,0:T(8,128)(2,1)S(1)}, u32[]{:S(2)}, u32[]{:S(2)}) collective-permute-start(bf16[1,600,128]{2,1,0:T(8,128)(2,1)S(1)} %get-tuple-element.80.refs_2_), channel_id=1, source_target_pairs={{0,2},{2,0},{4,6},{6,4},{8,10},{10,8},{12,14},{14,12},{16,18},{18,... | collective-permute-start | bytes 460808 | tf_op jit(solution)/shard_map/ppermute | solution.py:478
where the time goes:
time: 95.9 us; the launch traced here: 95.8 us
  waiting for transfers between devices  36.7 us (38%)
  starting transfers between devices  30.5 us (32%)
  Pallas kernels  25.6 us (27%)
  local copies, waits for them, and re-layouts  2.32 us (2%)
    ppermute x7, waiting for transfers between devices, do_extra(): across_came[d, 1 - part].append(lax.ppermute(extra, 'chan', across))  21.3 us
    ppermute x21, starting transfers between devices, permute_rows(): return [lax.ppermute(piece, 'rows', pairs) for piece in pieces]  18.1 us
    ppermute x21, waiting for transfers between devices, permute_rows(): return [lax.ppermute(piece, 'rows', pairs) for piece in pieces]  9.74 us
    pallas_call x3, Pallas kernels, correlate(): pl.pallas_call(functools.partial(corr_kernel, factor, tuple((len(part) fo...  9.29 us
    ppermute x7, starting transfers between devices, do_extra(): across_came[d, 1 - part].append(lax.ppermute(extra, 'chan', across))  8.03 us
    pallas_call x10, Pallas kernels, make_extra(): pl.pallas_call(functools.partial(extra_kernel, len(halves), 2 + len(carri...  7.18 us
    pallas_call x2, Pallas kernels, raw_rows(): pl.pallas_call(functools.partial(raw_kernel, factor, len(own), wide, land...  5.39 us
    ppermute x1, waiting for transfers between devices, ring_local(): partner = lax.ppermute(theirs, 'chan', across)  5.11 us
  transfers between devices with their start and end apart: 33, of which 16 were waited for; matrix products, arithmetic and copies ran while one was open for 1% of the time, Pallas kernels for 24%

commit v1 on v0

--- a/solution.py
+++ b/solution.py
@@ -8,7 +8,7 @@
 from jax.sharding import PartitionSpec as P
 
 LANES = 128
-PARAMS = {'LAG': 2, 'F0': 10, 'F1': 0, 'PS0': 1, 'JA': 3, 'JB': 1, 'C0POS': 2, 'GATE': 30, 'F3': 10, 'F2': 22, 'NL': 0, 'PE4': 0, 'CP2': 1, 'P4': 0, 'P3': 1, 'X00': 10, 'X01': 10, 'C0': 10, 'X10': 10, 'X11': 10, 'C1': 10, 'X20': 10, 'X21': 10, 'C2': 10, 'X30': 10, 'X31': 10, 'C3': 10, 'X40': 10, 'X41': 10, 'C4': 10}
+PARAMS = {'LAG': 2, 'F0': 10, 'F1': 0, 'PS0': 2, 'JA': 3, 'JB': 1, 'C0POS': 2, 'GATE': 30, 'F3': 10, 'F2': 22, 'NL': 1, 'PE4': 0, 'P4': 0, 'P3': 1, 'CPOS': 1, 'LC': 1, 'BSPL': 0, 'X00': 10, 'X01': 10, 'C0': 10, 'X10': 10, 'X11': 10, 'C1': 10, 'X20': 10, 'X21': 10, 'C2': 10, 'X30': 10, 'X31': 10, 'C3': 10, 'X40': 10, 'X41': 10, 'C4': 10}
 
 
 def G(name):
@@ -182,8 +182,8 @@
 
 
 def raw_kernel(factor, arrays, wide, landing, leaving, slots, meta, *refs):
-    own, other = strips_in(refs[:arrays]), strips_in(refs[arrays : 2 * arrays])
-    queries, *refs = refs[2 * arrays :]
+    own, other = strips_in(refs[: arrays[0]]), strips_in(refs[arrays[0] : sum(arrays)])
+    queries, *refs = refs[sum(arrays) :]
     landed = refs.pop(0) if landing else None
     leavers, refs = refs[: len(leaving)], refs[len(leaving) :]
     _, out, done, *refs = refs
@@ -253,19 +253,24 @@
         copy.wait()
 
 
-def came_kernel(factor, arrays, wide, late, pins, slots, late_whole, meta, *refs):
-    own, other = strips_in(refs[:arrays]), strips_in(refs[arrays : 2 * arrays])
-    queries, *refs = refs[2 * arrays :]
+def came_kernel(factor, arrays, wide, late, pins, slots, late_whole, landing, meta, *refs):
+    own, other = strips_in(refs[: arrays[0]]), strips_in(refs[arrays[0] : sum(arrays)])
+    queries, *refs = refs[sum(arrays) :]
     late_rows = refs.pop(0) if late else None
-    refs = refs[2 + late + pins :]
+    refs = refs[2 + late :]
+    landed = refs[0] if landing else None
+    refs = refs[pins:]
     out, done, *refs = refs
     late_done = refs.pop(0) if late else None
     pair = refs.pop(0) if wide else None
-    values, sems = refs
+    values, sems, land_sems = refs
     count, width = own[0].shape[0], done.shape[2]
     raw = done.shape[1] - count
     ones = count * 4 // 5
-    copies = []
+    copies, landings = [], []
+    for index, slot in enumerate(landing):
+        landings.append(pltpu.make_async_copy(landed.at[index], out.at[meta[slot]], land_sems.at[index]))
+        landings[-1].start()
 
     def leave(strip, whole=False):
         if slots:
@@ -306,7 +311,7 @@
             pair[index] = part[:, width:].astype(done.dtype)
         merge(done.at[index], part[:, :width])
         leave(done.at[index])
-    for copy in copies:
+    for copy in copies + landings:
         copy.wait()
 
 
@@ -410,7 +415,7 @@
         passive = ([landed] if landing else []) + list(leavers)
         pins = tuple(pins)
         return pl.pallas_call(
-            functools.partial(raw_kernel, factor, len(own), wide, landing, leaving, slots),
+            functools.partial(raw_kernel, factor, (len(own), len(other)), wide, landing, leaving, slots),
             out_shape=(out_type,) + (product_type(strips, raw + count),) * (1 + wide),
             in_specs=[scalars] + [in_vmem] * len(operands) + [anywhere] * (1 + len(passive)),
             out_specs=(anywhere,) + (in_vmem,) * (1 + wide),
@@ -426,19 +431,20 @@
             name="raw_rows",
         )(meta, *operands, *passive, out)
 
-    def came_rows(out, done, slots, own, other, wide, late=(), cost=0, pins=()):
+    def came_rows(out, done, slots, own, other, wide, late=(), cost=0, pins=(), landing=()):
         operands = [*own, *other, queries_wide if wide else queries, *late[:1]]
         first = 1 + len(operands)
         inout = [out, done, *late[1:]]
         extra_types = (product_type(done.shape[0], count),) if wide else ()
         return pl.pallas_call(
-            functools.partial(came_kernel, factor, len(own), wide, len(late) // 2, len(pins), slots, not G("NL")),
+            functools.partial(came_kernel, factor, (len(own), len(other)), wide, len(late) // 2, len(pins), slots, not G("NL"), landing),
             out_shape=tuple(jax.ShapeDtypeStruct(array.shape, array.dtype) for array in inout) + extra_types,
             in_specs=[scalars] + [in_vmem] * len(operands) + [anywhere] + [in_vmem] * (len(inout) - 1) + [anywhere] * len(pins),
             out_specs=(anywhere,) + (in_vmem,) * (len(inout) - 1 + wide),
             scratch_shapes=[
                 pltpu.VMEM((count, queries_n), jnp.float32),
                 pltpu.SemaphoreType.DMA((max(1, len(slots)),)),
+                pltpu.SemaphoreType.DMA((max(1, len(landing)),)),
             ],
             input_output_aliases={first + index: index for index in range(len(inout))},
             compiler_params=params,
@@ -551,10 +557,13 @@
         out = do_extra(out, d, 0, (d - 2, 0))
         out = product(out, d - 2)
         out = do_extra(out, d - 1, 1, (d, 1))
-    if G("CP2") == 0: out = product(out, near - 1, now=near)
     out = far_extra(out, 0, tuple(across_came[near - 1, 0]) if G("P4") else ())
-    if G("CP2") == 1: out = product(out, near - 1, now=near)
-    out = do_extra(out, near, 1, (far, 1) if G("P3") else None)
+    across_came[near, 0] = []
+    for index, piece in enumerate(came[near][1]):
+        if index == len(came[near][1]) - G("CPOS"):
+            out = product(out, near - 1, now=near)
+        extra, out = make_extra(out, [piece], G("X31"), tuple(across_came[far, 1]) if G("P3") == index + 1 else ())
+        across_came[near, 0].append(lax.ppermute(extra, "chan", across))
     out, near_done, near_pair = near_raw(out)
     out = far_extra(out, 1, (swapped[0],) if G("PS0") == 1 else ())
     near_late = swap_one(near_pair)
@@ -562,7 +571,11 @@
 
     slots = slots_of(near, 1) + slots_of(far, 0) + slots_of(far, 1)
 
-    out, near_done, near_rows = came_rows(out, near_done, (), across_came[near, 0], across_came[near, 1], True, cost=G("F2"), pins=pins)
+    landing_now, landed_now = landing(far) if G("LC") else ((), None)
+    pins = ((landed_now,) if landing_now else ()) + pins
+    out, near_done, near_rows = came_rows(
+        out, near_done, (), across_came[near, 0], across_came[near, 1], True, cost=G("F2"), pins=pins, landing=landing_now
+    )
     near_rows = swap_one(near_rows)
     out, far_done = raw_rows(
         out,

time: 95.9 us -> 95.8 us (level)
    ppermute x7 -> x6, starting transfers between devices: 8.03 us -> 7.11 us  [do_extra(): across_came[d, 1 - part].append(lax.ppermute(extra, 'chan', across))]
    ppermute x7 -> x6, waiting for transfers between devices: 21.3 us -> 21.3 us  [do_extra(): across_came[d, 1 - part].append(lax.ppermute(extra, 'chan', across))]
  transfers between devices with their start and end apart: 33 -> 33, of which waited for: 16 -> 16; matrix products, arithmetic and copies ran while one was open for 1% -> 1% of each run, Pallas kernels for 24% -> 25%
where the time goes in v1:
time: 95.8 us; the launch traced here: 95.6 us
  waiting for transfers between devices  36.4 us (38%)
  starting transfers between devices  30.5 us (32%)
  Pallas kernels  25.8 us (27%)
  local copies, waits for them, and re-layouts  2.32 us (2%)
    ppermute x6, waiting for transfers between devices, do_extra(): across_came[d, 1 - part].append(lax.ppermute(extra, 'chan', across))  21.3 us
    ppermute x21, starting transfers between devices, permute_rows(): return [lax.ppermute(piece, 'rows', pairs) for piece in pieces]  18.1 us
    ppermute x21, waiting for transfers between devices, permute_rows(): return [lax.ppermute(piece, 'rows', pairs) for piece in pieces]  9.79 us
    pallas_call x3, Pallas kernels, correlate(): pl.pallas_call(functools.partial(corr_kernel, factor, tuple((len(part) fo...  9.28 us
    pallas_call x10, Pallas kernels, make_extra(): pl.pallas_call(functools.partial(extra_kernel, len(halves), 2 + len(carri...  7.19 us
    ppermute x6, starting transfers between devices, do_extra(): across_came[d, 1 - part].append(lax.ppermute(extra, 'chan', across))  7.11 us
    ppermute x1, waiting for transfers between devices, ring_local(): partner = lax.ppermute(theirs, 'chan', across)  5.11 us
    pallas_call x2, Pallas kernels, raw_rows(): pl.pallas_call(functools.partial(raw_kernel, factor, (len(own), len(other...  5 us
  transfers between devices with their start and end apart: 33, of which 16 were waited for; matrix products, arithmetic and copies ran while one was open for 1% of the time, Pallas kernels for 25%

profile of v1, /device:TPU:0, one launch (start us, length us, event | category | flops | bytes accessed | tf_op | source)
XLA Modules:
  0.0 95.6 jit_solution(8399802693213669703)
XLA Ops:
  0.0 1.2 %dynamic-slice_bitcast_fusion = (bf16[1,4,480,128]{3,2,1,0:T(8,128)(2,1)S(1)}, bf16[1,4,480,128]{3,2,1,0:T(8,128)(2,1)S(1)}) fusion(bf16[8,480,128]{2,1,0:T(8,128)(2,1)} %param.3, s32[]{:T(128)S(6)} %select_n.72, s32[]{:T(128)S(6)} %select_n.71), kind=kLoop, calls=%fused_computation.2 | loop fusion | bytes 1966088 | tf_op jit(solution)/shard_map/broadcast_in_dim | solution.py:469
  1.8 2.6 %collective-permute-start = (bf16[1,4,480,128]{3,2,1,0:T(8,128)(2,1)S(1)}, bf16[1,4,480,128]{3,2,1,0:T(8,128)(2,1)S(1)}, u32[]{:S(2)}, u32[]{:S(2)}) collective-permute-start(bf16[1,4,480,128]{3,2,1,0:T(8,128)(2,1)S(1)} %get-tuple-element.86.refs_0_), channel_id=1, source_target_pairs={{0,8},{8,16},{16,24},{24,28},{28,20},{20,12},{12,4},{4,0},{2,6},{1... | collective-permute-start | bytes 1474568 | tf_op jit(solution)/shard_map/ppermute | solution.py:484
  4.4 1.5 %collective-permute-start.7 = (bf16[1,4,480,128]{3,2,1,0:T(8,128)(2,1)S(1)}, bf16[1,4,480,128]{3,2,1,0:T(8,128)(2,1)S(1)}, u32[]{:S(2)}, u32[]{:S(2)}) collective-permute-start(bf16[1,4,480,128]{3,2,1,0:T(8,128)(2,1)S(1)} %get-tuple-element.85.refs_0_), channel_id=1, source_target_pairs={{0,1},{1,0},{2,3},{3,2},{4,5},{5,4},{6,7},{7,6},{8,9},{9,8},{10,11... | collective-permute-start | bytes 1474568 | tf_op jit(solution)/shard_map/ppermute | solution.py:475
  5.9 0.9 copy.27
  8.2 1.6 %collective-permute-start.3 = (bf16[1,4,480,128]{3,2,1,0:T(8,128)(2,1)S(1)}, bf16[1,4,480,128]{3,2,1,0:T(8,128)(2,1)S(1)}, u32[]{:S(2)}, u32[]{:S(2)}) collective-permute-start(bf16[1,4,480,128]{3,2,1,0:T(8,128)(2,1)S(1)} %collective-permute-done.2), channel_id=1, source_target_pairs={{0,8},{8,16},{16,24},{24,28},{28,20},{20,12},{12,4},{4,0},{2,6},{1... | collective-permute-start | bytes 1474568 | tf_op jit(solution)/shard_map/ppermute | solution.py:484
  10.5 0.7 collective-permute-done.refs_0_
  11.2 2.1 %collective-permute-start.1 = (bf16[1,4,480,128]{3,2,1,0:T(8,128)(2,1)S(1)}, bf16[1,4,480,128]{3,2,1,0:T(8,128)(2,1)S(1)}, u32[]{:S(2)}, u32[]{:S(2)}) collective-permute-start(bf16[1,4,480,128]{3,2,1,0:T(8,128)(2,1)S(1)} %collective-permute-done.refs_0_), channel_id=1, source_target_pairs={{0,8},{8,16},{16,24},{24,28},{28,20},{20,12},{12,4},{4,0},{2,6},{1... | collective-permute-start | bytes 1474568 | tf_op jit(solution)/shard_map/ppermute | solution.py:484
  13.2 5.1 %collective-permute-done.7.refs_1_ = bf16[1,4,480,128]{3,2,1,0:T(8,128)(2,1)S(1)} collective-permute-done((bf16[1,4,480,128]{3,2,1,0:T(8,128)(2,1)S(1)}, bf16[1,4,480,128]{3,2,1,0:T(8,128)(2,1)S(1)}, u32[]{:S(2)}, u32[]{:S(2)}) %collective-permute-start.7) | collective-permute-done | bytes 491552 | tf_op jit(solution)/shard_map/ppermute | solution.py:475
  18.7 0.8 extra.12
  19.5 1.5 %collective-permute-start.11 = (bf16[2,600,128]{2,1,0:T(8,128)(2,1)S(1)}, bf16[2,600,128]{2,1,0:T(8,128)(2,1)S(1)}, u32[]{:S(2)}, u32[]{:S(2)}) collective-permute-start(bf16[2,600,128]{2,1,0:T(8,128)(2,1)S(1)} %get-tuple-element.48), channel_id=1, source_target_pairs={{0,1},{1,0},{2,3},{3,2},{4,5},{5,4},{6,7},{7,6},{8,9},{9,8},{10,11... | collective-permute-start | bytes 921608 | tf_op jit(solution)/shard_map/ppermute | solution.py:510
  21.2 1.6 %collective-permute-start.9 = (bf16[2,4,480,128]{3,2,1,0:T(8,128)(2,1)S(1)}, bf16[2,4,480,128]{3,2,1,0:T(8,128)(2,1)S(1)}, u32[]{:S(2)}, u32[]{:S(2)}) collective-permute-start(bf16[2,4,480,128]{3,2,1,0:T(8,128)(2,1)S(1)} %pad_maximum_fusion.1), channel_id=1, source_target_pairs={{0,8},{8,16},{16,24},{24,28},{28,20},{20,12},{12,4},{4,0},{2,6},{1... | collective-permute-start | bytes 2949128 | tf_op jit(solution)/shard_map/ppermute | solution.py:484
  22.9 6.2 %collective-permute-done.11.refs_3_.refs_4_ = bf16[2,600,128]{2,1,0:T(8,128)(2,1)S(1)} collective-permute-done((bf16[2,600,128]{2,1,0:T(8,128)(2,1)S(1)}, bf16[2,600,128]{2,1,0:T(8,128)(2,1)S(1)}, u32[]{:S(2)}, u32[]{:S(2)}) %collective-permute-start.11) | collective-permute-done | bytes 307232 | tf_op jit(solution)/shard_map/ppermute | solution.py:510
  29.0 0.8 extra.13
  29.8 1.3 %collective-permute-start.12 = (bf16[2,600,128]{2,1,0:T(8,128)(2,1)S(1)}, bf16[2,600,128]{2,1,0:T(8,128)(2,1)S(1)}, u32[]{:S(2)}, u32[]{:S(2)}) collective-permute-start(bf16[2,600,128]{2,1,0:T(8,128)(2,1)S(1)} %get-tuple-element.50), channel_id=1, source_target_pairs={{0,1},{1,0},{2,3},{3,2},{4,5},{5,4},{6,7},{7,6},{8,9},{9,8},{10,11... | collective-permute-start | bytes 921608 | tf_op jit(solution)/shard_map/ppermute | solution.py:510
  31.1 0.8 collective-permute-start.16
  32.0 1.6 %collective-permute-start.5 = (bf16[2,4,480,128]{3,2,1,0:T(8,128)(2,1)S(1)}, bf16[2,4,480,128]{3,2,1,0:T(8,128)(2,1)S(1)}, u32[]{:S(2)}, u32[]{:S(2)}) collective-permute-start(bf16[2,4,480,128]{3,2,1,0:T(8,128)(2,1)S(1)} %pad_maximum_fusion), channel_id=1, source_target_pairs={{0,8},{8,16},{16,24},{24,28},{28,20},{20,12},{12,4},{4,0},{2,6},{1... | collective-permute-start | bytes 2949128 | tf_op jit(solution)/shard_map/ppermute | solution.py:484
  33.7 6.4 %collective-permute-done.12.refs_2_.refs_4_ = bf16[2,600,128]{2,1,0:T(8,128)(2,1)S(1)} collective-permute-done((bf16[2,600,128]{2,1,0:T(8,128)(2,1)S(1)}, bf16[2,600,128]{2,1,0:T(8,128)(2,1)S(1)}, u32[]{:S(2)}, u32[]{:S(2)}) %collective-permute-start.12) | collective-permute-done | bytes 307232 | tf_op jit(solution)/shard_map/ppermute | solution.py:510
  40.1 0.8 extra.14
  40.9 1.1 %collective-permute-start.13 = (bf16[2,600,128]{2,1,0:T(8,128)(2,1)S(1)}, bf16[2,600,128]{2,1,0:T(8,128)(2,1)S(1)}, u32[]{:S(2)}, u32[]{:S(2)}) collective-permute-start(bf16[2,600,128]{2,1,0:T(8,128)(2,1)S(1)} %get-tuple-element.51), channel_id=1, source_target_pairs={{0,1},{1,0},{2,3},{3,2},{4,5},{5,4},{6,7},{7,6},{8,9},{9,8},{10,11... | collective-permute-start | bytes 921608 | tf_op jit(solution)/shard_map/ppermute | solution.py:510
  42.0 0.8 collective-permute-done.16.refs_3_
  42.8 2.5 %correlate.3 = (bf16[16,2520,256]{2,1,0:T(8,128)(2,1)}, bf16[1,2520,256]{2,1,0:T(8,128)(2,1)S(1)}) custom-call(s32[21]{0:T(128)S(1)} %concatenate.15.meta, bf16[1,4,480,128]{3,2,1,0:T(8,128)(2,1)S(1)} %get-tuple-element.86.refs_0_, bf16[1,4,480,128]{3,2,1,0:T(8,128)(2,1)S(1)} %collective-permute-done.7.refs_1_, ...), custom_call_target="tpu_custom_call", output_to_operand_aliasing={{0}: (6, {})} | custom-call | flops 10000001024 | bytes 1000 | tf_op jit(solution)/shard_map/correlate/pallas_call | solution.py:391
  45.3 1.2 %collective-permute-start.10 = (bf16[2,4,480,128]{3,2,1,0:T(8,128)(2,1)S(1)}, bf16[2,4,480,128]{3,2,1,0:T(8,128)(2,1)S(1)}, u32[]{:S(2)}, u32[]{:S(2)}) collective-permute-start(bf16[2,4,480,128]{3,2,1,0:T(8,128)(2,1)S(1)} %collective-permute-done.9.refs_0_.refs_2_), channel_id=1, source_target_pairs={{0,8},{8,16},{16,24},{24,28},{28,20},{20,12},{12,4},{4,0},{2,6},{1... | collective-permute-start | bytes 2949128 | tf_op jit(solution)/shard_map/ppermute | solution.py:484
  46.5 1.9 %collective-permute-done.13.refs_2_.refs_3_ = bf16[2,600,128]{2,1,0:T(8,128)(2,1)S(1)} collective-permute-done((bf16[2,600,128]{2,1,0:T(8,128)(2,1)S(1)}, bf16[2,600,128]{2,1,0:T(8,128)(2,1)S(1)}, u32[]{:S(2)}, u32[]{:S(2)}) %collective-permute-start.13) | collective-permute-done | bytes 307232 | tf_op jit(solution)/shard_map/ppermute | solution.py:510
  48.7 0.8 extra.15
  49.5 1.3 %collective-permute-start.17 = (bf16[2,600,128]{2,1,0:T(8,128)(2,1)S(1)}, bf16[2,600,128]{2,1,0:T(8,128)(2,1)S(1)}, u32[]{:S(2)}, u32[]{:S(2)}) collective-permute-start(bf16[2,600,128]{2,1,0:T(8,128)(2,1)S(1)} %get-tuple-element.58), channel_id=1, source_target_pairs={{0,1},{1,0},{2,3},{3,2},{4,5},{5,4},{6,7},{7,6},{8,9},{9,8},{10,11... | collective-permute-start | bytes 921608 | tf_op jit(solution)/shard_map/ppermute | solution.py:510
  50.8 1.6 %collective-permute-start.6 = (bf16[1,4,480,128]{3,2,1,0:T(8,128)(2,1)S(1)}, bf16[1,4,480,128]{3,2,1,0:T(8,128)(2,1)S(1)}, u32[]{:S(2)}, u32[]{:S(2)}) collective-permute-start(bf16[1,4,480,128]{3,2,1,0:T(8,128)(2,1)S(1)} %slice.8), channel_id=1, source_target_pairs={{0,8},{8,16},{16,24},{24,28},{28,20},{20,12},{12,4},{4,0},{2,6},{1... | collective-permute-start | bytes 1474568 | tf_op jit(solution)/shard_map/ppermute | solution.py:484
  52.5 3.3 %correlate.4 = (bf16[16,2520,256]{2,1,0:T(8,128)(2,1)}, bf16[2,2520,256]{2,1,0:T(8,128)(2,1)S(1)}) custom-call(s32[21]{0:T(128)S(1)} %concatenate.15.meta, bf16[1,4,480,128]{3,2,1,0:T(8,128)(2,1)S(1)} %collective-permute-done.refs_0_, bf16[1,4,480,128]{3,2,1,0:T(8,128)(2,1)S(1)} %collective-permute-done.3.refs_1_, ...), custom_call_target="tpu_custom_call", output_to_operand_aliasing={{0}: (7, {})} | custom-call | flops 10000001024 | bytes 1000 | tf_op jit(solution)/shard_map/correlate/pallas_call | solution.py:391
  55.9 2.1 %collective-permute-done.17.refs_2_.refs_1_ = bf16[2,600,128]{2,1,0:T(8,128)(2,1)S(1)} collective-permute-done((bf16[2,600,128]{2,1,0:T(8,128)(2,1)S(1)}, bf16[2,600,128]{2,1,0:T(8,128)(2,1)S(1)}, u32[]{:S(2)}, u32[]{:S(2)}) %collective-permute-start.17) | collective-permute-done | bytes 307232 | tf_op jit(solution)/shard_map/ppermute | solution.py:510
  58.0 1.5 %collective-permute-done.10.refs_0_.refs_2_ = bf16[2,4,480,128]{3,2,1,0:T(8,128)(2,1)S(1)} collective-permute-done((bf16[2,4,480,128]{3,2,1,0:T(8,128)(2,1)S(1)}, bf16[2,4,480,128]{3,2,1,0:T(8,128)(2,1)S(1)}, u32[]{:S(2)}, u32[]{:S(2)}) %collective-permute-start.10) | collective-permute-done | bytes 983072 | tf_op jit(solution)/shard_map/ppermute | solution.py:484
  59.5 0.8 extra.16
  60.2 1.1 %collective-permute-start.22 = (bf16[2,600,128]{2,1,0:T(8,128)(2,1)S(1)}, bf16[2,600,128]{2,1,0:T(8,128)(2,1)S(1)}, u32[]{:S(2)}, u32[]{:S(2)}) collective-permute-start(bf16[2,600,128]{2,1,0:T(8,128)(2,1)S(1)} %get-tuple-element.62), channel_id=1, source_target_pairs={{0,1},{1,0},{2,3},{3,2},{4,5},{5,4},{6,7},{7,6},{8,9},{9,8},{10,11... | collective-permute-start | bytes 921608 | tf_op jit(solution)/shard_map/ppermute | solution.py:510
  61.3 1.6 %collective-permute-start.19 = (bf16[2,4,480,128]{3,2,1,0:T(8,128)(2,1)S(1)}, bf16[2,4,480,128]{3,2,1,0:T(8,128)(2,1)S(1)}, u32[]{:S(2)}, u32[]{:S(2)}) collective-permute-start(bf16[2,4,480,128]{3,2,1,0:T(8,128)(2,1)S(1)} %collective-permute-done.10.refs_0_.refs_2_), channel_id=1, source_target_pairs={{0,8},{8,16},{16,24},{24,28},{28,20},{20,12},{12,4},{4,0},{2,6},{1... | collective-permute-start | bytes 2949128 | tf_op jit(solution)/shard_map/ppermute | solution.py:484
  62.9 1.8 %collective-permute-done.6.refs_0_ = bf16[1,4,480,128]{3,2,1,0:T(8,128)(2,1)S(1)} collective-permute-done((bf16[1,4,480,128]{3,2,1,0:T(8,128)(2,1)S(1)}, bf16[1,4,480,128]{3,2,1,0:T(8,128)(2,1)S(1)}, u32[]{:S(2)}, u32[]{:S(2)}) %collective-permute-start.6) | collective-permute-done | bytes 491552 | tf_op jit(solution)/shard_map/ppermute | solution.py:484
  64.7 0.7 extra.17
  65.4 1.2 %collective-permute-start.24 = (bf16[1,600,128]{2,1,0:T(8,128)(2,1)S(1)}, bf16[1,600,128]{2,1,0:T(8,128)(2,1)S(1)}, u32[]{:S(2)}, u32[]{:S(2)}) collective-permute-start(bf16[1,600,128]{2,1,0:T(8,128)(2,1)S(1)} %get-tuple-element.66), channel_id=1, source_target_pairs={{0,1},{1,0},{2,3},{3,2},{4,5},{5,4},{6,7},{7,6},{8,9},{9,8},{10,11... | collective-permute-start | bytes 460808 | tf_op jit(solution)/shard_map/ppermute | solution.py:548
  66.6 3.9 %collective-permute-done.22.refs_3_ = bf16[2,600,128]{2,1,0:T(8,128)(2,1)S(1)} collective-permute-done((bf16[2,600,128]{2,1,0:T(8,128)(2,1)S(1)}, bf16[2,600,128]{2,1,0:T(8,128)(2,1)S(1)}, u32[]{:S(2)}, u32[]{:S(2)}) %collective-permute-start.22) | collective-permute-done | bytes 307232 | tf_op jit(solution)/shard_map/ppermute | solution.py:510
  70.5 3.5 %correlate.5 = (bf16[16,2520,256]{2,1,0:T(8,128)(2,1)}, bf16[2,2520,256]{2,1,0:T(8,128)(2,1)S(1)}) custom-call(s32[21]{0:T(128)S(1)} %concatenate.15.meta, bf16[1,4,480,128]{3,2,1,0:T(8,128)(2,1)S(1)} %collective-permute-done.1.refs_0_, bf16[1,4,480,128]{3,2,1,0:T(8,128)(2,1)S(1)} %collective-permute-done.4.refs_1_, ...), custom_call_target="tpu_custom_call", output_to_operand_aliasing={{0}: (8, {})} | custom-call | flops 10000001024 | bytes 1000 | tf_op jit(solution)/shard_map/correlate/pallas_call | solution.py:391
  74.6 0.8 collective-permute-done.19.refs_0_.refs_1_
  75.5 1.6 %collective-permute-start.20 = (bf16[1,4,480,128]{3,2,1,0:T(8,128)(2,1)S(1)}, bf16[1,4,480,128]{3,2,1,0:T(8,128)(2,1)S(1)}, u32[]{:S(2)}, u32[]{:S(2)}) collective-permute-start(bf16[1,4,480,128]{3,2,1,0:T(8,128)(2,1)S(1)} %slice.9), channel_id=1, source_target_pairs={{0,8},{8,16},{16,24},{24,28},{28,20},{20,12},{12,4},{4,0},{2,6},{1... | collective-permute-start | bytes 1474568 | tf_op jit(solution)/shard_map/ppermute | solution.py:484
  77.1 0.8 extra.18
  77.9 0.9 collective-permute-start.26
  78.8 2.0 %raw_rows.2 = (bf16[16,2520,256]{2,1,0:T(8,128)(2,1)}, bf16[2,2520,256]{2,1,0:T(8,128)(2,1)S(1)}, bf16[2,2520,256]{2,1,0:T(8,128)(2,1)S(1)}) custom-call(s32[21]{0:T(128)S(1)} %concatenate.15.meta, bf16[2,4,480,128]{3,2,1,0:T(8,128)(2,1)S(1)} %collective-permute-done.5.refs_0_, ...), custom_call_target="tpu_custom_call", output_to_operand_aliasing={{0}: (5, {})} | custom-call | flops 10000001024 | bytes 1000 | tf_op jit(solution)/shard_map/raw_rows/pallas_call | solution.py:417
  80.9 3.4 %collective-permute-done.20.refs_0_ = bf16[1,4,480,128]{3,2,1,0:T(8,128)(2,1)S(1)} collective-permute-done((bf16[1,4,480,128]{3,2,1,0:T(8,128)(2,1)S(1)}, bf16[1,4,480,128]{3,2,1,0:T(8,128)(2,1)S(1)}, u32[]{:S(2)}, u32[]{:S(2)}) %collective-permute-start.20) | collective-permute-done | bytes 491552 | tf_op jit(solution)/shard_map/ppermute | solution.py:484
  85.1 1.0 %collective-permute-start.29 = (bf16[1,600,128]{2,1,0:T(8,128)(2,1)S(1)}, bf16[1,600,128]{2,1,0:T(8,128)(2,1)S(1)}, u32[]{:S(2)}, u32[]{:S(2)}) collective-permute-start(bf16[1,600,128]{2,1,0:T(8,128)(2,1)S(1)} %get-tuple-element.78), channel_id=1, source_target_pairs={{0,1},{1,0},{2,3},{3,2},{4,5},{5,4},{6,7},{7,6},{8,9},{9,8},{10,11... | collective-permute-start | bytes 460808 | tf_op jit(solution)/shard_map/ppermute | solution.py:548
  86.1 2.1 %came_rows.2 = (bf16[16,2520,256]{2,1,0:T(8,128)(2,1)}, bf16[2,2520,256]{2,1,0:T(8,128)(2,1)S(1)}, bf16[2,600,256]{2,1,0:T(8,128)(2,1)S(1)}) custom-call(s32[21]{0:T(128)S(1)} %concatenate.15.meta, bf16[2,600,128]{2,1,0:T(8,128)(2,1)S(1)} %collective-permute-done.26.refs_0_, ...), custom_call_target="tpu_custom_call", output_to_operand_aliasing={{0}: (4, {}), {1}: (5, {})} | custom-call | flops 22000001024 | bytes 1000 | tf_op jit(solution)/shard_map/came_rows/pallas_call | solution.py:439
  88.4 3.0 %raw_rows.3 = (bf16[16,2520,256]{2,1,0:T(8,128)(2,1)}, bf16[2,2520,256]{2,1,0:T(8,128)(2,1)S(1)}) custom-call(s32[21]{0:T(128)S(1)} %concatenate.15.meta, bf16[1,4,480,128]{3,2,1,0:T(8,128)(2,1)S(1)} %get-tuple-element.60.refs_0_, bf16[1,4,480,128]{3,2,1,0:T(8,128)(2,1)S(1)} %collective-permute-done.18.refs_6_.refs_1_, ...), custom_call_target="tpu_custom_call", output_to_operand_aliasing={{0}: (8, {})} | custom-call | flops 10000001024 | bytes 1000 | tf_op jit(solution)/shard_map/raw_rows/pallas_call | solution.py:417
  92.0 0.9 collective-permute-done.30.refs_1_
  93.2 2.2 %came_rows.3 = (bf16[16,2520,256]{2,1,0:T(8,128)(2,1)}, bf16[2,2520,256]{2,1,0:T(8,128)(2,1)S(1)}, bf16[2,2520,256]{2,1,0:T(8,128)(2,1)S(1)}) custom-call(s32[21]{0:T(128)S(1)} %concatenate.15.meta, bf16[1,600,128]{2,1,0:T(8,128)(2,1)S(1)} %get-tuple-element.79.refs_0_, ...), custom_call_target="tpu_custom_call", output_to_operand_aliasing={{0}: (7, {}), {1}: (8, {}), {2}: (9, {})} | custom-call | flops 1000 | bytes 1000 | tf_op jit(solution)/shard_map/came_rows/pallas_call | solution.py:439
  (47 shorter events, 6.2 us)
Async XLA Ops:
  1.2 7.0 %collective-permute-start.2 = (bf16[1,4,480,128]{3,2,1,0:T(8,128)(2,1)S(1)}, bf16[1,4,480,128]{3,2,1,0:T(8,128)(2,1)S(1)}, u32[]{:S(2)}, u32[]{:S(2)}) collective-permute-start(bf16[1,4,480,128]{3,2,1,0:T(8,128)(2,1)S(1)} %get-tuple-element.86.refs_0_), channel_id=1, source_target_pairs={{0,2},{2,0},{4,6},{6,4},{8,10},{10,8},{12,14},{14,12},{16,18},{18,... | collective-permute-start | bytes 1474568 | tf_op jit(solution)/shard_map/ppermute | solution.py:484
  1.8 9.4 %collective-permute-start = (bf16[1,4,480,128]{3,2,1,0:T(8,128)(2,1)S(1)}, bf16[1,4,480,128]{3,2,1,0:T(8,128)(2,1)S(1)}, u32[]{:S(2)}, u32[]{:S(2)}) collective-permute-start(bf16[1,4,480,128]{3,2,1,0:T(8,128)(2,1)S(1)} %get-tuple-element.86.refs_0_), channel_id=1, source_target_pairs={{0,8},{8,16},{16,24},{24,28},{28,20},{20,12},{12,4},{4,0},{2,6},{1... | collective-permute-start | bytes 1474568 | tf_op jit(solution)/shard_map/ppermute | solution.py:484
  4.4 13.9 %collective-permute-start.7 = (bf16[1,4,480,128]{3,2,1,0:T(8,128)(2,1)S(1)}, bf16[1,4,480,128]{3,2,1,0:T(8,128)(2,1)S(1)}, u32[]{:S(2)}, u32[]{:S(2)}) collective-permute-start(bf16[1,4,480,128]{3,2,1,0:T(8,128)(2,1)S(1)} %get-tuple-element.85.refs_0_), channel_id=1, source_target_pairs={{0,1},{1,0},{2,3},{3,2},{4,5},{5,4},{6,7},{7,6},{8,9},{9,8},{10,11... | collective-permute-start | bytes 1474568 | tf_op jit(solution)/shard_map/ppermute | solution.py:475
  6.8 14.2 %collective-permute-start.14 = (bf16[256,128]{0,1:T(8,128)(2,1)S(1)}, bf16[256,128]{0,1:T(8,128)(2,1)S(1)}, u32[]{:S(2)}, u32[]{:S(2)}) collective-permute-start(bf16[256,128]{0,1:T(8,128)(2,1)S(1)} %copy.27), channel_id=1, source_target_pairs={{0,1},{1,0},{2,3},{3,2},{4,5},{5,4},{6,7},{7,6},{8,9},{9,8},{10,11... | collective-permute-start | bytes 196616 | tf_op jit(solution)/shard_map/ppermute | solution.py:476
  8.2 10.1 %collective-permute-start.3 = (bf16[1,4,480,128]{3,2,1,0:T(8,128)(2,1)S(1)}, bf16[1,4,480,128]{3,2,1,0:T(8,128)(2,1)S(1)}, u32[]{:S(2)}, u32[]{:S(2)}) collective-permute-start(bf16[1,4,480,128]{3,2,1,0:T(8,128)(2,1)S(1)} %collective-permute-done.2), channel_id=1, source_target_pairs={{0,8},{8,16},{16,24},{24,28},{28,20},{20,12},{12,4},{4,0},{2,6},{1... | collective-permute-start | bytes 1474568 | tf_op jit(solution)/shard_map/ppermute | solution.py:484
  11.2 11.7 %collective-permute-start.1 = (bf16[1,4,480,128]{3,2,1,0:T(8,128)(2,1)S(1)}, bf16[1,4,480,128]{3,2,1,0:T(8,128)(2,1)S(1)}, u32[]{:S(2)}, u32[]{:S(2)}) collective-permute-start(bf16[1,4,480,128]{3,2,1,0:T(8,128)(2,1)S(1)} %collective-permute-done.refs_0_), channel_id=1, source_target_pairs={{0,8},{8,16},{16,24},{24,28},{28,20},{20,12},{12,4},{4,0},{2,6},{1... | collective-permute-start | bytes 1474568 | tf_op jit(solution)/shard_map/ppermute | solution.py:484
  18.3 2.8 %collective-permute-start.8 = (bf16[1,4,480,128]{3,2,1,0:T(8,128)(2,1)S(1)}, bf16[1,4,480,128]{3,2,1,0:T(8,128)(2,1)S(1)}, u32[]{:S(2)}, u32[]{:S(2)}) collective-permute-start(bf16[1,4,480,128]{3,2,1,0:T(8,128)(2,1)S(1)} %collective-permute-done.7.refs_1_), channel_id=1, source_target_pairs={{0,2},{2,0},{4,6},{6,4},{8,10},{10,8},{12,14},{14,12},{16,18},{18,... | collective-permute-start | bytes 1474568 | tf_op jit(solution)/shard_map/ppermute | solution.py:484
  18.3 10.7 %collective-permute-start.4 = (bf16[1,4,480,128]{3,2,1,0:T(8,128)(2,1)S(1)}, bf16[1,4,480,128]{3,2,1,0:T(8,128)(2,1)S(1)}, u32[]{:S(2)}, u32[]{:S(2)}) collective-permute-start(bf16[1,4,480,128]{3,2,1,0:T(8,128)(2,1)S(1)} %collective-permute-done.3.refs_1_), channel_id=1, source_target_pairs={{0,8},{8,16},{16,24},{24,28},{28,20},{20,12},{12,4},{4,0},{2,6},{1... | collective-permute-start | bytes 1474568 | tf_op jit(solution)/shard_map/ppermute | solution.py:484
  19.5 9.6 %collective-permute-start.11 = (bf16[2,600,128]{2,1,0:T(8,128)(2,1)S(1)}, bf16[2,600,128]{2,1,0:T(8,128)(2,1)S(1)}, u32[]{:S(2)}, u32[]{:S(2)}) collective-permute-start(bf16[2,600,128]{2,1,0:T(8,128)(2,1)S(1)} %get-tuple-element.48), channel_id=1, source_target_pairs={{0,1},{1,0},{2,3},{3,2},{4,5},{5,4},{6,7},{7,6},{8,9},{9,8},{10,11... | collective-permute-start | bytes 921608 | tf_op jit(solution)/shard_map/ppermute | solution.py:510
  21.0 10.9 %collective-permute-start.15 = (bf16[256,256]{1,0:T(8,128)(2,1)S(1)}, bf16[256,256]{1,0:T(8,128)(2,1)S(1)}, u32[]{:S(2)}, u32[]{:S(2)}) collective-permute-start(bf16[256,256]{1,0:T(8,128)(2,1)S(1)} %pad_maximum_fusion.3.refs_4_), channel_id=1, source_target_pairs={{0,2},{2,0},{4,6},{6,4},{8,10},{10,8},{12,14},{14,12},{16,18},{18,... | collective-permute-start | bytes 393224 | tf_op jit(solution)/shard_map/ppermute | solution.py:479
  21.2 18.9 %collective-permute-start.9 = (bf16[2,4,480,128]{3,2,1,0:T(8,128)(2,1)S(1)}, bf16[2,4,480,128]{3,2,1,0:T(8,128)(2,1)S(1)}, u32[]{:S(2)}, u32[]{:S(2)}) collective-permute-start(bf16[2,4,480,128]{3,2,1,0:T(8,128)(2,1)S(1)} %pad_maximum_fusion.1), channel_id=1, source_target_pairs={{0,8},{8,16},{16,24},{24,28},{28,20},{20,12},{12,4},{4,0},{2,6},{1... | collective-permute-start | bytes 2949128 | tf_op jit(solution)/shard_map/ppermute | solution.py:484
  29.8 10.3 %collective-permute-start.12 = (bf16[2,600,128]{2,1,0:T(8,128)(2,1)S(1)}, bf16[2,600,128]{2,1,0:T(8,128)(2,1)S(1)}, u32[]{:S(2)}, u32[]{:S(2)}) collective-permute-start(bf16[2,600,128]{2,1,0:T(8,128)(2,1)S(1)} %get-tuple-element.50), channel_id=1, source_target_pairs={{0,1},{1,0},{2,3},{3,2},{4,5},{5,4},{6,7},{7,6},{8,9},{9,8},{10,11... | collective-permute-start | bytes 921608 | tf_op jit(solution)/shard_map/ppermute | solution.py:510
  31.1 11.7 %collective-permute-start.16 = (bf16[1,600,128]{2,1,0:T(8,128)(2,1)S(1)}, bf16[1,600,128]{2,1,0:T(8,128)(2,1)S(1)}, u32[]{:S(2)}, u32[]{:S(2)}) collective-permute-start(bf16[1,600,128]{2,1,0:T(8,128)(2,1)S(1)} %get-tuple-element.53), channel_id=1, source_target_pairs={{0,1},{1,0},{2,3},{3,2},{4,5},{5,4},{6,7},{7,6},{8,9},{9,8},{10,11... | collective-permute-start | bytes 460808 | tf_op jit(solution)/shard_map/ppermute | solution.py:510
  32.0 16.7 %collective-permute-start.5 = (bf16[2,4,480,128]{3,2,1,0:T(8,128)(2,1)S(1)}, bf16[2,4,480,128]{3,2,1,0:T(8,128)(2,1)S(1)}, u32[]{:S(2)}, u32[]{:S(2)}) collective-permute-start(bf16[2,4,480,128]{3,2,1,0:T(8,128)(2,1)S(1)} %pad_maximum_fusion), channel_id=1, source_target_pairs={{0,8},{8,16},{16,24},{24,28},{28,20},{20,12},{12,4},{4,0},{2,6},{1... | collective-permute-start | bytes 2949128 | tf_op jit(solution)/shard_map/ppermute | solution.py:484
  40.9 7.6 %collective-permute-start.13 = (bf16[2,600,128]{2,1,0:T(8,128)(2,1)S(1)}, bf16[2,600,128]{2,1,0:T(8,128)(2,1)S(1)}, u32[]{:S(2)}, u32[]{:S(2)}) collective-permute-start(bf16[2,600,128]{2,1,0:T(8,128)(2,1)S(1)} %get-tuple-element.51), channel_id=1, source_target_pairs={{0,1},{1,0},{2,3},{3,2},{4,5},{5,4},{6,7},{7,6},{8,9},{9,8},{10,11... | collective-permute-start | bytes 921608 | tf_op jit(solution)/shard_map/ppermute | solution.py:510
  45.2 25.3 %collective-permute-start.23 = (bf16[1,2520,256]{2,1,0:T(8,128)(2,1)S(1)}, bf16[1,2520,256]{2,1,0:T(8,128)(2,1)S(1)}, u32[]{:S(2)}, u32[]{:S(2)}) collective-permute-start(bf16[1,2520,256]{2,1,0:T(8,128)(2,1)S(1)} %get-tuple-element.63), channel_id=1, source_target_pairs={{0,2},{2,0},{4,6},{6,4},{8,10},{10,8},{12,14},{14,12},{16,18},{18,... | collective-permute-start | bytes 3870728 | tf_op jit(solution)/shard_map/ppermute | solution.py:484
  45.3 14.1 %collective-permute-start.10 = (bf16[2,4,480,128]{3,2,1,0:T(8,128)(2,1)S(1)}, bf16[2,4,480,128]{3,2,1,0:T(8,128)(2,1)S(1)}, u32[]{:S(2)}, u32[]{:S(2)}) collective-permute-start(bf16[2,4,480,128]{3,2,1,0:T(8,128)(2,1)S(1)} %collective-permute-done.9.refs_0_.refs_2_), channel_id=1, source_target_pairs={{0,8},{8,16},{16,24},{24,28},{28,20},{20,12},{12,4},{4,0},{2,6},{1... | collective-permute-start | bytes 2949128 | tf_op jit(solution)/shard_map/ppermute | solution.py:484
  49.5 8.5 %collective-permute-start.17 = (bf16[2,600,128]{2,1,0:T(8,128)(2,1)S(1)}, bf16[2,600,128]{2,1,0:T(8,128)(2,1)S(1)}, u32[]{:S(2)}, u32[]{:S(2)}) collective-permute-start(bf16[2,600,128]{2,1,0:T(8,128)(2,1)S(1)} %get-tuple-element.58), channel_id=1, source_target_pairs={{0,1},{1,0},{2,3},{3,2},{4,5},{5,4},{6,7},{7,6},{8,9},{9,8},{10,11... | collective-permute-start | bytes 921608 | tf_op jit(solution)/shard_map/ppermute | solution.py:510
  50.8 13.9 %collective-permute-start.6 = (bf16[1,4,480,128]{3,2,1,0:T(8,128)(2,1)S(1)}, bf16[1,4,480,128]{3,2,1,0:T(8,128)(2,1)S(1)}, u32[]{:S(2)}, u32[]{:S(2)}) collective-permute-start(bf16[1,4,480,128]{3,2,1,0:T(8,128)(2,1)S(1)} %slice.8), channel_id=1, source_target_pairs={{0,8},{8,16},{16,24},{24,28},{28,20},{20,12},{12,4},{4,0},{2,6},{1... | collective-permute-start | bytes 1474568 | tf_op jit(solution)/shard_map/ppermute | solution.py:484
  55.8 23.0 %collective-permute-start.21 = (bf16[2,2520,256]{2,1,0:T(8,128)(2,1)S(1)}, bf16[2,2520,256]{2,1,0:T(8,128)(2,1)S(1)}, u32[]{:S(2)}, u32[]{:S(2)}) collective-permute-start(bf16[2,2520,256]{2,1,0:T(8,128)(2,1)S(1)} %get-tuple-element.61), channel_id=1, source_target_pairs={{0,2},{2,0},{4,6},{6,4},{8,10},{10,8},{12,14},{14,12},{16,18},{18,... | collective-permute-start | bytes 7741448 | tf_op jit(solution)/shard_map/ppermute | solution.py:484
  60.2 10.3 %collective-permute-start.22 = (bf16[2,600,128]{2,1,0:T(8,128)(2,1)S(1)}, bf16[2,600,128]{2,1,0:T(8,128)(2,1)S(1)}, u32[]{:S(2)}, u32[]{:S(2)}) collective-permute-start(bf16[2,600,128]{2,1,0:T(8,128)(2,1)S(1)} %get-tuple-element.62), channel_id=1, source_target_pairs={{0,1},{1,0},{2,3},{3,2},{4,5},{5,4},{6,7},{7,6},{8,9},{9,8},{10,11... | collective-permute-start | bytes 921608 | tf_op jit(solution)/shard_map/ppermute | solution.py:510
  61.3 14.1 %collective-permute-start.19 = (bf16[2,4,480,128]{3,2,1,0:T(8,128)(2,1)S(1)}, bf16[2,4,480,128]{3,2,1,0:T(8,128)(2,1)S(1)}, u32[]{:S(2)}, u32[]{:S(2)}) collective-permute-start(bf16[2,4,480,128]{3,2,1,0:T(8,128)(2,1)S(1)} %collective-permute-done.10.refs_0_.refs_2_), channel_id=1, source_target_pairs={{0,8},{8,16},{16,24},{24,28},{28,20},{20,12},{12,4},{4,0},{2,6},{1... | collective-permute-start | bytes 2949128 | tf_op jit(solution)/shard_map/ppermute | solution.py:484
  65.4 11.7 %collective-permute-start.24 = (bf16[1,600,128]{2,1,0:T(8,128)(2,1)S(1)}, bf16[1,600,128]{2,1,0:T(8,128)(2,1)S(1)}, u32[]{:S(2)}, u32[]{:S(2)}) collective-permute-start(bf16[1,600,128]{2,1,0:T(8,128)(2,1)S(1)} %get-tuple-element.66), channel_id=1, source_target_pairs={{0,1},{1,0},{2,3},{3,2},{4,5},{5,4},{6,7},{7,6},{8,9},{9,8},{10,11... | collective-permute-start | bytes 460808 | tf_op jit(solution)/shard_map/ppermute | solution.py:548
  70.5 14.6 %collective-permute-start.18 = (bf16[1,4,480,128]{3,2,1,0:T(8,128)(2,1)S(1)}, bf16[1,4,480,128]{3,2,1,0:T(8,128)(2,1)S(1)}, u32[]{:S(2)}, u32[]{:S(2)}) collective-permute-start(bf16[1,4,480,128]{3,2,1,0:T(8,128)(2,1)S(1)} %get-tuple-element.60.refs_0_), channel_id=1, source_target_pairs={{0,2},{2,0},{4,6},{6,4},{8,10},{10,8},{12,14},{14,12},{16,18},{18,... | collective-permute-start | bytes 1474568 | tf_op jit(solution)/shard_map/ppermute | solution.py:484
  74.0 12.1 %collective-permute-start.27 = (bf16[2,2520,256]{2,1,0:T(8,128)(2,1)S(1)}, bf16[2,2520,256]{2,1,0:T(8,128)(2,1)S(1)}, u32[]{:S(2)}, u32[]{:S(2)}) collective-permute-start(bf16[2,2520,256]{2,1,0:T(8,128)(2,1)S(1)} %get-tuple-element.73), channel_id=1, source_target_pairs={{0,2},{2,0},{4,6},{6,4},{8,10},{10,8},{12,14},{14,12},{16,18},{18,... | collective-permute-start | bytes 7741448 | tf_op jit(solution)/shard_map/ppermute | solution.py:484
  75.5 8.9 %collective-permute-start.20 = (bf16[1,4,480,128]{3,2,1,0:T(8,128)(2,1)S(1)}, bf16[1,4,480,128]{3,2,1,0:T(8,128)(2,1)S(1)}, u32[]{:S(2)}, u32[]{:S(2)}) collective-permute-start(bf16[1,4,480,128]{3,2,1,0:T(8,128)(2,1)S(1)} %slice.9), channel_id=1, source_target_pairs={{0,8},{8,16},{16,24},{24,28},{28,20},{20,12},{12,4},{4,0},{2,6},{1... | collective-permute-start | bytes 1474568 | tf_op jit(solution)/shard_map/ppermute | solution.py:484
  77.9 8.2 %collective-permute-start.26 = (bf16[2,600,128]{2,1,0:T(8,128)(2,1)S(1)}, bf16[2,600,128]{2,1,0:T(8,128)(2,1)S(1)}, u32[]{:S(2)}, u32[]{:S(2)}) collective-permute-start(bf16[2,600,128]{2,1,0:T(8,128)(2,1)S(1)} %get-tuple-element.70), channel_id=1, source_target_pairs={{0,1},{1,0},{2,3},{3,2},{4,5},{5,4},{6,7},{7,6},{8,9},{9,8},{10,11... | collective-permute-start | bytes 921608 | tf_op jit(solution)/shard_map/ppermute | solution.py:566
  80.9 7.6 %collective-permute-start.28 = (bf16[2,2520,256]{2,1,0:T(8,128)(2,1)S(1)}, bf16[2,2520,256]{2,1,0:T(8,128)(2,1)S(1)}, u32[]{:S(2)}, u32[]{:S(2)}) collective-permute-start(bf16[2,2520,256]{2,1,0:T(8,128)(2,1)S(1)} %get-tuple-element.75), channel_id=1, source_target_pairs={{0,2},{2,0},{4,6},{6,4},{8,10},{10,8},{12,14},{14,12},{16,18},{18,... | collective-permute-start | bytes 7741448 | tf_op jit(solution)/shard_map/ppermute | solution.py:484
  85.0 3.4 %collective-permute-start.25 = (bf16[1,4,480,128]{3,2,1,0:T(8,128)(2,1)S(1)}, bf16[1,4,480,128]{3,2,1,0:T(8,128)(2,1)S(1)}, u32[]{:S(2)}, u32[]{:S(2)}) collective-permute-start(bf16[1,4,480,128]{3,2,1,0:T(8,128)(2,1)S(1)} %get-tuple-element.69.refs_2_), channel_id=1, source_target_pairs={{0,2},{2,0},{4,6},{6,4},{8,10},{10,8},{12,14},{14,12},{16,18},{18,... | collective-permute-start | bytes 1474568 | tf_op jit(solution)/shard_map/ppermute | solution.py:484
  85.1 6.4 %collective-permute-start.29 = (bf16[1,600,128]{2,1,0:T(8,128)(2,1)S(1)}, bf16[1,600,128]{2,1,0:T(8,128)(2,1)S(1)}, u32[]{:S(2)}, u32[]{:S(2)}) collective-permute-start(bf16[1,600,128]{2,1,0:T(8,128)(2,1)S(1)} %get-tuple-element.78), channel_id=1, source_target_pairs={{0,1},{1,0},{2,3},{3,2},{4,5},{5,4},{6,7},{7,6},{8,9},{9,8},{10,11... | collective-permute-start | bytes 460808 | tf_op jit(solution)/shard_map/ppermute | solution.py:548
  88.2 3.8 %collective-permute-start.32 = (bf16[2,600,256]{2,1,0:T(8,128)(2,1)S(1)}, bf16[2,600,256]{2,1,0:T(8,128)(2,1)S(1)}, u32[]{:S(2)}, u32[]{:S(2)}) collective-permute-start(bf16[2,600,256]{2,1,0:T(8,128)(2,1)S(1)} %get-tuple-element.81), channel_id=1, source_target_pairs={{0,2},{2,0},{4,6},{6,4},{8,10},{10,8},{12,14},{14,12},{16,18},{18,... | collective-permute-start | bytes 1843208 | tf_op jit(solution)/shard_map/ppermute | solution.py:484
  91.5 1.4 %collective-permute-start.30 = (bf16[1,600,128]{2,1,0:T(8,128)(2,1)S(1)}, bf16[1,600,128]{2,1,0:T(8,128)(2,1)S(1)}, u32[]{:S(2)}, u32[]{:S(2)}) collective-permute-start(bf16[1,600,128]{2,1,0:T(8,128)(2,1)S(1)} %get-tuple-element.79.refs_0_), channel_id=1, source_target_pairs={{0,2},{2,0},{4,6},{6,4},{8,10},{10,8},{12,14},{14,12},{16,18},{18,... | collective-permute-start | bytes 460808 | tf_op jit(solution)/shard_map/ppermute | solution.py:484
  91.8 1.4 %collective-permute-start.31 = (bf16[1,600,128]{2,1,0:T(8,128)(2,1)S(1)}, bf16[1,600,128]{2,1,0:T(8,128)(2,1)S(1)}, u32[]{:S(2)}, u32[]{:S(2)}) collective-permute-start(bf16[1,600,128]{2,1,0:T(8,128)(2,1)S(1)} %get-tuple-element.80.refs_2_), channel_id=1, source_target_pairs={{0,2},{2,0},{4,6},{6,4},{8,10},{10,8},{12,14},{14,12},{16,18},{18,... | collective-permute-start | bytes 460808 | tf_op jit(solution)/shard_map/ppermute | solution.py:484

commit v2 on v1

--- a/solution.py
+++ b/solution.py
@@ -8,7 +8,7 @@
 from jax.sharding import PartitionSpec as P
 
 LANES = 128
-PARAMS = {'LAG': 2, 'F0': 10, 'F1': 0, 'PS0': 2, 'JA': 3, 'JB': 1, 'C0POS': 2, 'GATE': 30, 'F3': 10, 'F2': 22, 'NL': 1, 'PE4': 0, 'P4': 0, 'P3': 1, 'CPOS': 1, 'LC': 1, 'BSPL': 0, 'X00': 10, 'X01': 10, 'C0': 10, 'X10': 10, 'X11': 10, 'C1': 10, 'X20': 10, 'X21': 10, 'C2': 10, 'X30': 10, 'X31': 10, 'C3': 10, 'X40': 10, 'X41': 10, 'C4': 10}
+PARAMS = {'LAG': 2, 'F0': 10, 'F1': 0, 'PS0': 2, 'JA': 3, 'JB': 1, 'C0POS': 2, 'GATE': 30, 'F3': 0, 'F2': 22, 'NL': 1, 'PE4': 0, 'P4': 0, 'P3': 1, 'CPOS': 1, 'LC': 0, 'BSPL': 1, 'ONEX': 1, 'X00': 10, 'X01': 10, 'C0': 10, 'X10': 10, 'X11': 10, 'C1': 10, 'X20': 10, 'X21': 10, 'C2': 3, 'X30': 10, 'X31': 3, 'C3': 10, 'X40': 10, 'X41': 10, 'C4': 10}
 
 
 def G(name):
@@ -181,12 +181,12 @@
     return (2 * raw - total) // 16 * 16
 
 
-def raw_kernel(factor, arrays, wide, landing, leaving, slots, meta, *refs):
+def raw_kernel(factor, arrays, wide, landing, leaving, slots, pins, meta, *refs):
     own, other = strips_in(refs[: arrays[0]]), strips_in(refs[arrays[0] : sum(arrays)])
     queries, *refs = refs[sum(arrays) :]
     landed = refs.pop(0) if landing else None
     leavers, refs = refs[: len(leaving)], refs[len(leaving) :]
-    _, out, done, *refs = refs
+    out, done, *refs = refs[1 + pins :]
     pair = refs.pop(0) if wide else None
     values, sums, sums_two, land_sems, sems = refs
     rows_n, cols_n, _ = own[0].shape
@@ -415,9 +415,9 @@
         passive = ([landed] if landing else []) + list(leavers)
         pins = tuple(pins)
         return pl.pallas_call(
-            functools.partial(raw_kernel, factor, (len(own), len(other)), wide, landing, leaving, slots),
+            functools.partial(raw_kernel, factor, (len(own), len(other)), wide, landing, leaving, slots, len(pins)),
             out_shape=(out_type,) + (product_type(strips, raw + count),) * (1 + wide),
-            in_specs=[scalars] + [in_vmem] * len(operands) + [anywhere] * (1 + len(passive)),
+            in_specs=[scalars] + [in_vmem] * len(operands) + [anywhere] * (1 + len(passive) + len(pins)),
             out_specs=(anywhere,) + (in_vmem,) * (1 + wide),
             scratch_shapes=[
                 pltpu.VMEM((raw + count, queries_n * (1 + wide)), jnp.float32),
@@ -429,7 +429,7 @@
             compiler_params=params,
             cost_estimate=modelled(cost),
             name="raw_rows",
-        )(meta, *operands, *passive, out)
+        )(meta, *operands, *passive, out, *pins)
 
     def came_rows(out, done, slots, own, other, wide, late=(), cost=0, pins=(), landing=()):
         operands = [*own, *other, queries_wide if wide else queries, *late[:1]]
@@ -538,7 +538,7 @@
         return permute_rows(swap, [piece])[0]
 
     def near_raw(out):
-        return raw_rows(out, *came[near], True, *landing(near), G("F3"))
+        return raw_rows(out, *came[near], True, *landing(near), G("F3"), pins=tuple(across_came[far, 1]) if G("PR") else ())
 
     swapped = []
 
@@ -559,10 +559,11 @@
         out = do_extra(out, d - 1, 1, (d, 1))
     out = far_extra(out, 0, tuple(across_came[near - 1, 0]) if G("P4") else ())
     across_came[near, 0] = []
-    for index, piece in enumerate(came[near][1]):
-        if index == len(came[near][1]) - G("CPOS"):
+    groups = [came[near][1]] if G("ONEX") else [[piece] for piece in came[near][1]]
+    for index, pieces in enumerate(groups):
+        if index == len(groups) - G("CPOS"):
             out = product(out, near - 1, now=near)
-        extra, out = make_extra(out, [piece], G("X31"), tuple(across_came[far, 1]) if G("P3") == index + 1 else ())
+        extra, out = make_extra(out, pieces, G("X31"), tuple(across_came[far, 1]) if G("P3") == index + 1 else ())
         across_came[near, 0].append(lax.ppermute(extra, "chan", across))
     out, near_done, near_pair = near_raw(out)
     out = far_extra(out, 1, (swapped[0],) if G("PS0") == 1 else ())

time: 95.8 us -> 96.2 us (level)
    ppermute x1, waiting for transfers between devices: 0.01 us -> 3.92 us  [ring_local(): across_came[near, 0].append(lax.ppermute(extra, 'chan', across))]
    ppermute x21 -> x22, waiting for transfers between devices: 9.79 us -> 7.01 us  [permute_rows(): return [lax.ppermute(piece, 'rows', pairs) for piece in pieces]]
    ppermute x6, waiting for transfers between devices: 21.3 us -> 19.7 us  [do_extra(): across_came[d, 1 - part].append(lax.ppermute(extra, 'chan', across))]
    ppermute x21 -> x22, starting transfers between devices: 18.1 us -> 19.1 us  [permute_rows(): return [lax.ppermute(piece, 'rows', pairs) for piece in pieces]]
  transfers between devices with their start and end apart: 33 -> 34, of which waited for: 16 -> 17; matrix products, arithmetic and copies ran while one was open for 1% -> 1% of each run, Pallas kernels for 25% -> 25%
where the time goes in v2:
time: 96.2 us; the launch traced here: 96 us
  waiting for transfers between devices  35.8 us (37%)
  starting transfers between devices  31.3 us (33%)
  Pallas kernels  25.8 us (27%)
  local copies, waits for them, and re-layouts  2.36 us (2%)
    ppermute x6, waiting for transfers between devices, do_extra(): across_came[d, 1 - part].append(lax.ppermute(extra, 'chan', across))  19.7 us
    ppermute x22, starting transfers between devices, permute_rows(): return [lax.ppermute(piece, 'rows', pairs) for piece in pieces]  19.1 us
    pallas_call x3, Pallas kernels, correlate(): pl.pallas_call(functools.partial(corr_kernel, factor, tuple((len(part) fo...  9.3 us
    pallas_call x10, Pallas kernels, make_extra(): pl.pallas_call(functools.partial(extra_kernel, len(halves), 2 + len(carri...  7.2 us
    ppermute x6, starting transfers between devices, do_extra(): across_came[d, 1 - part].append(lax.ppermute(extra, 'chan', across))  7.09 us
    ppermute x22, waiting for transfers between devices, permute_rows(): return [lax.ppermute(piece, 'rows', pairs) for piece in pieces]  7.01 us
    pallas_call x2, Pallas kernels, raw_rows(): pl.pallas_call(functools.partial(raw_kernel, factor, (len(own), len(other...  5.81 us
    ppermute x1, waiting for transfers between devices, ring_local(): partner = lax.ppermute(theirs, 'chan', across)  5.11 us
  transfers between devices with their start and end apart: 34, of which 17 were waited for; matrix products, arithmetic and copies ran while one was open for 1% of the time, Pallas kernels for 25%

profile of v2, /device:TPU:0, one launch (start us, length us, event | category | flops | bytes accessed | tf_op | source)
XLA Modules:
  0.0 96.0 jit_solution(14424350491796577842)
XLA Ops:
  0.0 1.2 %dynamic-slice_bitcast_fusion = (bf16[1,4,480,128]{3,2,1,0:T(8,128)(2,1)S(1)}, bf16[1,4,480,128]{3,2,1,0:T(8,128)(2,1)S(1)}) fusion(bf16[8,480,128]{2,1,0:T(8,128)(2,1)} %param.3, s32[]{:T(128)S(6)} %select_n.72, s32[]{:T(128)S(6)} %select_n.71), kind=kLoop, calls=%fused_computation.2 | loop fusion | bytes 1966088 | tf_op jit(solution)/shard_map/broadcast_in_dim | solution.py:469
  1.8 2.6 %collective-permute-start = (bf16[1,4,480,128]{3,2,1,0:T(8,128)(2,1)S(1)}, bf16[1,4,480,128]{3,2,1,0:T(8,128)(2,1)S(1)}, u32[]{:S(2)}, u32[]{:S(2)}) collective-permute-start(bf16[1,4,480,128]{3,2,1,0:T(8,128)(2,1)S(1)} %get-tuple-element.88.refs_0_), channel_id=1, source_target_pairs={{0,8},{8,16},{16,24},{24,28},{28,20},{20,12},{12,4},{4,0},{2,6},{1... | collective-permute-start | bytes 1474568 | tf_op jit(solution)/shard_map/ppermute | solution.py:484
  4.4 1.5 %collective-permute-start.7 = (bf16[1,4,480,128]{3,2,1,0:T(8,128)(2,1)S(1)}, bf16[1,4,480,128]{3,2,1,0:T(8,128)(2,1)S(1)}, u32[]{:S(2)}, u32[]{:S(2)}) collective-permute-start(bf16[1,4,480,128]{3,2,1,0:T(8,128)(2,1)S(1)} %get-tuple-element.87.refs_0_), channel_id=1, source_target_pairs={{0,1},{1,0},{2,3},{3,2},{4,5},{5,4},{6,7},{7,6},{8,9},{9,8},{10,11... | collective-permute-start | bytes 1474568 | tf_op jit(solution)/shard_map/ppermute | solution.py:475
  5.9 0.9 copy.27
  8.2 1.6 %collective-permute-start.3 = (bf16[1,4,480,128]{3,2,1,0:T(8,128)(2,1)S(1)}, bf16[1,4,480,128]{3,2,1,0:T(8,128)(2,1)S(1)}, u32[]{:S(2)}, u32[]{:S(2)}) collective-permute-start(bf16[1,4,480,128]{3,2,1,0:T(8,128)(2,1)S(1)} %collective-permute-done.2), channel_id=1, source_target_pairs={{0,8},{8,16},{16,24},{24,28},{28,20},{20,12},{12,4},{4,0},{2,6},{1... | collective-permute-start | bytes 1474568 | tf_op jit(solution)/shard_map/ppermute | solution.py:484
  10.5 0.7 collective-permute-done.refs_0_
  11.2 2.1 %collective-permute-start.1 = (bf16[1,4,480,128]{3,2,1,0:T(8,128)(2,1)S(1)}, bf16[1,4,480,128]{3,2,1,0:T(8,128)(2,1)S(1)}, u32[]{:S(2)}, u32[]{:S(2)}) collective-permute-start(bf16[1,4,480,128]{3,2,1,0:T(8,128)(2,1)S(1)} %collective-permute-done.refs_0_), channel_id=1, source_target_pairs={{0,8},{8,16},{16,24},{24,28},{28,20},{20,12},{12,4},{4,0},{2,6},{1... | collective-permute-start | bytes 1474568 | tf_op jit(solution)/shard_map/ppermute | solution.py:484
  13.2 5.1 %collective-permute-done.7.refs_1_ = bf16[1,4,480,128]{3,2,1,0:T(8,128)(2,1)S(1)} collective-permute-done((bf16[1,4,480,128]{3,2,1,0:T(8,128)(2,1)S(1)}, bf16[1,4,480,128]{3,2,1,0:T(8,128)(2,1)S(1)}, u32[]{:S(2)}, u32[]{:S(2)}) %collective-permute-start.7) | collective-permute-done | bytes 491552 | tf_op jit(solution)/shard_map/ppermute | solution.py:475
  18.7 0.8 extra.12
  19.5 1.5 %collective-permute-start.11 = (bf16[2,600,128]{2,1,0:T(8,128)(2,1)S(1)}, bf16[2,600,128]{2,1,0:T(8,128)(2,1)S(1)}, u32[]{:S(2)}, u32[]{:S(2)}) collective-permute-start(bf16[2,600,128]{2,1,0:T(8,128)(2,1)S(1)} %get-tuple-element.48), channel_id=1, source_target_pairs={{0,1},{1,0},{2,3},{3,2},{4,5},{5,4},{6,7},{7,6},{8,9},{9,8},{10,11... | collective-permute-start | bytes 921608 | tf_op jit(solution)/shard_map/ppermute | solution.py:510
  21.2 1.6 %collective-permute-start.9 = (bf16[2,4,480,128]{3,2,1,0:T(8,128)(2,1)S(1)}, bf16[2,4,480,128]{3,2,1,0:T(8,128)(2,1)S(1)}, u32[]{:S(2)}, u32[]{:S(2)}) collective-permute-start(bf16[2,4,480,128]{3,2,1,0:T(8,128)(2,1)S(1)} %pad_maximum_fusion.1), channel_id=1, source_target_pairs={{0,8},{8,16},{16,24},{24,28},{28,20},{20,12},{12,4},{4,0},{2,6},{1... | collective-permute-start | bytes 2949128 | tf_op jit(solution)/shard_map/ppermute | solution.py:484
  22.9 6.2 %collective-permute-done.11.refs_3_.refs_4_ = bf16[2,600,128]{2,1,0:T(8,128)(2,1)S(1)} collective-permute-done((bf16[2,600,128]{2,1,0:T(8,128)(2,1)S(1)}, bf16[2,600,128]{2,1,0:T(8,128)(2,1)S(1)}, u32[]{:S(2)}, u32[]{:S(2)}) %collective-permute-start.11) | collective-permute-done | bytes 307232 | tf_op jit(solution)/shard_map/ppermute | solution.py:510
  29.0 0.8 extra.13
  29.8 1.3 %collective-permute-start.12 = (bf16[2,600,128]{2,1,0:T(8,128)(2,1)S(1)}, bf16[2,600,128]{2,1,0:T(8,128)(2,1)S(1)}, u32[]{:S(2)}, u32[]{:S(2)}) collective-permute-start(bf16[2,600,128]{2,1,0:T(8,128)(2,1)S(1)} %get-tuple-element.50), channel_id=1, source_target_pairs={{0,1},{1,0},{2,3},{3,2},{4,5},{5,4},{6,7},{7,6},{8,9},{9,8},{10,11... | collective-permute-start | bytes 921608 | tf_op jit(solution)/shard_map/ppermute | solution.py:510
  31.1 0.8 collective-permute-start.16
  32.0 1.6 %collective-permute-start.5 = (bf16[2,4,480,128]{3,2,1,0:T(8,128)(2,1)S(1)}, bf16[2,4,480,128]{3,2,1,0:T(8,128)(2,1)S(1)}, u32[]{:S(2)}, u32[]{:S(2)}) collective-permute-start(bf16[2,4,480,128]{3,2,1,0:T(8,128)(2,1)S(1)} %pad_maximum_fusion), channel_id=1, source_target_pairs={{0,8},{8,16},{16,24},{24,28},{28,20},{20,12},{12,4},{4,0},{2,6},{1... | collective-permute-start | bytes 2949128 | tf_op jit(solution)/shard_map/ppermute | solution.py:484
  33.7 6.4 %collective-permute-done.12.refs_2_.refs_4_ = bf16[2,600,128]{2,1,0:T(8,128)(2,1)S(1)} collective-permute-done((bf16[2,600,128]{2,1,0:T(8,128)(2,1)S(1)}, bf16[2,600,128]{2,1,0:T(8,128)(2,1)S(1)}, u32[]{:S(2)}, u32[]{:S(2)}) %collective-permute-start.12) | collective-permute-done | bytes 307232 | tf_op jit(solution)/shard_map/ppermute | solution.py:510
  40.1 0.8 extra.14
  40.9 1.1 %collective-permute-start.13 = (bf16[2,600,128]{2,1,0:T(8,128)(2,1)S(1)}, bf16[2,600,128]{2,1,0:T(8,128)(2,1)S(1)}, u32[]{:S(2)}, u32[]{:S(2)}) collective-permute-start(bf16[2,600,128]{2,1,0:T(8,128)(2,1)S(1)} %get-tuple-element.51), channel_id=1, source_target_pairs={{0,1},{1,0},{2,3},{3,2},{4,5},{5,4},{6,7},{7,6},{8,9},{9,8},{10,11... | collective-permute-start | bytes 921608 | tf_op jit(solution)/shard_map/ppermute | solution.py:510
  42.0 0.8 collective-permute-done.16.refs_3_
  42.8 2.5 %correlate.3 = (bf16[16,2520,256]{2,1,0:T(8,128)(2,1)}, bf16[1,2520,256]{2,1,0:T(8,128)(2,1)S(1)}) custom-call(s32[21]{0:T(128)S(1)} %concatenate.15.meta, bf16[1,4,480,128]{3,2,1,0:T(8,128)(2,1)S(1)} %get-tuple-element.88.refs_0_, bf16[1,4,480,128]{3,2,1,0:T(8,128)(2,1)S(1)} %collective-permute-done.7.refs_1_, ...), custom_call_target="tpu_custom_call", output_to_operand_aliasing={{0}: (6, {})} | custom-call | flops 10000001024 | bytes 1000 | tf_op jit(solution)/shard_map/correlate/pallas_call | solution.py:391
  45.3 1.2 %collective-permute-start.10 = (bf16[2,4,480,128]{3,2,1,0:T(8,128)(2,1)S(1)}, bf16[2,4,480,128]{3,2,1,0:T(8,128)(2,1)S(1)}, u32[]{:S(2)}, u32[]{:S(2)}) collective-permute-start(bf16[2,4,480,128]{3,2,1,0:T(8,128)(2,1)S(1)} %collective-permute-done.9.refs_0_.refs_2_), channel_id=1, source_target_pairs={{0,8},{8,16},{16,24},{24,28},{28,20},{20,12},{12,4},{4,0},{2,6},{1... | collective-permute-start | bytes 2949128 | tf_op jit(solution)/shard_map/ppermute | solution.py:484
  46.5 1.9 %collective-permute-done.13.refs_2_.refs_3_ = bf16[2,600,128]{2,1,0:T(8,128)(2,1)S(1)} collective-permute-done((bf16[2,600,128]{2,1,0:T(8,128)(2,1)S(1)}, bf16[2,600,128]{2,1,0:T(8,128)(2,1)S(1)}, u32[]{:S(2)}, u32[]{:S(2)}) %collective-permute-start.13) | collective-permute-done | bytes 307232 | tf_op jit(solution)/shard_map/ppermute | solution.py:510
  48.7 0.8 extra.15
  49.5 1.3 %collective-permute-start.17 = (bf16[2,600,128]{2,1,0:T(8,128)(2,1)S(1)}, bf16[2,600,128]{2,1,0:T(8,128)(2,1)S(1)}, u32[]{:S(2)}, u32[]{:S(2)}) collective-permute-start(bf16[2,600,128]{2,1,0:T(8,128)(2,1)S(1)} %get-tuple-element.58), channel_id=1, source_target_pairs={{0,1},{1,0},{2,3},{3,2},{4,5},{5,4},{6,7},{7,6},{8,9},{9,8},{10,11... | collective-permute-start | bytes 921608 | tf_op jit(solution)/shard_map/ppermute | solution.py:510
  50.8 1.6 %collective-permute-start.6 = (bf16[1,4,480,128]{3,2,1,0:T(8,128)(2,1)S(1)}, bf16[1,4,480,128]{3,2,1,0:T(8,128)(2,1)S(1)}, u32[]{:S(2)}, u32[]{:S(2)}) collective-permute-start(bf16[1,4,480,128]{3,2,1,0:T(8,128)(2,1)S(1)} %slice.12), channel_id=1, source_target_pairs={{0,8},{8,16},{16,24},{24,28},{28,20},{20,12},{12,4},{4,0},{2,6},{1... | collective-permute-start | bytes 1474568 | tf_op jit(solution)/shard_map/ppermute | solution.py:484
  52.5 3.3 %correlate.4 = (bf16[16,2520,256]{2,1,0:T(8,128)(2,1)}, bf16[2,2520,256]{2,1,0:T(8,128)(2,1)S(1)}) custom-call(s32[21]{0:T(128)S(1)} %concatenate.15.meta, bf16[1,4,480,128]{3,2,1,0:T(8,128)(2,1)S(1)} %collective-permute-done.refs_0_, bf16[1,4,480,128]{3,2,1,0:T(8,128)(2,1)S(1)} %collective-permute-done.3.refs_1_, ...), custom_call_target="tpu_custom_call", output_to_operand_aliasing={{0}: (7, {})} | custom-call | flops 10000001024 | bytes 1000 | tf_op jit(solution)/shard_map/correlate/pallas_call | solution.py:391
  55.9 2.1 %collective-permute-done.17.refs_2_.refs_1_ = bf16[2,600,128]{2,1,0:T(8,128)(2,1)S(1)} collective-permute-done((bf16[2,600,128]{2,1,0:T(8,128)(2,1)S(1)}, bf16[2,600,128]{2,1,0:T(8,128)(2,1)S(1)}, u32[]{:S(2)}, u32[]{:S(2)}) %collective-permute-start.17) | collective-permute-done | bytes 307232 | tf_op jit(solution)/shard_map/ppermute | solution.py:510
  58.0 1.5 %collective-permute-done.10.refs_0_.refs_2_ = bf16[2,4,480,128]{3,2,1,0:T(8,128)(2,1)S(1)} collective-permute-done((bf16[2,4,480,128]{3,2,1,0:T(8,128)(2,1)S(1)}, bf16[2,4,480,128]{3,2,1,0:T(8,128)(2,1)S(1)}, u32[]{:S(2)}, u32[]{:S(2)}) %collective-permute-start.10) | collective-permute-done | bytes 983072 | tf_op jit(solution)/shard_map/ppermute | solution.py:484
  59.5 0.8 extra.16
  60.2 1.1 %collective-permute-start.23 = (bf16[2,600,128]{2,1,0:T(8,128)(2,1)S(1)}, bf16[2,600,128]{2,1,0:T(8,128)(2,1)S(1)}, u32[]{:S(2)}, u32[]{:S(2)}) collective-permute-start(bf16[2,600,128]{2,1,0:T(8,128)(2,1)S(1)} %get-tuple-element.62), channel_id=1, source_target_pairs={{0,1},{1,0},{2,3},{3,2},{4,5},{5,4},{6,7},{7,6},{8,9},{9,8},{10,11... | collective-permute-start | bytes 921608 | tf_op jit(solution)/shard_map/ppermute | solution.py:510
  61.4 1.6 %collective-permute-start.19 = (bf16[1,4,480,128]{3,2,1,0:T(8,128)(2,1)S(1)}, bf16[1,4,480,128]{3,2,1,0:T(8,128)(2,1)S(1)}, u32[]{:S(2)}, u32[]{:S(2)}) collective-permute-start(bf16[1,4,480,128]{3,2,1,0:T(8,128)(2,1)S(1)} %get-tuple-element.86), channel_id=1, source_target_pairs={{0,8},{8,16},{16,24},{24,28},{28,20},{20,12},{12,4},{4,0},{2,6},{1... | collective-permute-start | bytes 1474568 | tf_op jit(solution)/shard_map/ppermute | solution.py:484
  63.0 1.7 %collective-permute-done.6.refs_0_ = bf16[1,4,480,128]{3,2,1,0:T(8,128)(2,1)S(1)} collective-permute-done((bf16[1,4,480,128]{3,2,1,0:T(8,128)(2,1)S(1)}, bf16[1,4,480,128]{3,2,1,0:T(8,128)(2,1)S(1)}, u32[]{:S(2)}, u32[]{:S(2)}) %collective-permute-start.6) | collective-permute-done | bytes 491552 | tf_op jit(solution)/shard_map/ppermute | solution.py:484
  64.7 1.4 %collective-permute-start.21 = (bf16[1,4,480,128]{3,2,1,0:T(8,128)(2,1)S(1)}, bf16[1,4,480,128]{3,2,1,0:T(8,128)(2,1)S(1)}, u32[]{:S(2)}, u32[]{:S(2)}) collective-permute-start(bf16[1,4,480,128]{3,2,1,0:T(8,128)(2,1)S(1)} %get-tuple-element.85), channel_id=1, source_target_pairs={{0,8},{8,16},{16,24},{24,28},{28,20},{20,12},{12,4},{4,0},{2,6},{1... | collective-permute-start | bytes 1474568 | tf_op jit(solution)/shard_map/ppermute | solution.py:484
  66.8 2.3 %collective-permute-done.23.refs_3_ = bf16[2,600,128]{2,1,0:T(8,128)(2,1)S(1)} collective-permute-done((bf16[2,600,128]{2,1,0:T(8,128)(2,1)S(1)}, bf16[2,600,128]{2,1,0:T(8,128)(2,1)S(1)}, u32[]{:S(2)}, u32[]{:S(2)}) %collective-permute-start.23) | collective-permute-done | bytes 307232 | tf_op jit(solution)/shard_map/ppermute | solution.py:510
  69.1 0.9 collective-permute-start.25
  70.3 1.6 %collective-permute-start.20 = (bf16[1,4,480,128]{3,2,1,0:T(8,128)(2,1)S(1)}, bf16[1,4,480,128]{3,2,1,0:T(8,128)(2,1)S(1)}, u32[]{:S(2)}, u32[]{:S(2)}) collective-permute-start(bf16[1,4,480,128]{3,2,1,0:T(8,128)(2,1)S(1)} %collective-permute-done.19.refs_0_.refs_1_), channel_id=1, source_target_pairs={{0,8},{8,16},{16,24},{24,28},{28,20},{20,12},{12,4},{4,0},{2,6},{1... | collective-permute-start | bytes 1474568 | tf_op jit(solution)/shard_map/ppermute | solution.py:484
  71.9 3.5 %correlate.5 = (bf16[16,2520,256]{2,1,0:T(8,128)(2,1)}, bf16[2,2520,256]{2,1,0:T(8,128)(2,1)S(1)}) custom-call(s32[21]{0:T(128)S(1)} %concatenate.15.meta, bf16[1,4,480,128]{3,2,1,0:T(8,128)(2,1)S(1)} %collective-permute-done.1.refs_0_, bf16[1,4,480,128]{3,2,1,0:T(8,128)(2,1)S(1)} %collective-permute-done.4.refs_1_, ...), custom_call_target="tpu_custom_call", output_to_operand_aliasing={{0}: (8, {})} | custom-call | flops 3000001024 | bytes 1000 | tf_op jit(solution)/shard_map/correlate/pallas_call | solution.py:391
  75.6 0.8 extra.18
  76.3 1.0 %collective-permute-start.28 = (bf16[2,600,128]{2,1,0:T(8,128)(2,1)S(1)}, bf16[2,600,128]{2,1,0:T(8,128)(2,1)S(1)}, u32[]{:S(2)}, u32[]{:S(2)}) collective-permute-start(bf16[2,600,128]{2,1,0:T(8,128)(2,1)S(1)} %get-tuple-element.71), channel_id=1, source_target_pairs={{0,1},{1,0},{2,3},{3,2},{4,5},{5,4},{6,7},{7,6},{8,9},{9,8},{10,11... | collective-permute-start | bytes 921608 | tf_op jit(solution)/shard_map/ppermute | solution.py:567
  77.4 2.0 %raw_rows.2 = (bf16[16,2520,256]{2,1,0:T(8,128)(2,1)}, bf16[2,2520,256]{2,1,0:T(8,128)(2,1)S(1)}, bf16[2,2520,256]{2,1,0:T(8,128)(2,1)S(1)}) custom-call(s32[21]{0:T(128)S(1)} %concatenate.15.meta, bf16[2,4,480,128]{3,2,1,0:T(8,128)(2,1)S(1)} %collective-permute-done.5.refs_0_, ...), custom_call_target="tpu_custom_call", output_to_operand_aliasing={{0}: (6, {})} | custom-call | flops 1000 | bytes 1000 | tf_op jit(solution)/shard_map/raw_rows/pallas_call | solution.py:417
  79.7 1.1 %collective-permute-done.20.refs_0_ = bf16[1,4,480,128]{3,2,1,0:T(8,128)(2,1)S(1)} collective-permute-done((bf16[1,4,480,128]{3,2,1,0:T(8,128)(2,1)S(1)}, bf16[1,4,480,128]{3,2,1,0:T(8,128)(2,1)S(1)}, u32[]{:S(2)}, u32[]{:S(2)}) %collective-permute-start.20) | collective-permute-done | bytes 491552 | tf_op jit(solution)/shard_map/ppermute | solution.py:484
  81.6 1.0 %collective-permute-start.30 = (bf16[1,600,128]{2,1,0:T(8,128)(2,1)S(1)}, bf16[1,600,128]{2,1,0:T(8,128)(2,1)S(1)}, u32[]{:S(2)}, u32[]{:S(2)}) collective-permute-start(bf16[1,600,128]{2,1,0:T(8,128)(2,1)S(1)} %get-tuple-element.78), channel_id=1, source_target_pairs={{0,1},{1,0},{2,3},{3,2},{4,5},{5,4},{6,7},{7,6},{8,9},{9,8},{10,11... | collective-permute-start | bytes 460808 | tf_op jit(solution)/shard_map/ppermute | solution.py:548
  82.6 3.9 %collective-permute-done.28.refs_0_ = bf16[2,600,128]{2,1,0:T(8,128)(2,1)S(1)} collective-permute-done((bf16[2,600,128]{2,1,0:T(8,128)(2,1)S(1)}, bf16[2,600,128]{2,1,0:T(8,128)(2,1)S(1)}, u32[]{:S(2)}, u32[]{:S(2)}) %collective-permute-start.28) | collective-permute-done | bytes 307232 | tf_op jit(solution)/shard_map/ppermute | solution.py:567
  86.5 1.3 %came_rows.2 = (bf16[16,2520,256]{2,1,0:T(8,128)(2,1)}, bf16[2,2520,256]{2,1,0:T(8,128)(2,1)S(1)}, bf16[2,600,256]{2,1,0:T(8,128)(2,1)S(1)}) custom-call(s32[21]{0:T(128)S(1)} %concatenate.15.meta, bf16[2,600,128]{2,1,0:T(8,128)(2,1)S(1)} %collective-permute-done.28.refs_0_, ...), custom_call_target="tpu_custom_call", output_to_operand_aliasing={{0}: (4, {}), {1}: (5, {})} | custom-call | flops 22000001024 | bytes 1000 | tf_op jit(solution)/shard_map/came_rows/pallas_call | solution.py:439
  87.9 3.8 %raw_rows.3 = (bf16[16,2520,256]{2,1,0:T(8,128)(2,1)}, bf16[2,2520,256]{2,1,0:T(8,128)(2,1)S(1)}) custom-call(s32[21]{0:T(128)S(1)} %concatenate.15.meta, bf16[1,4,480,128]{3,2,1,0:T(8,128)(2,1)S(1)} %get-tuple-element.60.refs_0_, bf16[1,4,480,128]{3,2,1,0:T(8,128)(2,1)S(1)} %collective-permute-done.18.refs_5_.refs_1_, ...), custom_call_target="tpu_custom_call", output_to_operand_aliasing={{0}: (9, {})} | custom-call | flops 10000001024 | bytes 1000 | tf_op jit(solution)/shard_map/raw_rows/pallas_call | solution.py:417
  92.3 0.9 collective-permute-done.31.refs_1_
  93.6 2.2 %came_rows.3 = (bf16[16,2520,256]{2,1,0:T(8,128)(2,1)}, bf16[2,2520,256]{2,1,0:T(8,128)(2,1)S(1)}, bf16[2,2520,256]{2,1,0:T(8,128)(2,1)S(1)}) custom-call(s32[21]{0:T(128)S(1)} %concatenate.15.meta, bf16[1,600,128]{2,1,0:T(8,128)(2,1)S(1)} %get-tuple-element.79.refs_0_, ...), custom_call_target="tpu_custom_call", output_to_operand_aliasing={{0}: (7, {}), {1}: (8, {}), {2}: (9, {})} | custom-call | flops 1000 | bytes 1000 | tf_op jit(solution)/shard_map/came_rows/pallas_call | solution.py:439
  (49 shorter events, 6.9 us)
Async XLA Ops:
  1.2 7.0 %collective-permute-start.2 = (bf16[1,4,480,128]{3,2,1,0:T(8,128)(2,1)S(1)}, bf16[1,4,480,128]{3,2,1,0:T(8,128)(2,1)S(1)}, u32[]{:S(2)}, u32[]{:S(2)}) collective-permute-start(bf16[1,4,480,128]{3,2,1,0:T(8,128)(2,1)S(1)} %get-tuple-element.88.refs_0_), channel_id=1, source_target_pairs={{0,2},{2,0},{4,6},{6,4},{8,10},{10,8},{12,14},{14,12},{16,18},{18,... | collective-permute-start | bytes 1474568 | tf_op jit(solution)/shard_map/ppermute | solution.py:484
  1.8 9.4 %collective-permute-start = (bf16[1,4,480,128]{3,2,1,0:T(8,128)(2,1)S(1)}, bf16[1,4,480,128]{3,2,1,0:T(8,128)(2,1)S(1)}, u32[]{:S(2)}, u32[]{:S(2)}) collective-permute-start(bf16[1,4,480,128]{3,2,1,0:T(8,128)(2,1)S(1)} %get-tuple-element.88.refs_0_), channel_id=1, source_target_pairs={{0,8},{8,16},{16,24},{24,28},{28,20},{20,12},{12,4},{4,0},{2,6},{1... | collective-permute-start | bytes 1474568 | tf_op jit(solution)/shard_map/ppermute | solution.py:484
  4.4 13.9 %collective-permute-start.7 = (bf16[1,4,480,128]{3,2,1,0:T(8,128)(2,1)S(1)}, bf16[1,4,480,128]{3,2,1,0:T(8,128)(2,1)S(1)}, u32[]{:S(2)}, u32[]{:S(2)}) collective-permute-start(bf16[1,4,480,128]{3,2,1,0:T(8,128)(2,1)S(1)} %get-tuple-element.87.refs_0_), channel_id=1, source_target_pairs={{0,1},{1,0},{2,3},{3,2},{4,5},{5,4},{6,7},{7,6},{8,9},{9,8},{10,11... | collective-permute-start | bytes 1474568 | tf_op jit(solution)/shard_map/ppermute | solution.py:475
  6.8 14.2 %collective-permute-start.14 = (bf16[256,128]{0,1:T(8,128)(2,1)S(1)}, bf16[256,128]{0,1:T(8,128)(2,1)S(1)}, u32[]{:S(2)}, u32[]{:S(2)}) collective-permute-start(bf16[256,128]{0,1:T(8,128)(2,1)S(1)} %copy.27), channel_id=1, source_target_pairs={{0,1},{1,0},{2,3},{3,2},{4,5},{5,4},{6,7},{7,6},{8,9},{9,8},{10,11... | collective-permute-start | bytes 196616 | tf_op jit(solution)/shard_map/ppermute | solution.py:476
  8.2 10.1 %collective-permute-start.3 = (bf16[1,4,480,128]{3,2,1,0:T(8,128)(2,1)S(1)}, bf16[1,4,480,128]{3,2,1,0:T(8,128)(2,1)S(1)}, u32[]{:S(2)}, u32[]{:S(2)}) collective-permute-start(bf16[1,4,480,128]{3,2,1,0:T(8,128)(2,1)S(1)} %collective-permute-done.2), channel_id=1, source_target_pairs={{0,8},{8,16},{16,24},{24,28},{28,20},{20,12},{12,4},{4,0},{2,6},{1... | collective-permute-start | bytes 1474568 | tf_op jit(solution)/shard_map/ppermute | solution.py:484
  11.2 11.7 %collective-permute-start.1 = (bf16[1,4,480,128]{3,2,1,0:T(8,128)(2,1)S(1)}, bf16[1,4,480,128]{3,2,1,0:T(8,128)(2,1)S(1)}, u32[]{:S(2)}, u32[]{:S(2)}) collective-permute-start(bf16[1,4,480,128]{3,2,1,0:T(8,128)(2,1)S(1)} %collective-permute-done.refs_0_), channel_id=1, source_target_pairs={{0,8},{8,16},{16,24},{24,28},{28,20},{20,12},{12,4},{4,0},{2,6},{1... | collective-permute-start | bytes 1474568 | tf_op jit(solution)/shard_map/ppermute | solution.py:484
  18.3 2.8 %collective-permute-start.8 = (bf16[1,4,480,128]{3,2,1,0:T(8,128)(2,1)S(1)}, bf16[1,4,480,128]{3,2,1,0:T(8,128)(2,1)S(1)}, u32[]{:S(2)}, u32[]{:S(2)}) collective-permute-start(bf16[1,4,480,128]{3,2,1,0:T(8,128)(2,1)S(1)} %collective-permute-done.7.refs_1_), channel_id=1, source_target_pairs={{0,2},{2,0},{4,6},{6,4},{8,10},{10,8},{12,14},{14,12},{16,18},{18,... | collective-permute-start | bytes 1474568 | tf_op jit(solution)/shard_map/ppermute | solution.py:484
  18.3 10.7 %collective-permute-start.4 = (bf16[1,4,480,128]{3,2,1,0:T(8,128)(2,1)S(1)}, bf16[1,4,480,128]{3,2,1,0:T(8,128)(2,1)S(1)}, u32[]{:S(2)}, u32[]{:S(2)}) collective-permute-start(bf16[1,4,480,128]{3,2,1,0:T(8,128)(2,1)S(1)} %collective-permute-done.3.refs_1_), channel_id=1, source_target_pairs={{0,8},{8,16},{16,24},{24,28},{28,20},{20,12},{12,4},{4,0},{2,6},{1... | collective-permute-start | bytes 1474568 | tf_op jit(solution)/shard_map/ppermute | solution.py:484
  19.5 9.6 %collective-permute-start.11 = (bf16[2,600,128]{2,1,0:T(8,128)(2,1)S(1)}, bf16[2,600,128]{2,1,0:T(8,128)(2,1)S(1)}, u32[]{:S(2)}, u32[]{:S(2)}) collective-permute-start(bf16[2,600,128]{2,1,0:T(8,128)(2,1)S(1)} %get-tuple-element.48), channel_id=1, source_target_pairs={{0,1},{1,0},{2,3},{3,2},{4,5},{5,4},{6,7},{7,6},{8,9},{9,8},{10,11... | collective-permute-start | bytes 921608 | tf_op jit(solution)/shard_map/ppermute | solution.py:510
  21.0 10.9 %collective-permute-start.15 = (bf16[256,256]{1,0:T(8,128)(2,1)S(1)}, bf16[256,256]{1,0:T(8,128)(2,1)S(1)}, u32[]{:S(2)}, u32[]{:S(2)}) collective-permute-start(bf16[256,256]{1,0:T(8,128)(2,1)S(1)} %pad_maximum_fusion.3.refs_4_), channel_id=1, source_target_pairs={{0,2},{2,0},{4,6},{6,4},{8,10},{10,8},{12,14},{14,12},{16,18},{18,... | collective-permute-start | bytes 393224 | tf_op jit(solution)/shard_map/ppermute | solution.py:479
  21.2 18.9 %collective-permute-start.9 = (bf16[2,4,480,128]{3,2,1,0:T(8,128)(2,1)S(1)}, bf16[2,4,480,128]{3,2,1,0:T(8,128)(2,1)S(1)}, u32[]{:S(2)}, u32[]{:S(2)}) collective-permute-start(bf16[2,4,480,128]{3,2,1,0:T(8,128)(2,1)S(1)} %pad_maximum_fusion.1), channel_id=1, source_target_pairs={{0,8},{8,16},{16,24},{24,28},{28,20},{20,12},{12,4},{4,0},{2,6},{1... | collective-permute-start | bytes 2949128 | tf_op jit(solution)/shard_map/ppermute | solution.py:484
  29.8 10.3 %collective-permute-start.12 = (bf16[2,600,128]{2,1,0:T(8,128)(2,1)S(1)}, bf16[2,600,128]{2,1,0:T(8,128)(2,1)S(1)}, u32[]{:S(2)}, u32[]{:S(2)}) collective-permute-start(bf16[2,600,128]{2,1,0:T(8,128)(2,1)S(1)} %get-tuple-element.50), channel_id=1, source_target_pairs={{0,1},{1,0},{2,3},{3,2},{4,5},{5,4},{6,7},{7,6},{8,9},{9,8},{10,11... | collective-permute-start | bytes 921608 | tf_op jit(solution)/shard_map/ppermute | solution.py:510
  31.1 11.7 %collective-permute-start.16 = (bf16[1,600,128]{2,1,0:T(8,128)(2,1)S(1)}, bf16[1,600,128]{2,1,0:T(8,128)(2,1)S(1)}, u32[]{:S(2)}, u32[]{:S(2)}) collective-permute-start(bf16[1,600,128]{2,1,0:T(8,128)(2,1)S(1)} %get-tuple-element.53), channel_id=1, source_target_pairs={{0,1},{1,0},{2,3},{3,2},{4,5},{5,4},{6,7},{7,6},{8,9},{9,8},{10,11... | collective-permute-start | bytes 460808 | tf_op jit(solution)/shard_map/ppermute | solution.py:510
  32.0 16.7 %collective-permute-start.5 = (bf16[2,4,480,128]{3,2,1,0:T(8,128)(2,1)S(1)}, bf16[2,4,480,128]{3,2,1,0:T(8,128)(2,1)S(1)}, u32[]{:S(2)}, u32[]{:S(2)}) collective-permute-start(bf16[2,4,480,128]{3,2,1,0:T(8,128)(2,1)S(1)} %pad_maximum_fusion), channel_id=1, source_target_pairs={{0,8},{8,16},{16,24},{24,28},{28,20},{20,12},{12,4},{4,0},{2,6},{1... | collective-permute-start | bytes 2949128 | tf_op jit(solution)/shard_map/ppermute | solution.py:484
  40.9 7.6 %collective-permute-start.13 = (bf16[2,600,128]{2,1,0:T(8,128)(2,1)S(1)}, bf16[2,600,128]{2,1,0:T(8,128)(2,1)S(1)}, u32[]{:S(2)}, u32[]{:S(2)}) collective-permute-start(bf16[2,600,128]{2,1,0:T(8,128)(2,1)S(1)} %get-tuple-element.51), channel_id=1, source_target_pairs={{0,1},{1,0},{2,3},{3,2},{4,5},{5,4},{6,7},{7,6},{8,9},{9,8},{10,11... | collective-permute-start | bytes 921608 | tf_op jit(solution)/shard_map/ppermute | solution.py:510
  45.2 24.7 %collective-permute-start.24 = (bf16[1,2520,256]{2,1,0:T(8,128)(2,1)S(1)}, bf16[1,2520,256]{2,1,0:T(8,128)(2,1)S(1)}, u32[]{:S(2)}, u32[]{:S(2)}) collective-permute-start(bf16[1,2520,256]{2,1,0:T(8,128)(2,1)S(1)} %get-tuple-element.63), channel_id=1, source_target_pairs={{0,2},{2,0},{4,6},{6,4},{8,10},{10,8},{12,14},{14,12},{16,18},{18,... | collective-permute-start | bytes 3870728 | tf_op jit(solution)/shard_map/ppermute | solution.py:484
  45.3 14.1 %collective-permute-start.10 = (bf16[2,4,480,128]{3,2,1,0:T(8,128)(2,1)S(1)}, bf16[2,4,480,128]{3,2,1,0:T(8,128)(2,1)S(1)}, u32[]{:S(2)}, u32[]{:S(2)}) collective-permute-start(bf16[2,4,480,128]{3,2,1,0:T(8,128)(2,1)S(1)} %collective-permute-done.9.refs_0_.refs_2_), channel_id=1, source_target_pairs={{0,8},{8,16},{16,24},{24,28},{28,20},{20,12},{12,4},{4,0},{2,6},{1... | collective-permute-start | bytes 2949128 | tf_op jit(solution)/shard_map/ppermute | solution.py:484
  49.5 8.5 %collective-permute-start.17 = (bf16[2,600,128]{2,1,0:T(8,128)(2,1)S(1)}, bf16[2,600,128]{2,1,0:T(8,128)(2,1)S(1)}, u32[]{:S(2)}, u32[]{:S(2)}) collective-permute-start(bf16[2,600,128]{2,1,0:T(8,128)(2,1)S(1)} %get-tuple-element.58), channel_id=1, source_target_pairs={{0,1},{1,0},{2,3},{3,2},{4,5},{5,4},{6,7},{7,6},{8,9},{9,8},{10,11... | collective-permute-start | bytes 921608 | tf_op jit(solution)/shard_map/ppermute | solution.py:510
  50.8 13.9 %collective-permute-start.6 = (bf16[1,4,480,128]{3,2,1,0:T(8,128)(2,1)S(1)}, bf16[1,4,480,128]{3,2,1,0:T(8,128)(2,1)S(1)}, u32[]{:S(2)}, u32[]{:S(2)}) collective-permute-start(bf16[1,4,480,128]{3,2,1,0:T(8,128)(2,1)S(1)} %slice.12), channel_id=1, source_target_pairs={{0,8},{8,16},{16,24},{24,28},{28,20},{20,12},{12,4},{4,0},{2,6},{1... | collective-permute-start | bytes 1474568 | tf_op jit(solution)/shard_map/ppermute | solution.py:484
  55.8 21.6 %collective-permute-start.22 = (bf16[2,2520,256]{2,1,0:T(8,128)(2,1)S(1)}, bf16[2,2520,256]{2,1,0:T(8,128)(2,1)S(1)}, u32[]{:S(2)}, u32[]{:S(2)}) collective-permute-start(bf16[2,2520,256]{2,1,0:T(8,128)(2,1)S(1)} %get-tuple-element.61), channel_id=1, source_target_pairs={{0,2},{2,0},{4,6},{6,4},{8,10},{10,8},{12,14},{14,12},{16,18},{18,... | collective-permute-start | bytes 7741448 | tf_op jit(solution)/shard_map/ppermute | solution.py:484
  60.2 8.8 %collective-permute-start.23 = (bf16[2,600,128]{2,1,0:T(8,128)(2,1)S(1)}, bf16[2,600,128]{2,1,0:T(8,128)(2,1)S(1)}, u32[]{:S(2)}, u32[]{:S(2)}) collective-permute-start(bf16[2,600,128]{2,1,0:T(8,128)(2,1)S(1)} %get-tuple-element.62), channel_id=1, source_target_pairs={{0,1},{1,0},{2,3},{3,2},{4,5},{5,4},{6,7},{7,6},{8,9},{9,8},{10,11... | collective-permute-start | bytes 921608 | tf_op jit(solution)/shard_map/ppermute | solution.py:510
  61.4 8.9 %collective-permute-start.19 = (bf16[1,4,480,128]{3,2,1,0:T(8,128)(2,1)S(1)}, bf16[1,4,480,128]{3,2,1,0:T(8,128)(2,1)S(1)}, u32[]{:S(2)}, u32[]{:S(2)}) collective-permute-start(bf16[1,4,480,128]{3,2,1,0:T(8,128)(2,1)S(1)} %get-tuple-element.86), channel_id=1, source_target_pairs={{0,8},{8,16},{16,24},{24,28},{28,20},{20,12},{12,4},{4,0},{2,6},{1... | collective-permute-start | bytes 1474568 | tf_op jit(solution)/shard_map/ppermute | solution.py:484
  64.7 10.8 %collective-permute-start.21 = (bf16[1,4,480,128]{3,2,1,0:T(8,128)(2,1)S(1)}, bf16[1,4,480,128]{3,2,1,0:T(8,128)(2,1)S(1)}, u32[]{:S(2)}, u32[]{:S(2)}) collective-permute-start(bf16[1,4,480,128]{3,2,1,0:T(8,128)(2,1)S(1)} %get-tuple-element.85), channel_id=1, source_target_pairs={{0,8},{8,16},{16,24},{24,28},{28,20},{20,12},{12,4},{4,0},{2,6},{1... | collective-permute-start | bytes 1474568 | tf_op jit(solution)/shard_map/ppermute | solution.py:484
  69.1 6.3 %collective-permute-start.25 = (bf16[1,600,128]{2,1,0:T(8,128)(2,1)S(1)}, bf16[1,600,128]{2,1,0:T(8,128)(2,1)S(1)}, u32[]{:S(2)}, u32[]{:S(2)}) collective-permute-start(bf16[1,600,128]{2,1,0:T(8,128)(2,1)S(1)} %get-tuple-element.66), channel_id=1, source_target_pairs={{0,1},{1,0},{2,3},{3,2},{4,5},{5,4},{6,7},{7,6},{8,9},{9,8},{10,11... | collective-permute-start | bytes 460808 | tf_op jit(solution)/shard_map/ppermute | solution.py:548
  70.0 11.6 %collective-permute-start.18 = (bf16[1,4,480,128]{3,2,1,0:T(8,128)(2,1)S(1)}, bf16[1,4,480,128]{3,2,1,0:T(8,128)(2,1)S(1)}, u32[]{:S(2)}, u32[]{:S(2)}) collective-permute-start(bf16[1,4,480,128]{3,2,1,0:T(8,128)(2,1)S(1)} %get-tuple-element.60.refs_0_), channel_id=1, source_target_pairs={{0,2},{2,0},{4,6},{6,4},{8,10},{10,8},{12,14},{14,12},{16,18},{18,... | collective-permute-start | bytes 1474568 | tf_op jit(solution)/shard_map/ppermute | solution.py:484
  70.3 10.5 %collective-permute-start.20 = (bf16[1,4,480,128]{3,2,1,0:T(8,128)(2,1)S(1)}, bf16[1,4,480,128]{3,2,1,0:T(8,128)(2,1)S(1)}, u32[]{:S(2)}, u32[]{:S(2)}) collective-permute-start(bf16[1,4,480,128]{3,2,1,0:T(8,128)(2,1)S(1)} %collective-permute-done.19.refs_0_.refs_1_), channel_id=1, source_target_pairs={{0,8},{8,16},{16,24},{24,28},{28,20},{20,12},{12,4},{4,0},{2,6},{1... | collective-permute-start | bytes 1474568 | tf_op jit(solution)/shard_map/ppermute | solution.py:484
  75.4 12.5 %collective-permute-start.27 = (bf16[2,2520,256]{2,1,0:T(8,128)(2,1)S(1)}, bf16[2,2520,256]{2,1,0:T(8,128)(2,1)S(1)}, u32[]{:S(2)}, u32[]{:S(2)}) collective-permute-start(bf16[2,2520,256]{2,1,0:T(8,128)(2,1)S(1)} %get-tuple-element.70), channel_id=1, source_target_pairs={{0,2},{2,0},{4,6},{6,4},{8,10},{10,8},{12,14},{14,12},{16,18},{18,... | collective-permute-start | bytes 7741448 | tf_op jit(solution)/shard_map/ppermute | solution.py:484
  76.3 10.1 %collective-permute-start.28 = (bf16[2,600,128]{2,1,0:T(8,128)(2,1)S(1)}, bf16[2,600,128]{2,1,0:T(8,128)(2,1)S(1)}, u32[]{:S(2)}, u32[]{:S(2)}) collective-permute-start(bf16[2,600,128]{2,1,0:T(8,128)(2,1)S(1)} %get-tuple-element.71), channel_id=1, source_target_pairs={{0,1},{1,0},{2,3},{3,2},{4,5},{5,4},{6,7},{7,6},{8,9},{9,8},{10,11... | collective-permute-start | bytes 921608 | tf_op jit(solution)/shard_map/ppermute | solution.py:567
  79.4 8.4 %collective-permute-start.29 = (bf16[2,2520,256]{2,1,0:T(8,128)(2,1)S(1)}, bf16[2,2520,256]{2,1,0:T(8,128)(2,1)S(1)}, u32[]{:S(2)}, u32[]{:S(2)}) collective-permute-start(bf16[2,2520,256]{2,1,0:T(8,128)(2,1)S(1)} %get-tuple-element.75), channel_id=1, source_target_pairs={{0,2},{2,0},{4,6},{6,4},{8,10},{10,8},{12,14},{14,12},{16,18},{18,... | collective-permute-start | bytes 7741448 | tf_op jit(solution)/shard_map/ppermute | solution.py:484
  81.5 6.4 %collective-permute-start.26 = (bf16[1,4,480,128]{3,2,1,0:T(8,128)(2,1)S(1)}, bf16[1,4,480,128]{3,2,1,0:T(8,128)(2,1)S(1)}, u32[]{:S(2)}, u32[]{:S(2)}) collective-permute-start(bf16[1,4,480,128]{3,2,1,0:T(8,128)(2,1)S(1)} %get-tuple-element.69.refs_2_), channel_id=1, source_target_pairs={{0,2},{2,0},{4,6},{6,4},{8,10},{10,8},{12,14},{14,12},{16,18},{18,... | collective-permute-start | bytes 1474568 | tf_op jit(solution)/shard_map/ppermute | solution.py:484
  81.6 10.1 %collective-permute-start.30 = (bf16[1,600,128]{2,1,0:T(8,128)(2,1)S(1)}, bf16[1,600,128]{2,1,0:T(8,128)(2,1)S(1)}, u32[]{:S(2)}, u32[]{:S(2)}) collective-permute-start(bf16[1,600,128]{2,1,0:T(8,128)(2,1)S(1)} %get-tuple-element.78), channel_id=1, source_target_pairs={{0,1},{1,0},{2,3},{3,2},{4,5},{5,4},{6,7},{7,6},{8,9},{9,8},{10,11... | collective-permute-start | bytes 460808 | tf_op jit(solution)/shard_map/ppermute | solution.py:548
  87.8 4.5 %collective-permute-start.33 = (bf16[2,600,256]{2,1,0:T(8,128)(2,1)S(1)}, bf16[2,600,256]{2,1,0:T(8,128)(2,1)S(1)}, u32[]{:S(2)}, u32[]{:S(2)}) collective-permute-start(bf16[2,600,256]{2,1,0:T(8,128)(2,1)S(1)} %get-tuple-element.81), channel_id=1, source_target_pairs={{0,2},{2,0},{4,6},{6,4},{8,10},{10,8},{12,14},{14,12},{16,18},{18,... | collective-permute-start | bytes 1843208 | tf_op jit(solution)/shard_map/ppermute | solution.py:484
  91.7 1.6 %collective-permute-start.31 = (bf16[1,600,128]{2,1,0:T(8,128)(2,1)S(1)}, bf16[1,600,128]{2,1,0:T(8,128)(2,1)S(1)}, u32[]{:S(2)}, u32[]{:S(2)}) collective-permute-start(bf16[1,600,128]{2,1,0:T(8,128)(2,1)S(1)} %get-tuple-element.79.refs_0_), channel_id=1, source_target_pairs={{0,2},{2,0},{4,6},{6,4},{8,10},{10,8},{12,14},{14,12},{16,18},{18,... | collective-permute-start | bytes 460808 | tf_op jit(solution)/shard_map/ppermute | solution.py:484
  92.2 1.4 %collective-permute-start.32 = (bf16[1,600,128]{2,1,0:T(8,128)(2,1)S(1)}, bf16[1,600,128]{2,1,0:T(8,128)(2,1)S(1)}, u32[]{:S(2)}, u32[]{:S(2)}) collective-permute-start(bf16[1,600,128]{2,1,0:T(8,128)(2,1)S(1)} %get-tuple-element.80.refs_2_), channel_id=1, source_target_pairs={{0,2},{2,0},{4,6},{6,4},{8,10},{10,8},{12,14},{14,12},{16,18},{18,... | collective-permute-start | bytes 460808 | tf_op jit(solution)/shard_map/ppermute | solution.py:484

commit v3 on v2

--- a/solution.py
+++ b/solution.py
@@ -8,7 +8,7 @@
 from jax.sharding import PartitionSpec as P
 
 LANES = 128
-PARAMS = {'LAG': 2, 'F0': 10, 'F1': 0, 'PS0': 2, 'JA': 3, 'JB': 1, 'C0POS': 2, 'GATE': 30, 'F3': 0, 'F2': 22, 'NL': 1, 'PE4': 0, 'P4': 0, 'P3': 1, 'CPOS': 1, 'LC': 0, 'BSPL': 1, 'ONEX': 1, 'X00': 10, 'X01': 10, 'C0': 10, 'X10': 10, 'X11': 10, 'C1': 10, 'X20': 10, 'X21': 10, 'C2': 3, 'X30': 10, 'X31': 3, 'C3': 10, 'X40': 10, 'X41': 10, 'C4': 10}
+PARAMS = {'LAG': 2, 'F0': 10, 'F1': 0, 'PS0': 2, 'JA': 3, 'JB': 1, 'C0POS': 2, 'GATE': 30, 'F3': 0, 'F2': 22, 'NL': 1, 'PE4': 0, 'P4': 0, 'P3': 1, 'CPOS': 1, 'LC': 0, 'BSPL': 1, 'ONEX': 1, 'EL': 1, 'WH': 0, 'X00': 10, 'X01': 10, 'C0': 10, 'X10': 10, 'X11': 10, 'C1': 10, 'X20': 10, 'X21': 10, 'C2': 3, 'X30': 10, 'X31': 3, 'C3': 10, 'X40': 10, 'X41': 10, 'C4': 10}
 
 
 def G(name):
@@ -201,15 +201,15 @@
     total, cut = done.shape[1], first_open_row(done.shape[1], rows_n * cols_n)
     slots = list(slots)
 
-    def leave(strip, whole):
-        rows = pl.ds(0, total if whole else cut)
+    def leave(strip, part):
+        rows = {"all": pl.ds(0, total), "settled": pl.ds(0, cut), "rest": pl.ds(cut, total - cut)}[part]
         number = len(copies) - len(landing)
         copies.append(pltpu.make_async_copy(strip.at[rows], out.at[meta[slots.pop(0)], rows], sems.at[number]))
         copies[-1].start()
 
-    for strips, whole in zip(leavers, leaving):
-        for index in range(strips.shape[0] if whole is not None else 0):
-            leave(strips.at[index], whole)
+    for strips, part in zip(leavers, leaving):
+        for index in range(strips.shape[0] if part else 0):
+            leave(strips.at[index], part)
 
     def times(left):
         return jnp.dot(left, queries[...], preferred_element_type=jnp.float32) * factor
@@ -248,7 +248,7 @@
                 store(index, at * step, joined(run))
 
         if slots:
-            leave(done.at[index], False)
+            leave(done.at[index], "settled")
     for copy in copies:
         copy.wait()
 
@@ -467,6 +467,8 @@
 
     mine = lax.dynamic_slice_in_dim(frame_two, side * half_rows, half_rows, axis=0)[None]
     theirs = lax.dynamic_slice_in_dim(frame_two, (1 - side) * half_rows, half_rows, axis=0)[None]
+    if G("WH"):
+        theirs = jnp.where(side == 0, frame_two[half_rows:], frame_two[:half_rows])[None]
     if G("XQ"):
         sent = jnp.concatenate([theirs.reshape(raw, chans), frame_one], axis=0)
         got = lax.ppermute(sent, "chan", across)
@@ -538,7 +540,7 @@
         return permute_rows(swap, [piece])[0]
 
     def near_raw(out):
-        return raw_rows(out, *came[near], True, *landing(near), G("F3"), pins=tuple(across_came[far, 1]) if G("PR") else ())
+        return raw_rows(out, *came[near], True, *landing(near), G("F3"), slots=slots_of(near, 0) if G("EL") else (), pins=tuple(across_came[far, 1]) if G("PR") else ())
 
     swapped = []
 
@@ -586,7 +588,7 @@
         *landing(far),
         G("F0"),
         (near_done, near_late),
-        (True, False if G("NL") else None),
+        ("rest" if G("EL") else "all", "settled" if G("NL") else None),
         slots_of(near, 0) + (slots if G("NL") else slots[len(slots_of(near, 1)) :]),
     )
     out, own, other = gate(out, [across_came[far, 0][0], across_came[far, 1][0]], G("GATE"))

time: 96.2 us -> 95.7 us (level)
  waiting for transfers between devices: 35.8 us -> 34.8 us
where the time goes in v3:
time: 95.7 us; the launch traced here: 95.6 us
  waiting for transfers between devices  34.8 us (36%)
  starting transfers between devices  31.5 us (33%)
  Pallas kernels  26.1 us (27%)
  local copies, waits for them, and re-layouts  2.36 us (2%)
    ppermute x6, waiting for transfers between devices, do_extra(): across_came[d, 1 - part].append(lax.ppermute(extra, 'chan', across))  19.7 us
    ppermute x22, starting transfers between devices, permute_rows(): return [lax.ppermute(piece, 'rows', pairs) for piece in pieces]  19.1 us
    pallas_call x3, Pallas kernels, correlate(): pl.pallas_call(functools.partial(corr_kernel, factor, tuple((len(part) fo...  9.3 us
    pallas_call x10, Pallas kernels, make_extra(): pl.pallas_call(functools.partial(extra_kernel, len(halves), 2 + len(carri...  7.2 us
    ppermute x6, starting transfers between devices, do_extra(): across_came[d, 1 - part].append(lax.ppermute(extra, 'chan', across))  7.09 us
    ppermute x22, waiting for transfers between devices, permute_rows(): return [lax.ppermute(piece, 'rows', pairs) for piece in pieces]  6.27 us
    pallas_call x2, Pallas kernels, raw_rows(): pl.pallas_call(functools.partial(raw_kernel, factor, (len(own), len(other...  6.13 us
    ppermute x1, waiting for transfers between devices, ring_local(): partner = lax.ppermute(theirs, 'chan', across)  5.11 us
  transfers between devices with their start and end apart: 34, of which 17 were waited for; matrix products, arithmetic and copies ran while one was open for 1% of the time, Pallas kernels for 25%

profile of v3, /device:TPU:0, one launch (start us, length us, event | category | flops | bytes accessed | tf_op | source)
XLA Modules:
  0.0 95.6 jit_solution(8865827962617748131)
XLA Ops:
  0.0 1.2 %dynamic-slice_bitcast_fusion = (bf16[1,4,480,128]{3,2,1,0:T(8,128)(2,1)S(1)}, bf16[1,4,480,128]{3,2,1,0:T(8,128)(2,1)S(1)}) fusion(bf16[8,480,128]{2,1,0:T(8,128)(2,1)} %param.3, s32[]{:T(128)S(6)} %select_n.72, s32[]{:T(128)S(6)} %select_n.71), kind=kLoop, calls=%fused_computation.2 | loop fusion | bytes 1966088 | tf_op jit(solution)/shard_map/broadcast_in_dim | solution.py:469
  1.8 2.6 %collective-permute-start = (bf16[1,4,480,128]{3,2,1,0:T(8,128)(2,1)S(1)}, bf16[1,4,480,128]{3,2,1,0:T(8,128)(2,1)S(1)}, u32[]{:S(2)}, u32[]{:S(2)}) collective-permute-start(bf16[1,4,480,128]{3,2,1,0:T(8,128)(2,1)S(1)} %get-tuple-element.88.refs_0_), channel_id=1, source_target_pairs={{0,8},{8,16},{16,24},{24,28},{28,20},{20,12},{12,4},{4,0},{2,6},{1... | collective-permute-start | bytes 1474568 | tf_op jit(solution)/shard_map/ppermute | solution.py:486
  4.4 1.5 %collective-permute-start.7 = (bf16[1,4,480,128]{3,2,1,0:T(8,128)(2,1)S(1)}, bf16[1,4,480,128]{3,2,1,0:T(8,128)(2,1)S(1)}, u32[]{:S(2)}, u32[]{:S(2)}) collective-permute-start(bf16[1,4,480,128]{3,2,1,0:T(8,128)(2,1)S(1)} %get-tuple-element.87.refs_0_), channel_id=1, source_target_pairs={{0,1},{1,0},{2,3},{3,2},{4,5},{5,4},{6,7},{7,6},{8,9},{9,8},{10,11... | collective-permute-start | bytes 1474568 | tf_op jit(solution)/shard_map/ppermute | solution.py:477
  5.9 0.9 copy.27
  8.2 1.6 %collective-permute-start.3 = (bf16[1,4,480,128]{3,2,1,0:T(8,128)(2,1)S(1)}, bf16[1,4,480,128]{3,2,1,0:T(8,128)(2,1)S(1)}, u32[]{:S(2)}, u32[]{:S(2)}) collective-permute-start(bf16[1,4,480,128]{3,2,1,0:T(8,128)(2,1)S(1)} %collective-permute-done.2), channel_id=1, source_target_pairs={{0,8},{8,16},{16,24},{24,28},{28,20},{20,12},{12,4},{4,0},{2,6},{1... | collective-permute-start | bytes 1474568 | tf_op jit(solution)/shard_map/ppermute | solution.py:486
  10.5 0.7 collective-permute-done.refs_0_
  11.2 2.1 %collective-permute-start.1 = (bf16[1,4,480,128]{3,2,1,0:T(8,128)(2,1)S(1)}, bf16[1,4,480,128]{3,2,1,0:T(8,128)(2,1)S(1)}, u32[]{:S(2)}, u32[]{:S(2)}) collective-permute-start(bf16[1,4,480,128]{3,2,1,0:T(8,128)(2,1)S(1)} %collective-permute-done.refs_0_), channel_id=1, source_target_pairs={{0,8},{8,16},{16,24},{24,28},{28,20},{20,12},{12,4},{4,0},{2,6},{1... | collective-permute-start | bytes 1474568 | tf_op jit(solution)/shard_map/ppermute | solution.py:486
  13.2 5.1 %collective-permute-done.7.refs_1_ = bf16[1,4,480,128]{3,2,1,0:T(8,128)(2,1)S(1)} collective-permute-done((bf16[1,4,480,128]{3,2,1,0:T(8,128)(2,1)S(1)}, bf16[1,4,480,128]{3,2,1,0:T(8,128)(2,1)S(1)}, u32[]{:S(2)}, u32[]{:S(2)}) %collective-permute-start.7) | collective-permute-done | bytes 491552 | tf_op jit(solution)/shard_map/ppermute | solution.py:477
  18.7 0.8 extra.12
  19.5 1.5 %collective-permute-start.11 = (bf16[2,600,128]{2,1,0:T(8,128)(2,1)S(1)}, bf16[2,600,128]{2,1,0:T(8,128)(2,1)S(1)}, u32[]{:S(2)}, u32[]{:S(2)}) collective-permute-start(bf16[2,600,128]{2,1,0:T(8,128)(2,1)S(1)} %get-tuple-element.48), channel_id=1, source_target_pairs={{0,1},{1,0},{2,3},{3,2},{4,5},{5,4},{6,7},{7,6},{8,9},{9,8},{10,11... | collective-permute-start | bytes 921608 | tf_op jit(solution)/shard_map/ppermute | solution.py:512
  21.2 1.6 %collective-permute-start.9 = (bf16[2,4,480,128]{3,2,1,0:T(8,128)(2,1)S(1)}, bf16[2,4,480,128]{3,2,1,0:T(8,128)(2,1)S(1)}, u32[]{:S(2)}, u32[]{:S(2)}) collective-permute-start(bf16[2,4,480,128]{3,2,1,0:T(8,128)(2,1)S(1)} %pad_maximum_fusion.1), channel_id=1, source_target_pairs={{0,8},{8,16},{16,24},{24,28},{28,20},{20,12},{12,4},{4,0},{2,6},{1... | collective-permute-start | bytes 2949128 | tf_op jit(solution)/shard_map/ppermute | solution.py:486
  22.9 6.2 %collective-permute-done.11.refs_3_.refs_4_ = bf16[2,600,128]{2,1,0:T(8,128)(2,1)S(1)} collective-permute-done((bf16[2,600,128]{2,1,0:T(8,128)(2,1)S(1)}, bf16[2,600,128]{2,1,0:T(8,128)(2,1)S(1)}, u32[]{:S(2)}, u32[]{:S(2)}) %collective-permute-start.11) | collective-permute-done | bytes 307232 | tf_op jit(solution)/shard_map/ppermute | solution.py:512
  29.0 0.8 extra.13
  29.8 1.3 %collective-permute-start.12 = (bf16[2,600,128]{2,1,0:T(8,128)(2,1)S(1)}, bf16[2,600,128]{2,1,0:T(8,128)(2,1)S(1)}, u32[]{:S(2)}, u32[]{:S(2)}) collective-permute-start(bf16[2,600,128]{2,1,0:T(8,128)(2,1)S(1)} %get-tuple-element.50), channel_id=1, source_target_pairs={{0,1},{1,0},{2,3},{3,2},{4,5},{5,4},{6,7},{7,6},{8,9},{9,8},{10,11... | collective-permute-start | bytes 921608 | tf_op jit(solution)/shard_map/ppermute | solution.py:512
  31.1 0.8 collective-permute-start.16
  32.0 1.6 %collective-permute-start.5 = (bf16[2,4,480,128]{3,2,1,0:T(8,128)(2,1)S(1)}, bf16[2,4,480,128]{3,2,1,0:T(8,128)(2,1)S(1)}, u32[]{:S(2)}, u32[]{:S(2)}) collective-permute-start(bf16[2,4,480,128]{3,2,1,0:T(8,128)(2,1)S(1)} %pad_maximum_fusion), channel_id=1, source_target_pairs={{0,8},{8,16},{16,24},{24,28},{28,20},{20,12},{12,4},{4,0},{2,6},{1... | collective-permute-start | bytes 2949128 | tf_op jit(solution)/shard_map/ppermute | solution.py:486
  33.7 6.4 %collective-permute-done.12.refs_2_.refs_4_ = bf16[2,600,128]{2,1,0:T(8,128)(2,1)S(1)} collective-permute-done((bf16[2,600,128]{2,1,0:T(8,128)(2,1)S(1)}, bf16[2,600,128]{2,1,0:T(8,128)(2,1)S(1)}, u32[]{:S(2)}, u32[]{:S(2)}) %collective-permute-start.12) | collective-permute-done | bytes 307232 | tf_op jit(solution)/shard_map/ppermute | solution.py:512
  40.1 0.8 extra.14
  40.9 1.1 %collective-permute-start.13 = (bf16[2,600,128]{2,1,0:T(8,128)(2,1)S(1)}, bf16[2,600,128]{2,1,0:T(8,128)(2,1)S(1)}, u32[]{:S(2)}, u32[]{:S(2)}) collective-permute-start(bf16[2,600,128]{2,1,0:T(8,128)(2,1)S(1)} %get-tuple-element.51), channel_id=1, source_target_pairs={{0,1},{1,0},{2,3},{3,2},{4,5},{5,4},{6,7},{7,6},{8,9},{9,8},{10,11... | collective-permute-start | bytes 921608 | tf_op jit(solution)/shard_map/ppermute | solution.py:512
  42.0 0.8 collective-permute-done.16.refs_3_
  42.8 2.5 %correlate.3 = (bf16[16,2520,256]{2,1,0:T(8,128)(2,1)}, bf16[1,2520,256]{2,1,0:T(8,128)(2,1)S(1)}) custom-call(s32[21]{0:T(128)S(1)} %concatenate.15.meta, bf16[1,4,480,128]{3,2,1,0:T(8,128)(2,1)S(1)} %get-tuple-element.88.refs_0_, bf16[1,4,480,128]{3,2,1,0:T(8,128)(2,1)S(1)} %collective-permute-done.7.refs_1_, ...), custom_call_target="tpu_custom_call", output_to_operand_aliasing={{0}: (6, {})} | custom-call | flops 10000001024 | bytes 1000 | tf_op jit(solution)/shard_map/correlate/pallas_call | solution.py:391
  45.3 1.2 %collective-permute-start.10 = (bf16[2,4,480,128]{3,2,1,0:T(8,128)(2,1)S(1)}, bf16[2,4,480,128]{3,2,1,0:T(8,128)(2,1)S(1)}, u32[]{:S(2)}, u32[]{:S(2)}) collective-permute-start(bf16[2,4,480,128]{3,2,1,0:T(8,128)(2,1)S(1)} %collective-permute-done.9.refs_0_.refs_2_), channel_id=1, source_target_pairs={{0,8},{8,16},{16,24},{24,28},{28,20},{20,12},{12,4},{4,0},{2,6},{1... | collective-permute-start | bytes 2949128 | tf_op jit(solution)/shard_map/ppermute | solution.py:486
  46.5 1.9 %collective-permute-done.13.refs_2_.refs_3_ = bf16[2,600,128]{2,1,0:T(8,128)(2,1)S(1)} collective-permute-done((bf16[2,600,128]{2,1,0:T(8,128)(2,1)S(1)}, bf16[2,600,128]{2,1,0:T(8,128)(2,1)S(1)}, u32[]{:S(2)}, u32[]{:S(2)}) %collective-permute-start.13) | collective-permute-done | bytes 307232 | tf_op jit(solution)/shard_map/ppermute | solution.py:512
  48.7 0.8 extra.15
  49.5 1.3 %collective-permute-start.17 = (bf16[2,600,128]{2,1,0:T(8,128)(2,1)S(1)}, bf16[2,600,128]{2,1,0:T(8,128)(2,1)S(1)}, u32[]{:S(2)}, u32[]{:S(2)}) collective-permute-start(bf16[2,600,128]{2,1,0:T(8,128)(2,1)S(1)} %get-tuple-element.58), channel_id=1, source_target_pairs={{0,1},{1,0},{2,3},{3,2},{4,5},{5,4},{6,7},{7,6},{8,9},{9,8},{10,11... | collective-permute-start | bytes 921608 | tf_op jit(solution)/shard_map/ppermute | solution.py:512
  50.8 1.6 %collective-permute-start.6 = (bf16[1,4,480,128]{3,2,1,0:T(8,128)(2,1)S(1)}, bf16[1,4,480,128]{3,2,1,0:T(8,128)(2,1)S(1)}, u32[]{:S(2)}, u32[]{:S(2)}) collective-permute-start(bf16[1,4,480,128]{3,2,1,0:T(8,128)(2,1)S(1)} %slice.12), channel_id=1, source_target_pairs={{0,8},{8,16},{16,24},{24,28},{28,20},{20,12},{12,4},{4,0},{2,6},{1... | collective-permute-start | bytes 1474568 | tf_op jit(solution)/shard_map/ppermute | solution.py:486
  52.5 3.3 %correlate.4 = (bf16[16,2520,256]{2,1,0:T(8,128)(2,1)}, bf16[2,2520,256]{2,1,0:T(8,128)(2,1)S(1)}) custom-call(s32[21]{0:T(128)S(1)} %concatenate.15.meta, bf16[1,4,480,128]{3,2,1,0:T(8,128)(2,1)S(1)} %collective-permute-done.refs_0_, bf16[1,4,480,128]{3,2,1,0:T(8,128)(2,1)S(1)} %collective-permute-done.3.refs_1_, ...), custom_call_target="tpu_custom_call", output_to_operand_aliasing={{0}: (7, {})} | custom-call | flops 10000001024 | bytes 1000 | tf_op jit(solution)/shard_map/correlate/pallas_call | solution.py:391
  55.9 2.1 %collective-permute-done.17.refs_2_.refs_1_ = bf16[2,600,128]{2,1,0:T(8,128)(2,1)S(1)} collective-permute-done((bf16[2,600,128]{2,1,0:T(8,128)(2,1)S(1)}, bf16[2,600,128]{2,1,0:T(8,128)(2,1)S(1)}, u32[]{:S(2)}, u32[]{:S(2)}) %collective-permute-start.17) | collective-permute-done | bytes 307232 | tf_op jit(solution)/shard_map/ppermute | solution.py:512
  58.0 1.5 %collective-permute-done.10.refs_0_.refs_2_ = bf16[2,4,480,128]{3,2,1,0:T(8,128)(2,1)S(1)} collective-permute-done((bf16[2,4,480,128]{3,2,1,0:T(8,128)(2,1)S(1)}, bf16[2,4,480,128]{3,2,1,0:T(8,128)(2,1)S(1)}, u32[]{:S(2)}, u32[]{:S(2)}) %collective-permute-start.10) | collective-permute-done | bytes 983072 | tf_op jit(solution)/shard_map/ppermute | solution.py:486
  59.5 0.8 extra.16
  60.2 1.1 %collective-permute-start.23 = (bf16[2,600,128]{2,1,0:T(8,128)(2,1)S(1)}, bf16[2,600,128]{2,1,0:T(8,128)(2,1)S(1)}, u32[]{:S(2)}, u32[]{:S(2)}) collective-permute-start(bf16[2,600,128]{2,1,0:T(8,128)(2,1)S(1)} %get-tuple-element.62), channel_id=1, source_target_pairs={{0,1},{1,0},{2,3},{3,2},{4,5},{5,4},{6,7},{7,6},{8,9},{9,8},{10,11... | collective-permute-start | bytes 921608 | tf_op jit(solution)/shard_map/ppermute | solution.py:512
  61.4 1.6 %collective-permute-start.19 = (bf16[1,4,480,128]{3,2,1,0:T(8,128)(2,1)S(1)}, bf16[1,4,480,128]{3,2,1,0:T(8,128)(2,1)S(1)}, u32[]{:S(2)}, u32[]{:S(2)}) collective-permute-start(bf16[1,4,480,128]{3,2,1,0:T(8,128)(2,1)S(1)} %get-tuple-element.86), channel_id=1, source_target_pairs={{0,8},{8,16},{16,24},{24,28},{28,20},{20,12},{12,4},{4,0},{2,6},{1... | collective-permute-start | bytes 1474568 | tf_op jit(solution)/shard_map/ppermute | solution.py:486
  63.0 1.7 %collective-permute-done.6.refs_0_ = bf16[1,4,480,128]{3,2,1,0:T(8,128)(2,1)S(1)} collective-permute-done((bf16[1,4,480,128]{3,2,1,0:T(8,128)(2,1)S(1)}, bf16[1,4,480,128]{3,2,1,0:T(8,128)(2,1)S(1)}, u32[]{:S(2)}, u32[]{:S(2)}) %collective-permute-start.6) | collective-permute-done | bytes 491552 | tf_op jit(solution)/shard_map/ppermute | solution.py:486
  64.7 1.4 %collective-permute-start.21 = (bf16[1,4,480,128]{3,2,1,0:T(8,128)(2,1)S(1)}, bf16[1,4,480,128]{3,2,1,0:T(8,128)(2,1)S(1)}, u32[]{:S(2)}, u32[]{:S(2)}) collective-permute-start(bf16[1,4,480,128]{3,2,1,0:T(8,128)(2,1)S(1)} %get-tuple-element.85), channel_id=1, source_target_pairs={{0,8},{8,16},{16,24},{24,28},{28,20},{20,12},{12,4},{4,0},{2,6},{1... | collective-permute-start | bytes 1474568 | tf_op jit(solution)/shard_map/ppermute | solution.py:486
  66.8 2.3 %collective-permute-done.23.refs_3_ = bf16[2,600,128]{2,1,0:T(8,128)(2,1)S(1)} collective-permute-done((bf16[2,600,128]{2,1,0:T(8,128)(2,1)S(1)}, bf16[2,600,128]{2,1,0:T(8,128)(2,1)S(1)}, u32[]{:S(2)}, u32[]{:S(2)}) %collective-permute-start.23) | collective-permute-done | bytes 307232 | tf_op jit(solution)/shard_map/ppermute | solution.py:512
  69.1 0.9 collective-permute-start.25
  70.3 1.6 %collective-permute-start.20 = (bf16[1,4,480,128]{3,2,1,0:T(8,128)(2,1)S(1)}, bf16[1,4,480,128]{3,2,1,0:T(8,128)(2,1)S(1)}, u32[]{:S(2)}, u32[]{:S(2)}) collective-permute-start(bf16[1,4,480,128]{3,2,1,0:T(8,128)(2,1)S(1)} %collective-permute-done.19.refs_0_.refs_1_), channel_id=1, source_target_pairs={{0,8},{8,16},{16,24},{24,28},{28,20},{20,12},{12,4},{4,0},{2,6},{1... | collective-permute-start | bytes 1474568 | tf_op jit(solution)/shard_map/ppermute | solution.py:486
  71.9 3.5 %correlate.5 = (bf16[16,2520,256]{2,1,0:T(8,128)(2,1)}, bf16[2,2520,256]{2,1,0:T(8,128)(2,1)S(1)}) custom-call(s32[21]{0:T(128)S(1)} %concatenate.15.meta, bf16[1,4,480,128]{3,2,1,0:T(8,128)(2,1)S(1)} %collective-permute-done.1.refs_0_, bf16[1,4,480,128]{3,2,1,0:T(8,128)(2,1)S(1)} %collective-permute-done.4.refs_1_, ...), custom_call_target="tpu_custom_call", output_to_operand_aliasing={{0}: (8, {})} | custom-call | flops 3000001024 | bytes 1000 | tf_op jit(solution)/shard_map/correlate/pallas_call | solution.py:391
  75.6 0.8 extra.18
  76.3 1.0 %collective-permute-start.28 = (bf16[2,600,128]{2,1,0:T(8,128)(2,1)S(1)}, bf16[2,600,128]{2,1,0:T(8,128)(2,1)S(1)}, u32[]{:S(2)}, u32[]{:S(2)}) collective-permute-start(bf16[2,600,128]{2,1,0:T(8,128)(2,1)S(1)} %get-tuple-element.71), channel_id=1, source_target_pairs={{0,1},{1,0},{2,3},{3,2},{4,5},{5,4},{6,7},{7,6},{8,9},{9,8},{10,11... | collective-permute-start | bytes 921608 | tf_op jit(solution)/shard_map/ppermute | solution.py:569
  77.4 2.8 %raw_rows.2 = (bf16[16,2520,256]{2,1,0:T(8,128)(2,1)}, bf16[2,2520,256]{2,1,0:T(8,128)(2,1)S(1)}, bf16[2,2520,256]{2,1,0:T(8,128)(2,1)S(1)}) custom-call(s32[21]{0:T(128)S(1)} %concatenate.15.meta, bf16[2,4,480,128]{3,2,1,0:T(8,128)(2,1)S(1)} %collective-permute-done.5.refs_0_, ...), custom_call_target="tpu_custom_call", output_to_operand_aliasing={{0}: (6, {})} | custom-call | flops 1000 | bytes 1000 | tf_op jit(solution)/shard_map/raw_rows/pallas_call | solution.py:417
  80.8 0.7 extra.19
  81.6 1.2 %collective-permute-start.30 = (bf16[1,600,128]{2,1,0:T(8,128)(2,1)S(1)}, bf16[1,600,128]{2,1,0:T(8,128)(2,1)S(1)}, u32[]{:S(2)}, u32[]{:S(2)}) collective-permute-start(bf16[1,600,128]{2,1,0:T(8,128)(2,1)S(1)} %get-tuple-element.78), channel_id=1, source_target_pairs={{0,1},{1,0},{2,3},{3,2},{4,5},{5,4},{6,7},{7,6},{8,9},{9,8},{10,11... | collective-permute-start | bytes 460808 | tf_op jit(solution)/shard_map/ppermute | solution.py:550
  82.8 3.7 %collective-permute-done.28.refs_0_ = bf16[2,600,128]{2,1,0:T(8,128)(2,1)S(1)} collective-permute-done((bf16[2,600,128]{2,1,0:T(8,128)(2,1)S(1)}, bf16[2,600,128]{2,1,0:T(8,128)(2,1)S(1)}, u32[]{:S(2)}, u32[]{:S(2)}) %collective-permute-start.28) | collective-permute-done | bytes 307232 | tf_op jit(solution)/shard_map/ppermute | solution.py:569
  86.5 1.3 %came_rows.2 = (bf16[16,2520,256]{2,1,0:T(8,128)(2,1)}, bf16[2,2520,256]{2,1,0:T(8,128)(2,1)S(1)}, bf16[2,600,256]{2,1,0:T(8,128)(2,1)S(1)}) custom-call(s32[21]{0:T(128)S(1)} %concatenate.15.meta, bf16[2,600,128]{2,1,0:T(8,128)(2,1)S(1)} %collective-permute-done.28.refs_0_, ...), custom_call_target="tpu_custom_call", output_to_operand_aliasing={{0}: (4, {}), {1}: (5, {})} | custom-call | flops 22000001024 | bytes 1000 | tf_op jit(solution)/shard_map/came_rows/pallas_call | solution.py:439
  87.9 3.3 %raw_rows.3 = (bf16[16,2520,256]{2,1,0:T(8,128)(2,1)}, bf16[2,2520,256]{2,1,0:T(8,128)(2,1)S(1)}) custom-call(s32[21]{0:T(128)S(1)} %concatenate.15.meta, bf16[1,4,480,128]{3,2,1,0:T(8,128)(2,1)S(1)} %get-tuple-element.60.refs_0_, bf16[1,4,480,128]{3,2,1,0:T(8,128)(2,1)S(1)} %collective-permute-done.18.refs_5_.refs_1_, ...), custom_call_target="tpu_custom_call", output_to_operand_aliasing={{0}: (9, {})} | custom-call | flops 10000001024 | bytes 1000 | tf_op jit(solution)/shard_map/raw_rows/pallas_call | solution.py:417
  91.9 0.9 collective-permute-done.31.refs_1_
  93.2 2.2 %came_rows.3 = (bf16[16,2520,256]{2,1,0:T(8,128)(2,1)}, bf16[2,2520,256]{2,1,0:T(8,128)(2,1)S(1)}, bf16[2,2520,256]{2,1,0:T(8,128)(2,1)S(1)}) custom-call(s32[21]{0:T(128)S(1)} %concatenate.15.meta, bf16[1,600,128]{2,1,0:T(8,128)(2,1)S(1)} %get-tuple-element.79.refs_0_, ...), custom_call_target="tpu_custom_call", output_to_operand_aliasing={{0}: (7, {}), {1}: (8, {}), {2}: (9, {})} | custom-call | flops 1000 | bytes 1000 | tf_op jit(solution)/shard_map/came_rows/pallas_call | solution.py:439
  (49 shorter events, 6.6 us)
Async XLA Ops:
  1.2 7.0 %collective-permute-start.2 = (bf16[1,4,480,128]{3,2,1,0:T(8,128)(2,1)S(1)}, bf16[1,4,480,128]{3,2,1,0:T(8,128)(2,1)S(1)}, u32[]{:S(2)}, u32[]{:S(2)}) collective-permute-start(bf16[1,4,480,128]{3,2,1,0:T(8,128)(2,1)S(1)} %get-tuple-element.88.refs_0_), channel_id=1, source_target_pairs={{0,2},{2,0},{4,6},{6,4},{8,10},{10,8},{12,14},{14,12},{16,18},{18,... | collective-permute-start | bytes 1474568 | tf_op jit(solution)/shard_map/ppermute | solution.py:486
  1.8 9.4 %collective-permute-start = (bf16[1,4,480,128]{3,2,1,0:T(8,128)(2,1)S(1)}, bf16[1,4,480,128]{3,2,1,0:T(8,128)(2,1)S(1)}, u32[]{:S(2)}, u32[]{:S(2)}) collective-permute-start(bf16[1,4,480,128]{3,2,1,0:T(8,128)(2,1)S(1)} %get-tuple-element.88.refs_0_), channel_id=1, source_target_pairs={{0,8},{8,16},{16,24},{24,28},{28,20},{20,12},{12,4},{4,0},{2,6},{1... | collective-permute-start | bytes 1474568 | tf_op jit(solution)/shard_map/ppermute | solution.py:486
  4.4 13.9 %collective-permute-start.7 = (bf16[1,4,480,128]{3,2,1,0:T(8,128)(2,1)S(1)}, bf16[1,4,480,128]{3,2,1,0:T(8,128)(2,1)S(1)}, u32[]{:S(2)}, u32[]{:S(2)}) collective-permute-start(bf16[1,4,480,128]{3,2,1,0:T(8,128)(2,1)S(1)} %get-tuple-element.87.refs_0_), channel_id=1, source_target_pairs={{0,1},{1,0},{2,3},{3,2},{4,5},{5,4},{6,7},{7,6},{8,9},{9,8},{10,11... | collective-permute-start | bytes 1474568 | tf_op jit(solution)/shard_map/ppermute | solution.py:477
  6.8 14.2 %collective-permute-start.14 = (bf16[256,128]{0,1:T(8,128)(2,1)S(1)}, bf16[256,128]{0,1:T(8,128)(2,1)S(1)}, u32[]{:S(2)}, u32[]{:S(2)}) collective-permute-start(bf16[256,128]{0,1:T(8,128)(2,1)S(1)} %copy.27), channel_id=1, source_target_pairs={{0,1},{1,0},{2,3},{3,2},{4,5},{5,4},{6,7},{7,6},{8,9},{9,8},{10,11... | collective-permute-start | bytes 196616 | tf_op jit(solution)/shard_map/ppermute | solution.py:478
  8.2 10.1 %collective-permute-start.3 = (bf16[1,4,480,128]{3,2,1,0:T(8,128)(2,1)S(1)}, bf16[1,4,480,128]{3,2,1,0:T(8,128)(2,1)S(1)}, u32[]{:S(2)}, u32[]{:S(2)}) collective-permute-start(bf16[1,4,480,128]{3,2,1,0:T(8,128)(2,1)S(1)} %collective-permute-done.2), channel_id=1, source_target_pairs={{0,8},{8,16},{16,24},{24,28},{28,20},{20,12},{12,4},{4,0},{2,6},{1... | collective-permute-start | bytes 1474568 | tf_op jit(solution)/shard_map/ppermute | solution.py:486
  11.2 11.7 %collective-permute-start.1 = (bf16[1,4,480,128]{3,2,1,0:T(8,128)(2,1)S(1)}, bf16[1,4,480,128]{3,2,1,0:T(8,128)(2,1)S(1)}, u32[]{:S(2)}, u32[]{:S(2)}) collective-permute-start(bf16[1,4,480,128]{3,2,1,0:T(8,128)(2,1)S(1)} %collective-permute-done.refs_0_), channel_id=1, source_target_pairs={{0,8},{8,16},{16,24},{24,28},{28,20},{20,12},{12,4},{4,0},{2,6},{1... | collective-permute-start | bytes 1474568 | tf_op jit(solution)/shard_map/ppermute | solution.py:486
  18.3 2.8 %collective-permute-start.8 = (bf16[1,4,480,128]{3,2,1,0:T(8,128)(2,1)S(1)}, bf16[1,4,480,128]{3,2,1,0:T(8,128)(2,1)S(1)}, u32[]{:S(2)}, u32[]{:S(2)}) collective-permute-start(bf16[1,4,480,128]{3,2,1,0:T(8,128)(2,1)S(1)} %collective-permute-done.7.refs_1_), channel_id=1, source_target_pairs={{0,2},{2,0},{4,6},{6,4},{8,10},{10,8},{12,14},{14,12},{16,18},{18,... | collective-permute-start | bytes 1474568 | tf_op jit(solution)/shard_map/ppermute | solution.py:486
  18.3 10.7 %collective-permute-start.4 = (bf16[1,4,480,128]{3,2,1,0:T(8,128)(2,1)S(1)}, bf16[1,4,480,128]{3,2,1,0:T(8,128)(2,1)S(1)}, u32[]{:S(2)}, u32[]{:S(2)}) collective-permute-start(bf16[1,4,480,128]{3,2,1,0:T(8,128)(2,1)S(1)} %collective-permute-done.3.refs_1_), channel_id=1, source_target_pairs={{0,8},{8,16},{16,24},{24,28},{28,20},{20,12},{12,4},{4,0},{2,6},{1... | collective-permute-start | bytes 1474568 | tf_op jit(solution)/shard_map/ppermute | solution.py:486
  19.5 9.6 %collective-permute-start.11 = (bf16[2,600,128]{2,1,0:T(8,128)(2,1)S(1)}, bf16[2,600,128]{2,1,0:T(8,128)(2,1)S(1)}, u32[]{:S(2)}, u32[]{:S(2)}) collective-permute-start(bf16[2,600,128]{2,1,0:T(8,128)(2,1)S(1)} %get-tuple-element.48), channel_id=1, source_target_pairs={{0,1},{1,0},{2,3},{3,2},{4,5},{5,4},{6,7},{7,6},{8,9},{9,8},{10,11... | collective-permute-start | bytes 921608 | tf_op jit(solution)/shard_map/ppermute | solution.py:512
  21.0 10.9 %collective-permute-start.15 = (bf16[256,256]{1,0:T(8,128)(2,1)S(1)}, bf16[256,256]{1,0:T(8,128)(2,1)S(1)}, u32[]{:S(2)}, u32[]{:S(2)}) collective-permute-start(bf16[256,256]{1,0:T(8,128)(2,1)S(1)} %pad_maximum_fusion.3.refs_4_), channel_id=1, source_target_pairs={{0,2},{2,0},{4,6},{6,4},{8,10},{10,8},{12,14},{14,12},{16,18},{18,... | collective-permute-start | bytes 393224 | tf_op jit(solution)/shard_map/ppermute | solution.py:481
  21.2 18.9 %collective-permute-start.9 = (bf16[2,4,480,128]{3,2,1,0:T(8,128)(2,1)S(1)}, bf16[2,4,480,128]{3,2,1,0:T(8,128)(2,1)S(1)}, u32[]{:S(2)}, u32[]{:S(2)}) collective-permute-start(bf16[2,4,480,128]{3,2,1,0:T(8,128)(2,1)S(1)} %pad_maximum_fusion.1), channel_id=1, source_target_pairs={{0,8},{8,16},{16,24},{24,28},{28,20},{20,12},{12,4},{4,0},{2,6},{1... | collective-permute-start | bytes 2949128 | tf_op jit(solution)/shard_map/ppermute | solution.py:486
  29.8 10.3 %collective-permute-start.12 = (bf16[2,600,128]{2,1,0:T(8,128)(2,1)S(1)}, bf16[2,600,128]{2,1,0:T(8,128)(2,1)S(1)}, u32[]{:S(2)}, u32[]{:S(2)}) collective-permute-start(bf16[2,600,128]{2,1,0:T(8,128)(2,1)S(1)} %get-tuple-element.50), channel_id=1, source_target_pairs={{0,1},{1,0},{2,3},{3,2},{4,5},{5,4},{6,7},{7,6},{8,9},{9,8},{10,11... | collective-permute-start | bytes 921608 | tf_op jit(solution)/shard_map/ppermute | solution.py:512
  31.1 11.7 %collective-permute-start.16 = (bf16[1,600,128]{2,1,0:T(8,128)(2,1)S(1)}, bf16[1,600,128]{2,1,0:T(8,128)(2,1)S(1)}, u32[]{:S(2)}, u32[]{:S(2)}) collective-permute-start(bf16[1,600,128]{2,1,0:T(8,128)(2,1)S(1)} %get-tuple-element.53), channel_id=1, source_target_pairs={{0,1},{1,0},{2,3},{3,2},{4,5},{5,4},{6,7},{7,6},{8,9},{9,8},{10,11... | collective-permute-start | bytes 460808 | tf_op jit(solution)/shard_map/ppermute | solution.py:512
  32.0 16.7 %collective-permute-start.5 = (bf16[2,4,480,128]{3,2,1,0:T(8,128)(2,1)S(1)}, bf16[2,4,480,128]{3,2,1,0:T(8,128)(2,1)S(1)}, u32[]{:S(2)}, u32[]{:S(2)}) collective-permute-start(bf16[2,4,480,128]{3,2,1,0:T(8,128)(2,1)S(1)} %pad_maximum_fusion), channel_id=1, source_target_pairs={{0,8},{8,16},{16,24},{24,28},{28,20},{20,12},{12,4},{4,0},{2,6},{1... | collective-permute-start | bytes 2949128 | tf_op jit(solution)/shard_map/ppermute | solution.py:486
  40.9 7.6 %collective-permute-start.13 = (bf16[2,600,128]{2,1,0:T(8,128)(2,1)S(1)}, bf16[2,600,128]{2,1,0:T(8,128)(2,1)S(1)}, u32[]{:S(2)}, u32[]{:S(2)}) collective-permute-start(bf16[2,600,128]{2,1,0:T(8,128)(2,1)S(1)} %get-tuple-element.51), channel_id=1, source_target_pairs={{0,1},{1,0},{2,3},{3,2},{4,5},{5,4},{6,7},{7,6},{8,9},{9,8},{10,11... | collective-permute-start | bytes 921608 | tf_op jit(solution)/shard_map/ppermute | solution.py:512
  45.2 24.7 %collective-permute-start.24 = (bf16[1,2520,256]{2,1,0:T(8,128)(2,1)S(1)}, bf16[1,2520,256]{2,1,0:T(8,128)(2,1)S(1)}, u32[]{:S(2)}, u32[]{:S(2)}) collective-permute-start(bf16[1,2520,256]{2,1,0:T(8,128)(2,1)S(1)} %get-tuple-element.63), channel_id=1, source_target_pairs={{0,2},{2,0},{4,6},{6,4},{8,10},{10,8},{12,14},{14,12},{16,18},{18,... | collective-permute-start | bytes 3870728 | tf_op jit(solution)/shard_map/ppermute | solution.py:486
  45.3 14.1 %collective-permute-start.10 = (bf16[2,4,480,128]{3,2,1,0:T(8,128)(2,1)S(1)}, bf16[2,4,480,128]{3,2,1,0:T(8,128)(2,1)S(1)}, u32[]{:S(2)}, u32[]{:S(2)}) collective-permute-start(bf16[2,4,480,128]{3,2,1,0:T(8,128)(2,1)S(1)} %collective-permute-done.9.refs_0_.refs_2_), channel_id=1, source_target_pairs={{0,8},{8,16},{16,24},{24,28},{28,20},{20,12},{12,4},{4,0},{2,6},{1... | collective-permute-start | bytes 2949128 | tf_op jit(solution)/shard_map/ppermute | solution.py:486
  49.5 8.5 %collective-permute-start.17 = (bf16[2,600,128]{2,1,0:T(8,128)(2,1)S(1)}, bf16[2,600,128]{2,1,0:T(8,128)(2,1)S(1)}, u32[]{:S(2)}, u32[]{:S(2)}) collective-permute-start(bf16[2,600,128]{2,1,0:T(8,128)(2,1)S(1)} %get-tuple-element.58), channel_id=1, source_target_pairs={{0,1},{1,0},{2,3},{3,2},{4,5},{5,4},{6,7},{7,6},{8,9},{9,8},{10,11... | collective-permute-start | bytes 921608 | tf_op jit(solution)/shard_map/ppermute | solution.py:512
  50.8 13.9 %collective-permute-start.6 = (bf16[1,4,480,128]{3,2,1,0:T(8,128)(2,1)S(1)}, bf16[1,4,480,128]{3,2,1,0:T(8,128)(2,1)S(1)}, u32[]{:S(2)}, u32[]{:S(2)}) collective-permute-start(bf16[1,4,480,128]{3,2,1,0:T(8,128)(2,1)S(1)} %slice.12), channel_id=1, source_target_pairs={{0,8},{8,16},{16,24},{24,28},{28,20},{20,12},{12,4},{4,0},{2,6},{1... | collective-permute-start | bytes 1474568 | tf_op jit(solution)/shard_map/ppermute | solution.py:486
  55.8 21.6 %collective-permute-start.22 = (bf16[2,2520,256]{2,1,0:T(8,128)(2,1)S(1)}, bf16[2,2520,256]{2,1,0:T(8,128)(2,1)S(1)}, u32[]{:S(2)}, u32[]{:S(2)}) collective-permute-start(bf16[2,2520,256]{2,1,0:T(8,128)(2,1)S(1)} %get-tuple-element.61), channel_id=1, source_target_pairs={{0,2},{2,0},{4,6},{6,4},{8,10},{10,8},{12,14},{14,12},{16,18},{18,... | collective-permute-start | bytes 7741448 | tf_op jit(solution)/shard_map/ppermute | solution.py:486
  60.2 8.8 %collective-permute-start.23 = (bf16[2,600,128]{2,1,0:T(8,128)(2,1)S(1)}, bf16[2,600,128]{2,1,0:T(8,128)(2,1)S(1)}, u32[]{:S(2)}, u32[]{:S(2)}) collective-permute-start(bf16[2,600,128]{2,1,0:T(8,128)(2,1)S(1)} %get-tuple-element.62), channel_id=1, source_target_pairs={{0,1},{1,0},{2,3},{3,2},{4,5},{5,4},{6,7},{7,6},{8,9},{9,8},{10,11... | collective-permute-start | bytes 921608 | tf_op jit(solution)/shard_map/ppermute | solution.py:512
  61.4 8.9 %collective-permute-start.19 = (bf16[1,4,480,128]{3,2,1,0:T(8,128)(2,1)S(1)}, bf16[1,4,480,128]{3,2,1,0:T(8,128)(2,1)S(1)}, u32[]{:S(2)}, u32[]{:S(2)}) collective-permute-start(bf16[1,4,480,128]{3,2,1,0:T(8,128)(2,1)S(1)} %get-tuple-element.86), channel_id=1, source_target_pairs={{0,8},{8,16},{16,24},{24,28},{28,20},{20,12},{12,4},{4,0},{2,6},{1... | collective-permute-start | bytes 1474568 | tf_op jit(solution)/shard_map/ppermute | solution.py:486
  64.7 10.8 %collective-permute-start.21 = (bf16[1,4,480,128]{3,2,1,0:T(8,128)(2,1)S(1)}, bf16[1,4,480,128]{3,2,1,0:T(8,128)(2,1)S(1)}, u32[]{:S(2)}, u32[]{:S(2)}) collective-permute-start(bf16[1,4,480,128]{3,2,1,0:T(8,128)(2,1)S(1)} %get-tuple-element.85), channel_id=1, source_target_pairs={{0,8},{8,16},{16,24},{24,28},{28,20},{20,12},{12,4},{4,0},{2,6},{1... | collective-permute-start | bytes 1474568 | tf_op jit(solution)/shard_map/ppermute | solution.py:486
  69.1 6.3 %collective-permute-start.25 = (bf16[1,600,128]{2,1,0:T(8,128)(2,1)S(1)}, bf16[1,600,128]{2,1,0:T(8,128)(2,1)S(1)}, u32[]{:S(2)}, u32[]{:S(2)}) collective-permute-start(bf16[1,600,128]{2,1,0:T(8,128)(2,1)S(1)} %get-tuple-element.66), channel_id=1, source_target_pairs={{0,1},{1,0},{2,3},{3,2},{4,5},{5,4},{6,7},{7,6},{8,9},{9,8},{10,11... | collective-permute-start | bytes 460808 | tf_op jit(solution)/shard_map/ppermute | solution.py:550
  70.0 11.6 %collective-permute-start.18 = (bf16[1,4,480,128]{3,2,1,0:T(8,128)(2,1)S(1)}, bf16[1,4,480,128]{3,2,1,0:T(8,128)(2,1)S(1)}, u32[]{:S(2)}, u32[]{:S(2)}) collective-permute-start(bf16[1,4,480,128]{3,2,1,0:T(8,128)(2,1)S(1)} %get-tuple-element.60.refs_0_), channel_id=1, source_target_pairs={{0,2},{2,0},{4,6},{6,4},{8,10},{10,8},{12,14},{14,12},{16,18},{18,... | collective-permute-start | bytes 1474568 | tf_op jit(solution)/shard_map/ppermute | solution.py:486
  70.3 10.5 %collective-permute-start.20 = (bf16[1,4,480,128]{3,2,1,0:T(8,128)(2,1)S(1)}, bf16[1,4,480,128]{3,2,1,0:T(8,128)(2,1)S(1)}, u32[]{:S(2)}, u32[]{:S(2)}) collective-permute-start(bf16[1,4,480,128]{3,2,1,0:T(8,128)(2,1)S(1)} %collective-permute-done.19.refs_0_.refs_1_), channel_id=1, source_target_pairs={{0,8},{8,16},{16,24},{24,28},{28,20},{20,12},{12,4},{4,0},{2,6},{1... | collective-permute-start | bytes 1474568 | tf_op jit(solution)/shard_map/ppermute | solution.py:486
  75.4 12.5 %collective-permute-start.27 = (bf16[2,2520,256]{2,1,0:T(8,128)(2,1)S(1)}, bf16[2,2520,256]{2,1,0:T(8,128)(2,1)S(1)}, u32[]{:S(2)}, u32[]{:S(2)}) collective-permute-start(bf16[2,2520,256]{2,1,0:T(8,128)(2,1)S(1)} %get-tuple-element.70), channel_id=1, source_target_pairs={{0,2},{2,0},{4,6},{6,4},{8,10},{10,8},{12,14},{14,12},{16,18},{18,... | collective-permute-start | bytes 7741448 | tf_op jit(solution)/shard_map/ppermute | solution.py:486
  76.3 10.1 %collective-permute-start.28 = (bf16[2,600,128]{2,1,0:T(8,128)(2,1)S(1)}, bf16[2,600,128]{2,1,0:T(8,128)(2,1)S(1)}, u32[]{:S(2)}, u32[]{:S(2)}) collective-permute-start(bf16[2,600,128]{2,1,0:T(8,128)(2,1)S(1)} %get-tuple-element.71), channel_id=1, source_target_pairs={{0,1},{1,0},{2,3},{3,2},{4,5},{5,4},{6,7},{7,6},{8,9},{9,8},{10,11... | collective-permute-start | bytes 921608 | tf_op jit(solution)/shard_map/ppermute | solution.py:569
  80.2 7.7 %collective-permute-start.29 = (bf16[2,2520,256]{2,1,0:T(8,128)(2,1)S(1)}, bf16[2,2520,256]{2,1,0:T(8,128)(2,1)S(1)}, u32[]{:S(2)}, u32[]{:S(2)}) collective-permute-start(bf16[2,2520,256]{2,1,0:T(8,128)(2,1)S(1)} %get-tuple-element.75), channel_id=1, source_target_pairs={{0,2},{2,0},{4,6},{6,4},{8,10},{10,8},{12,14},{14,12},{16,18},{18,... | collective-permute-start | bytes 7741448 | tf_op jit(solution)/shard_map/ppermute | solution.py:486
  81.5 6.4 %collective-permute-start.26 = (bf16[1,4,480,128]{3,2,1,0:T(8,128)(2,1)S(1)}, bf16[1,4,480,128]{3,2,1,0:T(8,128)(2,1)S(1)}, u32[]{:S(2)}, u32[]{:S(2)}) collective-permute-start(bf16[1,4,480,128]{3,2,1,0:T(8,128)(2,1)S(1)} %get-tuple-element.69.refs_2_), channel_id=1, source_target_pairs={{0,2},{2,0},{4,6},{6,4},{8,10},{10,8},{12,14},{14,12},{16,18},{18,... | collective-permute-start | bytes 1474568 | tf_op jit(solution)/shard_map/ppermute | solution.py:486
  81.6 9.6 %collective-permute-start.30 = (bf16[1,600,128]{2,1,0:T(8,128)(2,1)S(1)}, bf16[1,600,128]{2,1,0:T(8,128)(2,1)S(1)}, u32[]{:S(2)}, u32[]{:S(2)}) collective-permute-start(bf16[1,600,128]{2,1,0:T(8,128)(2,1)S(1)} %get-tuple-element.78), channel_id=1, source_target_pairs={{0,1},{1,0},{2,3},{3,2},{4,5},{5,4},{6,7},{7,6},{8,9},{9,8},{10,11... | collective-permute-start | bytes 460808 | tf_op jit(solution)/shard_map/ppermute | solution.py:550
  87.8 4.1 %collective-permute-start.33 = (bf16[2,600,256]{2,1,0:T(8,128)(2,1)S(1)}, bf16[2,600,256]{2,1,0:T(8,128)(2,1)S(1)}, u32[]{:S(2)}, u32[]{:S(2)}) collective-permute-start(bf16[2,600,256]{2,1,0:T(8,128)(2,1)S(1)} %get-tuple-element.81), channel_id=1, source_target_pairs={{0,2},{2,0},{4,6},{6,4},{8,10},{10,8},{12,14},{14,12},{16,18},{18,... | collective-permute-start | bytes 1843208 | tf_op jit(solution)/shard_map/ppermute | solution.py:486
  91.2 1.6 %collective-permute-start.31 = (bf16[1,600,128]{2,1,0:T(8,128)(2,1)S(1)}, bf16[1,600,128]{2,1,0:T(8,128)(2,1)S(1)}, u32[]{:S(2)}, u32[]{:S(2)}) collective-permute-start(bf16[1,600,128]{2,1,0:T(8,128)(2,1)S(1)} %get-tuple-element.79.refs_0_), channel_id=1, source_target_pairs={{0,2},{2,0},{4,6},{6,4},{8,10},{10,8},{12,14},{14,12},{16,18},{18,... | collective-permute-start | bytes 460808 | tf_op jit(solution)/shard_map/ppermute | solution.py:486
  91.8 1.4 %collective-permute-start.32 = (bf16[1,600,128]{2,1,0:T(8,128)(2,1)S(1)}, bf16[1,600,128]{2,1,0:T(8,128)(2,1)S(1)}, u32[]{:S(2)}, u32[]{:S(2)}) collective-permute-start(bf16[1,600,128]{2,1,0:T(8,128)(2,1)S(1)} %get-tuple-element.80.refs_2_), channel_id=1, source_target_pairs={{0,2},{2,0},{4,6},{6,4},{8,10},{10,8},{12,14},{14,12},{16,18},{18,... | collective-permute-start | bytes 460808 | tf_op jit(solution)/shard_map/ppermute | solution.py:486

commit v4 on v3

--- a/solution.py
+++ b/solution.py
@@ -8,7 +8,7 @@
 from jax.sharding import PartitionSpec as P
 
 LANES = 128
-PARAMS = {'LAG': 2, 'F0': 10, 'F1': 0, 'PS0': 2, 'JA': 3, 'JB': 1, 'C0POS': 2, 'GATE': 30, 'F3': 0, 'F2': 22, 'NL': 1, 'PE4': 0, 'P4': 0, 'P3': 1, 'CPOS': 1, 'LC': 0, 'BSPL': 1, 'ONEX': 1, 'EL': 1, 'WH': 0, 'X00': 10, 'X01': 10, 'C0': 10, 'X10': 10, 'X11': 10, 'C1': 10, 'X20': 10, 'X21': 10, 'C2': 3, 'X30': 10, 'X31': 3, 'C3': 10, 'X40': 10, 'X41': 10, 'C4': 10}
+PARAMS = {'LAG': 2, 'F0': 10, 'F1': 0, 'PS0': 2, 'JA': 3, 'JB': 1, 'C0POS': 2, 'GATE': 30, 'F3': 0, 'F2': 22, 'NL': 1, 'PE4': 0, 'P4': 0, 'P3': 1, 'CPOS': 1, 'LC': 1, 'BSPL': 1, 'ONEX': 1, 'EL': 1, 'WH': 0, 'X00': 10, 'X01': 10, 'C0': 10, 'X10': 10, 'X11': 10, 'C1': 10, 'X20': 10, 'X21': 10, 'C2': 3, 'X30': 10, 'X31': 3, 'C3': 10, 'X40': 10, 'X41': 24, 'C4': 10}
 
 
 def G(name):

time: 95.7 us -> 96.2 us (level)
  transfers between devices with their start and end apart: 34 -> 34, of which waited for: 17 -> 16; matrix products, arithmetic and copies ran while one was open for 1% -> 1% of each run, Pallas kernels for 25% -> 25%
where the time goes in v4:
time: 96.2 us; the launch traced here: 96 us
  waiting for transfers between devices  34.5 us (36%)
  starting transfers between devices  32.4 us (34%)
  Pallas kernels  26.1 us (27%)
  local copies, waits for them, and re-layouts  2.36 us (2%)
    ppermute x22, starting transfers between devices, permute_rows(): return [lax.ppermute(piece, 'rows', pairs) for piece in pieces]  19.8 us
    ppermute x6, waiting for transfers between devices, do_extra(): across_came[d, 1 - part].append(lax.ppermute(extra, 'chan', across))  19.7 us
    pallas_call x3, Pallas kernels, correlate(): pl.pallas_call(functools.partial(corr_kernel, factor, tuple((len(part) fo...  9.29 us
    pallas_call x10, Pallas kernels, make_extra(): pl.pallas_call(functools.partial(extra_kernel, len(halves), 2 + len(carri...  7.18 us
    ppermute x6, starting transfers between devices, do_extra(): across_came[d, 1 - part].append(lax.ppermute(extra, 'chan', across))  7.11 us
    ppermute x22, waiting for transfers between devices, permute_rows(): return [lax.ppermute(piece, 'rows', pairs) for piece in pieces]  5.91 us
    pallas_call x2, Pallas kernels, raw_rows(): pl.pallas_call(functools.partial(raw_kernel, factor, (len(own), len(other...  5.31 us
    ppermute x1, waiting for transfers between devices, ring_local(): partner = lax.ppermute(theirs, 'chan', across)  5.11 us
  transfers between devices with their start and end apart: 34, of which 16 were waited for; matrix products, arithmetic and copies ran while one was open for 1% of the time, Pallas kernels for 25%

profile of v4, /device:TPU:0, one launch (start us, length us, event | category | flops | bytes accessed | tf_op | source)
XLA Modules:
  0.0 96.0 jit_solution(13315735556391627353)
XLA Ops:
  0.0 1.2 %dynamic-slice_bitcast_fusion = (bf16[1,4,480,128]{3,2,1,0:T(8,128)(2,1)S(1)}, bf16[1,4,480,128]{3,2,1,0:T(8,128)(2,1)S(1)}) fusion(bf16[8,480,128]{2,1,0:T(8,128)(2,1)} %param.3, s32[]{:T(128)S(6)} %select_n.72, s32[]{:T(128)S(6)} %select_n.71), kind=kLoop, calls=%fused_computation.2 | loop fusion | bytes 1966088 | tf_op jit(solution)/shard_map/broadcast_in_dim | solution.py:469
  1.8 2.6 %collective-permute-start = (bf16[1,4,480,128]{3,2,1,0:T(8,128)(2,1)S(1)}, bf16[1,4,480,128]{3,2,1,0:T(8,128)(2,1)S(1)}, u32[]{:S(2)}, u32[]{:S(2)}) collective-permute-start(bf16[1,4,480,128]{3,2,1,0:T(8,128)(2,1)S(1)} %get-tuple-element.88.refs_0_), channel_id=1, source_target_pairs={{0,8},{8,16},{16,24},{24,28},{28,20},{20,12},{12,4},{4,0},{2,6},{1... | collective-permute-start | bytes 1474568 | tf_op jit(solution)/shard_map/ppermute | solution.py:486
  4.4 1.5 %collective-permute-start.7 = (bf16[1,4,480,128]{3,2,1,0:T(8,128)(2,1)S(1)}, bf16[1,4,480,128]{3,2,1,0:T(8,128)(2,1)S(1)}, u32[]{:S(2)}, u32[]{:S(2)}) collective-permute-start(bf16[1,4,480,128]{3,2,1,0:T(8,128)(2,1)S(1)} %get-tuple-element.87.refs_0_), channel_id=1, source_target_pairs={{0,1},{1,0},{2,3},{3,2},{4,5},{5,4},{6,7},{7,6},{8,9},{9,8},{10,11... | collective-permute-start | bytes 1474568 | tf_op jit(solution)/shard_map/ppermute | solution.py:477
  5.9 0.9 copy.27
  8.2 1.6 %collective-permute-start.3 = (bf16[1,4,480,128]{3,2,1,0:T(8,128)(2,1)S(1)}, bf16[1,4,480,128]{3,2,1,0:T(8,128)(2,1)S(1)}, u32[]{:S(2)}, u32[]{:S(2)}) collective-permute-start(bf16[1,4,480,128]{3,2,1,0:T(8,128)(2,1)S(1)} %collective-permute-done.2), channel_id=1, source_target_pairs={{0,8},{8,16},{16,24},{24,28},{28,20},{20,12},{12,4},{4,0},{2,6},{1... | collective-permute-start | bytes 1474568 | tf_op jit(solution)/shard_map/ppermute | solution.py:486
  10.5 0.7 collective-permute-done.refs_0_
  11.2 2.1 %collective-permute-start.1 = (bf16[1,4,480,128]{3,2,1,0:T(8,128)(2,1)S(1)}, bf16[1,4,480,128]{3,2,1,0:T(8,128)(2,1)S(1)}, u32[]{:S(2)}, u32[]{:S(2)}) collective-permute-start(bf16[1,4,480,128]{3,2,1,0:T(8,128)(2,1)S(1)} %collective-permute-done.refs_0_), channel_id=1, source_target_pairs={{0,8},{8,16},{16,24},{24,28},{28,20},{20,12},{12,4},{4,0},{2,6},{1... | collective-permute-start | bytes 1474568 | tf_op jit(solution)/shard_map/ppermute | solution.py:486
  13.2 5.1 %collective-permute-done.7.refs_1_ = bf16[1,4,480,128]{3,2,1,0:T(8,128)(2,1)S(1)} collective-permute-done((bf16[1,4,480,128]{3,2,1,0:T(8,128)(2,1)S(1)}, bf16[1,4,480,128]{3,2,1,0:T(8,128)(2,1)S(1)}, u32[]{:S(2)}, u32[]{:S(2)}) %collective-permute-start.7) | collective-permute-done | bytes 491552 | tf_op jit(solution)/shard_map/ppermute | solution.py:477
  18.7 0.8 extra.12
  19.5 1.5 %collective-permute-start.11 = (bf16[2,600,128]{2,1,0:T(8,128)(2,1)S(1)}, bf16[2,600,128]{2,1,0:T(8,128)(2,1)S(1)}, u32[]{:S(2)}, u32[]{:S(2)}) collective-permute-start(bf16[2,600,128]{2,1,0:T(8,128)(2,1)S(1)} %get-tuple-element.48), channel_id=1, source_target_pairs={{0,1},{1,0},{2,3},{3,2},{4,5},{5,4},{6,7},{7,6},{8,9},{9,8},{10,11... | collective-permute-start | bytes 921608 | tf_op jit(solution)/shard_map/ppermute | solution.py:512
  21.2 1.6 %collective-permute-start.9 = (bf16[2,4,480,128]{3,2,1,0:T(8,128)(2,1)S(1)}, bf16[2,4,480,128]{3,2,1,0:T(8,128)(2,1)S(1)}, u32[]{:S(2)}, u32[]{:S(2)}) collective-permute-start(bf16[2,4,480,128]{3,2,1,0:T(8,128)(2,1)S(1)} %pad_maximum_fusion.1), channel_id=1, source_target_pairs={{0,8},{8,16},{16,24},{24,28},{28,20},{20,12},{12,4},{4,0},{2,6},{1... | collective-permute-start | bytes 2949128 | tf_op jit(solution)/shard_map/ppermute | solution.py:486
  22.9 6.2 %collective-permute-done.11.refs_3_.refs_4_ = bf16[2,600,128]{2,1,0:T(8,128)(2,1)S(1)} collective-permute-done((bf16[2,600,128]{2,1,0:T(8,128)(2,1)S(1)}, bf16[2,600,128]{2,1,0:T(8,128)(2,1)S(1)}, u32[]{:S(2)}, u32[]{:S(2)}) %collective-permute-start.11) | collective-permute-done | bytes 307232 | tf_op jit(solution)/shard_map/ppermute | solution.py:512
  29.0 0.8 extra.13
  29.8 1.3 %collective-permute-start.12 = (bf16[2,600,128]{2,1,0:T(8,128)(2,1)S(1)}, bf16[2,600,128]{2,1,0:T(8,128)(2,1)S(1)}, u32[]{:S(2)}, u32[]{:S(2)}) collective-permute-start(bf16[2,600,128]{2,1,0:T(8,128)(2,1)S(1)} %get-tuple-element.50), channel_id=1, source_target_pairs={{0,1},{1,0},{2,3},{3,2},{4,5},{5,4},{6,7},{7,6},{8,9},{9,8},{10,11... | collective-permute-start | bytes 921608 | tf_op jit(solution)/shard_map/ppermute | solution.py:512
  31.1 0.8 collective-permute-start.16
  32.0 1.6 %collective-permute-start.5 = (bf16[2,4,480,128]{3,2,1,0:T(8,128)(2,1)S(1)}, bf16[2,4,480,128]{3,2,1,0:T(8,128)(2,1)S(1)}, u32[]{:S(2)}, u32[]{:S(2)}) collective-permute-start(bf16[2,4,480,128]{3,2,1,0:T(8,128)(2,1)S(1)} %pad_maximum_fusion), channel_id=1, source_target_pairs={{0,8},{8,16},{16,24},{24,28},{28,20},{20,12},{12,4},{4,0},{2,6},{1... | collective-permute-start | bytes 2949128 | tf_op jit(solution)/shard_map/ppermute | solution.py:486
  33.7 6.4 %collective-permute-done.12.refs_2_.refs_4_ = bf16[2,600,128]{2,1,0:T(8,128)(2,1)S(1)} collective-permute-done((bf16[2,600,128]{2,1,0:T(8,128)(2,1)S(1)}, bf16[2,600,128]{2,1,0:T(8,128)(2,1)S(1)}, u32[]{:S(2)}, u32[]{:S(2)}) %collective-permute-start.12) | collective-permute-done | bytes 307232 | tf_op jit(solution)/shard_map/ppermute | solution.py:512
  40.1 0.8 extra.14
  40.9 1.1 %collective-permute-start.13 = (bf16[2,600,128]{2,1,0:T(8,128)(2,1)S(1)}, bf16[2,600,128]{2,1,0:T(8,128)(2,1)S(1)}, u32[]{:S(2)}, u32[]{:S(2)}) collective-permute-start(bf16[2,600,128]{2,1,0:T(8,128)(2,1)S(1)} %get-tuple-element.51), channel_id=1, source_target_pairs={{0,1},{1,0},{2,3},{3,2},{4,5},{5,4},{6,7},{7,6},{8,9},{9,8},{10,11... | collective-permute-start | bytes 921608 | tf_op jit(solution)/shard_map/ppermute | solution.py:512
  42.0 0.8 collective-permute-done.16.refs_3_
  42.8 2.5 %correlate.3 = (bf16[16,2520,256]{2,1,0:T(8,128)(2,1)}, bf16[1,2520,256]{2,1,0:T(8,128)(2,1)S(1)}) custom-call(s32[21]{0:T(128)S(1)} %concatenate.15.meta, bf16[1,4,480,128]{3,2,1,0:T(8,128)(2,1)S(1)} %get-tuple-element.88.refs_0_, bf16[1,4,480,128]{3,2,1,0:T(8,128)(2,1)S(1)} %collective-permute-done.7.refs_1_, ...), custom_call_target="tpu_custom_call", output_to_operand_aliasing={{0}: (6, {})} | custom-call | flops 10000001024 | bytes 1000 | tf_op jit(solution)/shard_map/correlate/pallas_call | solution.py:391
  45.3 1.2 %collective-permute-start.10 = (bf16[2,4,480,128]{3,2,1,0:T(8,128)(2,1)S(1)}, bf16[2,4,480,128]{3,2,1,0:T(8,128)(2,1)S(1)}, u32[]{:S(2)}, u32[]{:S(2)}) collective-permute-start(bf16[2,4,480,128]{3,2,1,0:T(8,128)(2,1)S(1)} %collective-permute-done.9.refs_0_.refs_2_), channel_id=1, source_target_pairs={{0,8},{8,16},{16,24},{24,28},{28,20},{20,12},{12,4},{4,0},{2,6},{1... | collective-permute-start | bytes 2949128 | tf_op jit(solution)/shard_map/ppermute | solution.py:486
  46.5 1.9 %collective-permute-done.13.refs_2_.refs_3_ = bf16[2,600,128]{2,1,0:T(8,128)(2,1)S(1)} collective-permute-done((bf16[2,600,128]{2,1,0:T(8,128)(2,1)S(1)}, bf16[2,600,128]{2,1,0:T(8,128)(2,1)S(1)}, u32[]{:S(2)}, u32[]{:S(2)}) %collective-permute-start.13) | collective-permute-done | bytes 307232 | tf_op jit(solution)/shard_map/ppermute | solution.py:512
  48.7 0.8 extra.15
  49.5 1.3 %collective-permute-start.17 = (bf16[2,600,128]{2,1,0:T(8,128)(2,1)S(1)}, bf16[2,600,128]{2,1,0:T(8,128)(2,1)S(1)}, u32[]{:S(2)}, u32[]{:S(2)}) collective-permute-start(bf16[2,600,128]{2,1,0:T(8,128)(2,1)S(1)} %get-tuple-element.58), channel_id=1, source_target_pairs={{0,1},{1,0},{2,3},{3,2},{4,5},{5,4},{6,7},{7,6},{8,9},{9,8},{10,11... | collective-permute-start | bytes 921608 | tf_op jit(solution)/shard_map/ppermute | solution.py:512
  50.8 1.6 %collective-permute-start.6 = (bf16[1,4,480,128]{3,2,1,0:T(8,128)(2,1)S(1)}, bf16[1,4,480,128]{3,2,1,0:T(8,128)(2,1)S(1)}, u32[]{:S(2)}, u32[]{:S(2)}) collective-permute-start(bf16[1,4,480,128]{3,2,1,0:T(8,128)(2,1)S(1)} %slice.12), channel_id=1, source_target_pairs={{0,8},{8,16},{16,24},{24,28},{28,20},{20,12},{12,4},{4,0},{2,6},{1... | collective-permute-start | bytes 1474568 | tf_op jit(solution)/shard_map/ppermute | solution.py:486
  52.5 3.3 %correlate.4 = (bf16[16,2520,256]{2,1,0:T(8,128)(2,1)}, bf16[2,2520,256]{2,1,0:T(8,128)(2,1)S(1)}) custom-call(s32[21]{0:T(128)S(1)} %concatenate.15.meta, bf16[1,4,480,128]{3,2,1,0:T(8,128)(2,1)S(1)} %collective-permute-done.refs_0_, bf16[1,4,480,128]{3,2,1,0:T(8,128)(2,1)S(1)} %collective-permute-done.3.refs_1_, ...), custom_call_target="tpu_custom_call", output_to_operand_aliasing={{0}: (7, {})} | custom-call | flops 10000001024 | bytes 1000 | tf_op jit(solution)/shard_map/correlate/pallas_call | solution.py:391
  55.9 2.1 %collective-permute-done.17.refs_2_.refs_1_ = bf16[2,600,128]{2,1,0:T(8,128)(2,1)S(1)} collective-permute-done((bf16[2,600,128]{2,1,0:T(8,128)(2,1)S(1)}, bf16[2,600,128]{2,1,0:T(8,128)(2,1)S(1)}, u32[]{:S(2)}, u32[]{:S(2)}) %collective-permute-start.17) | collective-permute-done | bytes 307232 | tf_op jit(solution)/shard_map/ppermute | solution.py:512
  58.0 1.5 %collective-permute-done.10.refs_0_.refs_2_ = bf16[2,4,480,128]{3,2,1,0:T(8,128)(2,1)S(1)} collective-permute-done((bf16[2,4,480,128]{3,2,1,0:T(8,128)(2,1)S(1)}, bf16[2,4,480,128]{3,2,1,0:T(8,128)(2,1)S(1)}, u32[]{:S(2)}, u32[]{:S(2)}) %collective-permute-start.10) | collective-permute-done | bytes 983072 | tf_op jit(solution)/shard_map/ppermute | solution.py:486
  59.5 0.8 extra.16
  60.2 1.1 %collective-permute-start.23 = (bf16[2,600,128]{2,1,0:T(8,128)(2,1)S(1)}, bf16[2,600,128]{2,1,0:T(8,128)(2,1)S(1)}, u32[]{:S(2)}, u32[]{:S(2)}) collective-permute-start(bf16[2,600,128]{2,1,0:T(8,128)(2,1)S(1)} %get-tuple-element.62), channel_id=1, source_target_pairs={{0,1},{1,0},{2,3},{3,2},{4,5},{5,4},{6,7},{7,6},{8,9},{9,8},{10,11... | collective-permute-start | bytes 921608 | tf_op jit(solution)/shard_map/ppermute | solution.py:512
  61.4 1.6 %collective-permute-start.19 = (bf16[1,4,480,128]{3,2,1,0:T(8,128)(2,1)S(1)}, bf16[1,4,480,128]{3,2,1,0:T(8,128)(2,1)S(1)}, u32[]{:S(2)}, u32[]{:S(2)}) collective-permute-start(bf16[1,4,480,128]{3,2,1,0:T(8,128)(2,1)S(1)} %get-tuple-element.86), channel_id=1, source_target_pairs={{0,8},{8,16},{16,24},{24,28},{28,20},{20,12},{12,4},{4,0},{2,6},{1... | collective-permute-start | bytes 1474568 | tf_op jit(solution)/shard_map/ppermute | solution.py:486
  63.0 1.7 %collective-permute-done.6.refs_0_ = bf16[1,4,480,128]{3,2,1,0:T(8,128)(2,1)S(1)} collective-permute-done((bf16[1,4,480,128]{3,2,1,0:T(8,128)(2,1)S(1)}, bf16[1,4,480,128]{3,2,1,0:T(8,128)(2,1)S(1)}, u32[]{:S(2)}, u32[]{:S(2)}) %collective-permute-start.6) | collective-permute-done | bytes 491552 | tf_op jit(solution)/shard_map/ppermute | solution.py:486
  64.7 1.4 %collective-permute-start.21 = (bf16[1,4,480,128]{3,2,1,0:T(8,128)(2,1)S(1)}, bf16[1,4,480,128]{3,2,1,0:T(8,128)(2,1)S(1)}, u32[]{:S(2)}, u32[]{:S(2)}) collective-permute-start(bf16[1,4,480,128]{3,2,1,0:T(8,128)(2,1)S(1)} %get-tuple-element.85), channel_id=1, source_target_pairs={{0,8},{8,16},{16,24},{24,28},{28,20},{20,12},{12,4},{4,0},{2,6},{1... | collective-permute-start | bytes 1474568 | tf_op jit(solution)/shard_map/ppermute | solution.py:486
  66.8 2.3 %collective-permute-done.23.refs_3_ = bf16[2,600,128]{2,1,0:T(8,128)(2,1)S(1)} collective-permute-done((bf16[2,600,128]{2,1,0:T(8,128)(2,1)S(1)}, bf16[2,600,128]{2,1,0:T(8,128)(2,1)S(1)}, u32[]{:S(2)}, u32[]{:S(2)}) %collective-permute-start.23) | collective-permute-done | bytes 307232 | tf_op jit(solution)/shard_map/ppermute | solution.py:512
  69.1 0.9 collective-permute-start.25
  70.3 1.6 %collective-permute-start.20 = (bf16[1,4,480,128]{3,2,1,0:T(8,128)(2,1)S(1)}, bf16[1,4,480,128]{3,2,1,0:T(8,128)(2,1)S(1)}, u32[]{:S(2)}, u32[]{:S(2)}) collective-permute-start(bf16[1,4,480,128]{3,2,1,0:T(8,128)(2,1)S(1)} %collective-permute-done.19.refs_0_.refs_1_), channel_id=1, source_target_pairs={{0,8},{8,16},{16,24},{24,28},{28,20},{20,12},{12,4},{4,0},{2,6},{1... | collective-permute-start | bytes 1474568 | tf_op jit(solution)/shard_map/ppermute | solution.py:486
  71.9 3.5 %correlate.5 = (bf16[16,2520,256]{2,1,0:T(8,128)(2,1)}, bf16[2,2520,256]{2,1,0:T(8,128)(2,1)S(1)}) custom-call(s32[21]{0:T(128)S(1)} %concatenate.15.meta, bf16[1,4,480,128]{3,2,1,0:T(8,128)(2,1)S(1)} %collective-permute-done.1.refs_0_, bf16[1,4,480,128]{3,2,1,0:T(8,128)(2,1)S(1)} %collective-permute-done.4.refs_1_, ...), custom_call_target="tpu_custom_call", output_to_operand_aliasing={{0}: (8, {})} | custom-call | flops 3000001024 | bytes 1000 | tf_op jit(solution)/shard_map/correlate/pallas_call | solution.py:391
  76.0 0.8 extra.18
  76.8 1.1 %collective-permute-start.27 = (bf16[2,600,128]{2,1,0:T(8,128)(2,1)S(1)}, bf16[2,600,128]{2,1,0:T(8,128)(2,1)S(1)}, u32[]{:S(2)}, u32[]{:S(2)}) collective-permute-start(bf16[2,600,128]{2,1,0:T(8,128)(2,1)S(1)} %get-tuple-element.70), channel_id=1, source_target_pairs={{0,1},{1,0},{2,3},{3,2},{4,5},{5,4},{6,7},{7,6},{8,9},{9,8},{10,11... | collective-permute-start | bytes 921608 | tf_op jit(solution)/shard_map/ppermute | solution.py:569
  77.9 2.8 %raw_rows.2 = (bf16[16,2520,256]{2,1,0:T(8,128)(2,1)}, bf16[2,2520,256]{2,1,0:T(8,128)(2,1)S(1)}, bf16[2,2520,256]{2,1,0:T(8,128)(2,1)S(1)}) custom-call(s32[21]{0:T(128)S(1)} %concatenate.15.meta, bf16[2,4,480,128]{3,2,1,0:T(8,128)(2,1)S(1)} %collective-permute-done.5.refs_0_, ...), custom_call_target="tpu_custom_call", output_to_operand_aliasing={{0}: (6, {})} | custom-call | flops 1000 | bytes 1000 | tf_op jit(solution)/shard_map/raw_rows/pallas_call | solution.py:417
  80.8 0.7 extra.19
  82.0 1.2 %collective-permute-start.30 = (bf16[1,600,128]{2,1,0:T(8,128)(2,1)S(1)}, bf16[1,600,128]{2,1,0:T(8,128)(2,1)S(1)}, u32[]{:S(2)}, u32[]{:S(2)}) collective-permute-start(bf16[1,600,128]{2,1,0:T(8,128)(2,1)S(1)} %get-tuple-element.78), channel_id=1, source_target_pairs={{0,1},{1,0},{2,3},{3,2},{4,5},{5,4},{6,7},{7,6},{8,9},{9,8},{10,11... | collective-permute-start | bytes 460808 | tf_op jit(solution)/shard_map/ppermute | solution.py:550
  83.2 3.7 %collective-permute-done.27.refs_0_ = bf16[2,600,128]{2,1,0:T(8,128)(2,1)S(1)} collective-permute-done((bf16[2,600,128]{2,1,0:T(8,128)(2,1)S(1)}, bf16[2,600,128]{2,1,0:T(8,128)(2,1)S(1)}, u32[]{:S(2)}, u32[]{:S(2)}) %collective-permute-start.27) | collective-permute-done | bytes 307232 | tf_op jit(solution)/shard_map/ppermute | solution.py:569
  87.0 2.1 %came_rows.2 = (bf16[16,2520,256]{2,1,0:T(8,128)(2,1)}, bf16[2,2520,256]{2,1,0:T(8,128)(2,1)S(1)}, bf16[2,600,256]{2,1,0:T(8,128)(2,1)S(1)}) custom-call(s32[21]{0:T(128)S(1)} %concatenate.15.meta, bf16[2,600,128]{2,1,0:T(8,128)(2,1)S(1)} %collective-permute-done.27.refs_0_, ...), custom_call_target="tpu_custom_call", output_to_operand_aliasing={{0}: (4, {}), {1}: (5, {})} | custom-call | flops 22000001024 | bytes 1000 | tf_op jit(solution)/shard_map/came_rows/pallas_call | solution.py:439
  89.1 2.5 %raw_rows.3 = (bf16[16,2520,256]{2,1,0:T(8,128)(2,1)}, bf16[2,2520,256]{2,1,0:T(8,128)(2,1)S(1)}) custom-call(s32[21]{0:T(128)S(1)} %concatenate.15.meta, bf16[1,4,480,128]{3,2,1,0:T(8,128)(2,1)S(1)} %get-tuple-element.60.refs_0_, bf16[1,4,480,128]{3,2,1,0:T(8,128)(2,1)S(1)} %collective-permute-done.18.refs_6_.refs_1_, ...), custom_call_target="tpu_custom_call", output_to_operand_aliasing={{0}: (8, {})} | custom-call | flops 10000001024 | bytes 1000 | tf_op jit(solution)/shard_map/raw_rows/pallas_call | solution.py:417
  92.3 0.9 collective-permute-done.31.refs_1_
  93.6 2.2 %came_rows.3 = (bf16[16,2520,256]{2,1,0:T(8,128)(2,1)}, bf16[2,2520,256]{2,1,0:T(8,128)(2,1)S(1)}, bf16[2,2520,256]{2,1,0:T(8,128)(2,1)S(1)}) custom-call(s32[21]{0:T(128)S(1)} %concatenate.15.meta, bf16[1,600,128]{2,1,0:T(8,128)(2,1)S(1)} %get-tuple-element.79.refs_0_, ...), custom_call_target="tpu_custom_call", output_to_operand_aliasing={{0}: (7, {}), {1}: (8, {}), {2}: (9, {})} | custom-call | flops 1000 | bytes 1000 | tf_op jit(solution)/shard_map/came_rows/pallas_call | solution.py:439
  (49 shorter events, 6.9 us)
Async XLA Ops:
  1.2 7.0 %collective-permute-start.2 = (bf16[1,4,480,128]{3,2,1,0:T(8,128)(2,1)S(1)}, bf16[1,4,480,128]{3,2,1,0:T(8,128)(2,1)S(1)}, u32[]{:S(2)}, u32[]{:S(2)}) collective-permute-start(bf16[1,4,480,128]{3,2,1,0:T(8,128)(2,1)S(1)} %get-tuple-element.88.refs_0_), channel_id=1, source_target_pairs={{0,2},{2,0},{4,6},{6,4},{8,10},{10,8},{12,14},{14,12},{16,18},{18,... | collective-permute-start | bytes 1474568 | tf_op jit(solution)/shard_map/ppermute | solution.py:486
  1.8 9.4 %collective-permute-start = (bf16[1,4,480,128]{3,2,1,0:T(8,128)(2,1)S(1)}, bf16[1,4,480,128]{3,2,1,0:T(8,128)(2,1)S(1)}, u32[]{:S(2)}, u32[]{:S(2)}) collective-permute-start(bf16[1,4,480,128]{3,2,1,0:T(8,128)(2,1)S(1)} %get-tuple-element.88.refs_0_), channel_id=1, source_target_pairs={{0,8},{8,16},{16,24},{24,28},{28,20},{20,12},{12,4},{4,0},{2,6},{1... | collective-permute-start | bytes 1474568 | tf_op jit(solution)/shard_map/ppermute | solution.py:486
  4.4 13.9 %collective-permute-start.7 = (bf16[1,4,480,128]{3,2,1,0:T(8,128)(2,1)S(1)}, bf16[1,4,480,128]{3,2,1,0:T(8,128)(2,1)S(1)}, u32[]{:S(2)}, u32[]{:S(2)}) collective-permute-start(bf16[1,4,480,128]{3,2,1,0:T(8,128)(2,1)S(1)} %get-tuple-element.87.refs_0_), channel_id=1, source_target_pairs={{0,1},{1,0},{2,3},{3,2},{4,5},{5,4},{6,7},{7,6},{8,9},{9,8},{10,11... | collective-permute-start | bytes 1474568 | tf_op jit(solution)/shard_map/ppermute | solution.py:477
  6.8 14.2 %collective-permute-start.14 = (bf16[256,128]{0,1:T(8,128)(2,1)S(1)}, bf16[256,128]{0,1:T(8,128)(2,1)S(1)}, u32[]{:S(2)}, u32[]{:S(2)}) collective-permute-start(bf16[256,128]{0,1:T(8,128)(2,1)S(1)} %copy.27), channel_id=1, source_target_pairs={{0,1},{1,0},{2,3},{3,2},{4,5},{5,4},{6,7},{7,6},{8,9},{9,8},{10,11... | collective-permute-start | bytes 196616 | tf_op jit(solution)/shard_map/ppermute | solution.py:478
  8.2 10.1 %collective-permute-start.3 = (bf16[1,4,480,128]{3,2,1,0:T(8,128)(2,1)S(1)}, bf16[1,4,480,128]{3,2,1,0:T(8,128)(2,1)S(1)}, u32[]{:S(2)}, u32[]{:S(2)}) collective-permute-start(bf16[1,4,480,128]{3,2,1,0:T(8,128)(2,1)S(1)} %collective-permute-done.2), channel_id=1, source_target_pairs={{0,8},{8,16},{16,24},{24,28},{28,20},{20,12},{12,4},{4,0},{2,6},{1... | collective-permute-start | bytes 1474568 | tf_op jit(solution)/shard_map/ppermute | solution.py:486
  11.2 11.7 %collective-permute-start.1 = (bf16[1,4,480,128]{3,2,1,0:T(8,128)(2,1)S(1)}, bf16[1,4,480,128]{3,2,1,0:T(8,128)(2,1)S(1)}, u32[]{:S(2)}, u32[]{:S(2)}) collective-permute-start(bf16[1,4,480,128]{3,2,1,0:T(8,128)(2,1)S(1)} %collective-permute-done.refs_0_), channel_id=1, source_target_pairs={{0,8},{8,16},{16,24},{24,28},{28,20},{20,12},{12,4},{4,0},{2,6},{1... | collective-permute-start | bytes 1474568 | tf_op jit(solution)/shard_map/ppermute | solution.py:486
  18.3 2.8 %collective-permute-start.8 = (bf16[1,4,480,128]{3,2,1,0:T(8,128)(2,1)S(1)}, bf16[1,4,480,128]{3,2,1,0:T(8,128)(2,1)S(1)}, u32[]{:S(2)}, u32[]{:S(2)}) collective-permute-start(bf16[1,4,480,128]{3,2,1,0:T(8,128)(2,1)S(1)} %collective-permute-done.7.refs_1_), channel_id=1, source_target_pairs={{0,2},{2,0},{4,6},{6,4},{8,10},{10,8},{12,14},{14,12},{16,18},{18,... | collective-permute-start | bytes 1474568 | tf_op jit(solution)/shard_map/ppermute | solution.py:486
  18.3 10.7 %collective-permute-start.4 = (bf16[1,4,480,128]{3,2,1,0:T(8,128)(2,1)S(1)}, bf16[1,4,480,128]{3,2,1,0:T(8,128)(2,1)S(1)}, u32[]{:S(2)}, u32[]{:S(2)}) collective-permute-start(bf16[1,4,480,128]{3,2,1,0:T(8,128)(2,1)S(1)} %collective-permute-done.3.refs_1_), channel_id=1, source_target_pairs={{0,8},{8,16},{16,24},{24,28},{28,20},{20,12},{12,4},{4,0},{2,6},{1... | collective-permute-start | bytes 1474568 | tf_op jit(solution)/shard_map/ppermute | solution.py:486
  19.5 9.6 %collective-permute-start.11 = (bf16[2,600,128]{2,1,0:T(8,128)(2,1)S(1)}, bf16[2,600,128]{2,1,0:T(8,128)(2,1)S(1)}, u32[]{:S(2)}, u32[]{:S(2)}) collective-permute-start(bf16[2,600,128]{2,1,0:T(8,128)(2,1)S(1)} %get-tuple-element.48), channel_id=1, source_target_pairs={{0,1},{1,0},{2,3},{3,2},{4,5},{5,4},{6,7},{7,6},{8,9},{9,8},{10,11... | collective-permute-start | bytes 921608 | tf_op jit(solution)/shard_map/ppermute | solution.py:512
  21.0 10.9 %collective-permute-start.15 = (bf16[256,256]{1,0:T(8,128)(2,1)S(1)}, bf16[256,256]{1,0:T(8,128)(2,1)S(1)}, u32[]{:S(2)}, u32[]{:S(2)}) collective-permute-start(bf16[256,256]{1,0:T(8,128)(2,1)S(1)} %pad_maximum_fusion.3.refs_4_), channel_id=1, source_target_pairs={{0,2},{2,0},{4,6},{6,4},{8,10},{10,8},{12,14},{14,12},{16,18},{18,... | collective-permute-start | bytes 393224 | tf_op jit(solution)/shard_map/ppermute | solution.py:481
  21.2 18.9 %collective-permute-start.9 = (bf16[2,4,480,128]{3,2,1,0:T(8,128)(2,1)S(1)}, bf16[2,4,480,128]{3,2,1,0:T(8,128)(2,1)S(1)}, u32[]{:S(2)}, u32[]{:S(2)}) collective-permute-start(bf16[2,4,480,128]{3,2,1,0:T(8,128)(2,1)S(1)} %pad_maximum_fusion.1), channel_id=1, source_target_pairs={{0,8},{8,16},{16,24},{24,28},{28,20},{20,12},{12,4},{4,0},{2,6},{1... | collective-permute-start | bytes 2949128 | tf_op jit(solution)/shard_map/ppermute | solution.py:486
  29.8 10.3 %collective-permute-start.12 = (bf16[2,600,128]{2,1,0:T(8,128)(2,1)S(1)}, bf16[2,600,128]{2,1,0:T(8,128)(2,1)S(1)}, u32[]{:S(2)}, u32[]{:S(2)}) collective-permute-start(bf16[2,600,128]{2,1,0:T(8,128)(2,1)S(1)} %get-tuple-element.50), channel_id=1, source_target_pairs={{0,1},{1,0},{2,3},{3,2},{4,5},{5,4},{6,7},{7,6},{8,9},{9,8},{10,11... | collective-permute-start | bytes 921608 | tf_op jit(solution)/shard_map/ppermute | solution.py:512
  31.1 11.7 %collective-permute-start.16 = (bf16[1,600,128]{2,1,0:T(8,128)(2,1)S(1)}, bf16[1,600,128]{2,1,0:T(8,128)(2,1)S(1)}, u32[]{:S(2)}, u32[]{:S(2)}) collective-permute-start(bf16[1,600,128]{2,1,0:T(8,128)(2,1)S(1)} %get-tuple-element.53), channel_id=1, source_target_pairs={{0,1},{1,0},{2,3},{3,2},{4,5},{5,4},{6,7},{7,6},{8,9},{9,8},{10,11... | collective-permute-start | bytes 460808 | tf_op jit(solution)/shard_map/ppermute | solution.py:512
  32.0 16.7 %collective-permute-start.5 = (bf16[2,4,480,128]{3,2,1,0:T(8,128)(2,1)S(1)}, bf16[2,4,480,128]{3,2,1,0:T(8,128)(2,1)S(1)}, u32[]{:S(2)}, u32[]{:S(2)}) collective-permute-start(bf16[2,4,480,128]{3,2,1,0:T(8,128)(2,1)S(1)} %pad_maximum_fusion), channel_id=1, source_target_pairs={{0,8},{8,16},{16,24},{24,28},{28,20},{20,12},{12,4},{4,0},{2,6},{1... | collective-permute-start | bytes 2949128 | tf_op jit(solution)/shard_map/ppermute | solution.py:486
  40.9 7.6 %collective-permute-start.13 = (bf16[2,600,128]{2,1,0:T(8,128)(2,1)S(1)}, bf16[2,600,128]{2,1,0:T(8,128)(2,1)S(1)}, u32[]{:S(2)}, u32[]{:S(2)}) collective-permute-start(bf16[2,600,128]{2,1,0:T(8,128)(2,1)S(1)} %get-tuple-element.51), channel_id=1, source_target_pairs={{0,1},{1,0},{2,3},{3,2},{4,5},{5,4},{6,7},{7,6},{8,9},{9,8},{10,11... | collective-permute-start | bytes 921608 | tf_op jit(solution)/shard_map/ppermute | solution.py:512
  45.2 26.6 %collective-permute-start.24 = (bf16[1,2520,256]{2,1,0:T(8,128)(2,1)S(1)}, bf16[1,2520,256]{2,1,0:T(8,128)(2,1)S(1)}, u32[]{:S(2)}, u32[]{:S(2)}) collective-permute-start(bf16[1,2520,256]{2,1,0:T(8,128)(2,1)S(1)} %get-tuple-element.63), channel_id=1, source_target_pairs={{0,2},{2,0},{4,6},{6,4},{8,10},{10,8},{12,14},{14,12},{16,18},{18,... | collective-permute-start | bytes 3870728 | tf_op jit(solution)/shard_map/ppermute | solution.py:486
  45.3 14.1 %collective-permute-start.10 = (bf16[2,4,480,128]{3,2,1,0:T(8,128)(2,1)S(1)}, bf16[2,4,480,128]{3,2,1,0:T(8,128)(2,1)S(1)}, u32[]{:S(2)}, u32[]{:S(2)}) collective-permute-start(bf16[2,4,480,128]{3,2,1,0:T(8,128)(2,1)S(1)} %collective-permute-done.9.refs_0_.refs_2_), channel_id=1, source_target_pairs={{0,8},{8,16},{16,24},{24,28},{28,20},{20,12},{12,4},{4,0},{2,6},{1... | collective-permute-start | bytes 2949128 | tf_op jit(solution)/shard_map/ppermute | solution.py:486
  49.5 8.5 %collective-permute-start.17 = (bf16[2,600,128]{2,1,0:T(8,128)(2,1)S(1)}, bf16[2,600,128]{2,1,0:T(8,128)(2,1)S(1)}, u32[]{:S(2)}, u32[]{:S(2)}) collective-permute-start(bf16[2,600,128]{2,1,0:T(8,128)(2,1)S(1)} %get-tuple-element.58), channel_id=1, source_target_pairs={{0,1},{1,0},{2,3},{3,2},{4,5},{5,4},{6,7},{7,6},{8,9},{9,8},{10,11... | collective-permute-start | bytes 921608 | tf_op jit(solution)/shard_map/ppermute | solution.py:512
  50.8 13.9 %collective-permute-start.6 = (bf16[1,4,480,128]{3,2,1,0:T(8,128)(2,1)S(1)}, bf16[1,4,480,128]{3,2,1,0:T(8,128)(2,1)S(1)}, u32[]{:S(2)}, u32[]{:S(2)}) collective-permute-start(bf16[1,4,480,128]{3,2,1,0:T(8,128)(2,1)S(1)} %slice.12), channel_id=1, source_target_pairs={{0,8},{8,16},{16,24},{24,28},{28,20},{20,12},{12,4},{4,0},{2,6},{1... | collective-permute-start | bytes 1474568 | tf_op jit(solution)/shard_map/ppermute | solution.py:486
  55.8 22.1 %collective-permute-start.22 = (bf16[2,2520,256]{2,1,0:T(8,128)(2,1)S(1)}, bf16[2,2520,256]{2,1,0:T(8,128)(2,1)S(1)}, u32[]{:S(2)}, u32[]{:S(2)}) collective-permute-start(bf16[2,2520,256]{2,1,0:T(8,128)(2,1)S(1)} %get-tuple-element.61), channel_id=1, source_target_pairs={{0,2},{2,0},{4,6},{6,4},{8,10},{10,8},{12,14},{14,12},{16,18},{18,... | collective-permute-start | bytes 7741448 | tf_op jit(solution)/shard_map/ppermute | solution.py:486
  60.2 8.8 %collective-permute-start.23 = (bf16[2,600,128]{2,1,0:T(8,128)(2,1)S(1)}, bf16[2,600,128]{2,1,0:T(8,128)(2,1)S(1)}, u32[]{:S(2)}, u32[]{:S(2)}) collective-permute-start(bf16[2,600,128]{2,1,0:T(8,128)(2,1)S(1)} %get-tuple-element.62), channel_id=1, source_target_pairs={{0,1},{1,0},{2,3},{3,2},{4,5},{5,4},{6,7},{7,6},{8,9},{9,8},{10,11... | collective-permute-start | bytes 921608 | tf_op jit(solution)/shard_map/ppermute | solution.py:512
  61.4 8.9 %collective-permute-start.19 = (bf16[1,4,480,128]{3,2,1,0:T(8,128)(2,1)S(1)}, bf16[1,4,480,128]{3,2,1,0:T(8,128)(2,1)S(1)}, u32[]{:S(2)}, u32[]{:S(2)}) collective-permute-start(bf16[1,4,480,128]{3,2,1,0:T(8,128)(2,1)S(1)} %get-tuple-element.86), channel_id=1, source_target_pairs={{0,8},{8,16},{16,24},{24,28},{28,20},{20,12},{12,4},{4,0},{2,6},{1... | collective-permute-start | bytes 1474568 | tf_op jit(solution)/shard_map/ppermute | solution.py:486
  64.7 11.2 %collective-permute-start.21 = (bf16[1,4,480,128]{3,2,1,0:T(8,128)(2,1)S(1)}, bf16[1,4,480,128]{3,2,1,0:T(8,128)(2,1)S(1)}, u32[]{:S(2)}, u32[]{:S(2)}) collective-permute-start(bf16[1,4,480,128]{3,2,1,0:T(8,128)(2,1)S(1)} %get-tuple-element.85), channel_id=1, source_target_pairs={{0,8},{8,16},{16,24},{24,28},{28,20},{20,12},{12,4},{4,0},{2,6},{1... | collective-permute-start | bytes 1474568 | tf_op jit(solution)/shard_map/ppermute | solution.py:486
  69.1 6.4 %collective-permute-start.25 = (bf16[1,600,128]{2,1,0:T(8,128)(2,1)S(1)}, bf16[1,600,128]{2,1,0:T(8,128)(2,1)S(1)}, u32[]{:S(2)}, u32[]{:S(2)}) collective-permute-start(bf16[1,600,128]{2,1,0:T(8,128)(2,1)S(1)} %get-tuple-element.66), channel_id=1, source_target_pairs={{0,1},{1,0},{2,3},{3,2},{4,5},{5,4},{6,7},{7,6},{8,9},{9,8},{10,11... | collective-permute-start | bytes 460808 | tf_op jit(solution)/shard_map/ppermute | solution.py:550
  70.3 10.5 %collective-permute-start.20 = (bf16[1,4,480,128]{3,2,1,0:T(8,128)(2,1)S(1)}, bf16[1,4,480,128]{3,2,1,0:T(8,128)(2,1)S(1)}, u32[]{:S(2)}, u32[]{:S(2)}) collective-permute-start(bf16[1,4,480,128]{3,2,1,0:T(8,128)(2,1)S(1)} %collective-permute-done.19.refs_0_.refs_1_), channel_id=1, source_target_pairs={{0,8},{8,16},{16,24},{24,28},{28,20},{20,12},{12,4},{4,0},{2,6},{1... | collective-permute-start | bytes 1474568 | tf_op jit(solution)/shard_map/ppermute | solution.py:486
  75.4 11.6 %collective-permute-start.28 = (bf16[2,2520,256]{2,1,0:T(8,128)(2,1)S(1)}, bf16[2,2520,256]{2,1,0:T(8,128)(2,1)S(1)}, u32[]{:S(2)}, u32[]{:S(2)}) collective-permute-start(bf16[2,2520,256]{2,1,0:T(8,128)(2,1)S(1)} %get-tuple-element.73), channel_id=1, source_target_pairs={{0,2},{2,0},{4,6},{6,4},{8,10},{10,8},{12,14},{14,12},{16,18},{18,... | collective-permute-start | bytes 7741448 | tf_op jit(solution)/shard_map/ppermute | solution.py:486
  75.5 6.5 %collective-permute-start.18 = (bf16[1,4,480,128]{3,2,1,0:T(8,128)(2,1)S(1)}, bf16[1,4,480,128]{3,2,1,0:T(8,128)(2,1)S(1)}, u32[]{:S(2)}, u32[]{:S(2)}) collective-permute-start(bf16[1,4,480,128]{3,2,1,0:T(8,128)(2,1)S(1)} %get-tuple-element.60.refs_0_), channel_id=1, source_target_pairs={{0,2},{2,0},{4,6},{6,4},{8,10},{10,8},{12,14},{14,12},{16,18},{18,... | collective-permute-start | bytes 1474568 | tf_op jit(solution)/shard_map/ppermute | solution.py:486
  76.8 10.2 %collective-permute-start.27 = (bf16[2,600,128]{2,1,0:T(8,128)(2,1)S(1)}, bf16[2,600,128]{2,1,0:T(8,128)(2,1)S(1)}, u32[]{:S(2)}, u32[]{:S(2)}) collective-permute-start(bf16[2,600,128]{2,1,0:T(8,128)(2,1)S(1)} %get-tuple-element.70), channel_id=1, source_target_pairs={{0,1},{1,0},{2,3},{3,2},{4,5},{5,4},{6,7},{7,6},{8,9},{9,8},{10,11... | collective-permute-start | bytes 921608 | tf_op jit(solution)/shard_map/ppermute | solution.py:569
  80.7 8.4 %collective-permute-start.29 = (bf16[2,2520,256]{2,1,0:T(8,128)(2,1)S(1)}, bf16[2,2520,256]{2,1,0:T(8,128)(2,1)S(1)}, u32[]{:S(2)}, u32[]{:S(2)}) collective-permute-start(bf16[2,2520,256]{2,1,0:T(8,128)(2,1)S(1)} %get-tuple-element.75), channel_id=1, source_target_pairs={{0,2},{2,0},{4,6},{6,4},{8,10},{10,8},{12,14},{14,12},{16,18},{18,... | collective-permute-start | bytes 7741448 | tf_op jit(solution)/shard_map/ppermute | solution.py:486
  81.5 7.6 %collective-permute-start.26 = (bf16[1,4,480,128]{3,2,1,0:T(8,128)(2,1)S(1)}, bf16[1,4,480,128]{3,2,1,0:T(8,128)(2,1)S(1)}, u32[]{:S(2)}, u32[]{:S(2)}) collective-permute-start(bf16[1,4,480,128]{3,2,1,0:T(8,128)(2,1)S(1)} %get-tuple-element.69.refs_2_), channel_id=1, source_target_pairs={{0,2},{2,0},{4,6},{6,4},{8,10},{10,8},{12,14},{14,12},{16,18},{18,... | collective-permute-start | bytes 1474568 | tf_op jit(solution)/shard_map/ppermute | solution.py:486
  82.0 9.7 %collective-permute-start.30 = (bf16[1,600,128]{2,1,0:T(8,128)(2,1)S(1)}, bf16[1,600,128]{2,1,0:T(8,128)(2,1)S(1)}, u32[]{:S(2)}, u32[]{:S(2)}) collective-permute-start(bf16[1,600,128]{2,1,0:T(8,128)(2,1)S(1)} %get-tuple-element.78), channel_id=1, source_target_pairs={{0,1},{1,0},{2,3},{3,2},{4,5},{5,4},{6,7},{7,6},{8,9},{9,8},{10,11... | collective-permute-start | bytes 460808 | tf_op jit(solution)/shard_map/ppermute | solution.py:550
  89.0 3.3 %collective-permute-start.33 = (bf16[2,600,256]{2,1,0:T(8,128)(2,1)S(1)}, bf16[2,600,256]{2,1,0:T(8,128)(2,1)S(1)}, u32[]{:S(2)}, u32[]{:S(2)}) collective-permute-start(bf16[2,600,256]{2,1,0:T(8,128)(2,1)S(1)} %get-tuple-element.81), channel_id=1, source_target_pairs={{0,2},{2,0},{4,6},{6,4},{8,10},{10,8},{12,14},{14,12},{16,18},{18,... | collective-permute-start | bytes 1843208 | tf_op jit(solution)/shard_map/ppermute | solution.py:486
  91.7 1.6 %collective-permute-start.31 = (bf16[1,600,128]{2,1,0:T(8,128)(2,1)S(1)}, bf16[1,600,128]{2,1,0:T(8,128)(2,1)S(1)}, u32[]{:S(2)}, u32[]{:S(2)}) collective-permute-start(bf16[1,600,128]{2,1,0:T(8,128)(2,1)S(1)} %get-tuple-element.79.refs_0_), channel_id=1, source_target_pairs={{0,2},{2,0},{4,6},{6,4},{8,10},{10,8},{12,14},{14,12},{16,18},{18,... | collective-permute-start | bytes 460808 | tf_op jit(solution)/shard_map/ppermute | solution.py:486
  92.2 1.4 %collective-permute-start.32 = (bf16[1,600,128]{2,1,0:T(8,128)(2,1)S(1)}, bf16[1,600,128]{2,1,0:T(8,128)(2,1)S(1)}, u32[]{:S(2)}, u32[]{:S(2)}) collective-permute-start(bf16[1,600,128]{2,1,0:T(8,128)(2,1)S(1)} %get-tuple-element.80.refs_2_), channel_id=1, source_target_pairs={{0,2},{2,0},{4,6},{6,4},{8,10},{10,8},{12,14},{14,12},{16,18},{18,... | collective-permute-start | bytes 460808 | tf_op jit(solution)/shard_map/ppermute | solution.py:486

commit v5 on v4

--- a/solution.py
+++ b/solution.py
@@ -168,6 +168,15 @@
                 store(index, at * step, joined(run))
 
         copies.append(pltpu.make_async_copy(done.at[index], out.at[meta[slots[index]]], sems.at[index]))
+        copies[-1].start()
+    for copy in copies:
+        copy.wait()
+
+
+def land_kernel(slots, meta, strips, _, out, sems):
+    copies = []
+    for index, slot in enumerate(slots):
+        copies.append(pltpu.make_async_copy(strips.at[index], out.at[meta[slot]], sems.at[index]))
         copies[-1].start()
     for copy in copies:
         copy.wait()
@@ -574,8 +583,19 @@
 
     slots = slots_of(near, 1) + slots_of(far, 0) + slots_of(far, 1)
 
-    landing_now, landed_now = landing(far) if G("LC") else ((), None)
-    pins = ((landed_now,) if landing_now else ()) + pins
+    landing_now, landed_now = landing(far)
+    out = pl.pallas_call(
+        functools.partial(land_kernel, landing_now),
+        out_shape=out_type,
+        in_specs=[scalars, anywhere, anywhere],
+        out_specs=anywhere,
+        scratch_shapes=[pltpu.SemaphoreType.DMA((len(landing_now),))],
+        input_output_aliases={2: 0},
+        compiler_params=params,
+        cost_estimate=modelled(0),
+        name="land",
+    )(meta, landed_now, out)
+    landing_now = ()
     out, near_done, near_rows = came_rows(
         out, near_done, (), across_came[near, 0], across_came[near, 1], True, cost=G("F2"), pins=pins, landing=landing_now
     )

time: 96.2 us -> 95.4 us (level)
  waiting for transfers between devices: 34.5 us -> 32.4 us
  Pallas kernels: 26.1 us -> 27.3 us
    ppermute x1, waiting for transfers between devices: 3.72 us -> 1.67 us  [ring_local(): across_came[near, 0].append(lax.ppermute(extra, 'chan', across))]
    pallas_call x0 -> x1, Pallas kernels: none -> 2.03 us  [ring_local(): pl.pallas_call(functools.partial(land_kernel, landing_now), out_shape=out...]
  transfers between devices with their start and end apart: 34 -> 34, of which waited for: 16 -> 16; matrix products, arithmetic and copies ran while one was open for 1% -> 1% of each run, Pallas kernels for 25% -> 26%
where the time goes in v5:
time: 95.4 us; the launch traced here: 95.2 us
  starting transfers between devices  32.4 us (34%)
  waiting for transfers between devices  32.4 us (34%)
  Pallas kernels  27.3 us (29%)
  local copies, waits for them, and re-layouts  2.36 us (2%)
    ppermute x22, starting transfers between devices, permute_rows(): return [lax.ppermute(piece, 'rows', pairs) for piece in pieces]  19.8 us
    ppermute x6, waiting for transfers between devices, do_extra(): across_came[d, 1 - part].append(lax.ppermute(extra, 'chan', across))  19.7 us
    pallas_call x3, Pallas kernels, correlate(): pl.pallas_call(functools.partial(corr_kernel, factor, tuple((len(part) fo...  9.29 us
    pallas_call x10, Pallas kernels, make_extra(): pl.pallas_call(functools.partial(extra_kernel, len(halves), 2 + len(carri...  7.18 us
    ppermute x6, starting transfers between devices, do_extra(): across_came[d, 1 - part].append(lax.ppermute(extra, 'chan', across))  7.11 us
    ppermute x22, waiting for transfers between devices, permute_rows(): return [lax.ppermute(piece, 'rows', pairs) for piece in pieces]  5.91 us
    pallas_call x2, Pallas kernels, raw_rows(): pl.pallas_call(functools.partial(raw_kernel, factor, (len(own), len(other...  5.31 us
    ppermute x1, waiting for transfers between devices, ring_local(): partner = lax.ppermute(theirs, 'chan', across)  5.11 us
  transfers between devices with their start and end apart: 34, of which 16 were waited for; matrix products, arithmetic and copies ran while one was open for 1% of the time, Pallas kernels for 26%

profile of v5, /device:TPU:0, one launch (start us, length us, event | category | flops | bytes accessed | tf_op | source)
XLA Modules:
  0.0 95.2 jit_solution(11724555044540972520)
XLA Ops:
  0.0 1.2 %dynamic-slice_bitcast_fusion = (bf16[1,4,480,128]{3,2,1,0:T(8,128)(2,1)S(1)}, bf16[1,4,480,128]{3,2,1,0:T(8,128)(2,1)S(1)}) fusion(bf16[8,480,128]{2,1,0:T(8,128)(2,1)} %param.3, s32[]{:T(128)S(6)} %select_n.72, s32[]{:T(128)S(6)} %select_n.71), kind=kLoop, calls=%fused_computation.2 | loop fusion | bytes 1966088 | tf_op jit(solution)/shard_map/broadcast_in_dim | solution.py:478
  1.8 2.6 %collective-permute-start = (bf16[1,4,480,128]{3,2,1,0:T(8,128)(2,1)S(1)}, bf16[1,4,480,128]{3,2,1,0:T(8,128)(2,1)S(1)}, u32[]{:S(2)}, u32[]{:S(2)}) collective-permute-start(bf16[1,4,480,128]{3,2,1,0:T(8,128)(2,1)S(1)} %get-tuple-element.88.refs_0_), channel_id=1, source_target_pairs={{0,8},{8,16},{16,24},{24,28},{28,20},{20,12},{12,4},{4,0},{2,6},{1... | collective-permute-start | bytes 1474568 | tf_op jit(solution)/shard_map/ppermute | solution.py:495
  4.4 1.5 %collective-permute-start.7 = (bf16[1,4,480,128]{3,2,1,0:T(8,128)(2,1)S(1)}, bf16[1,4,480,128]{3,2,1,0:T(8,128)(2,1)S(1)}, u32[]{:S(2)}, u32[]{:S(2)}) collective-permute-start(bf16[1,4,480,128]{3,2,1,0:T(8,128)(2,1)S(1)} %get-tuple-element.87.refs_0_), channel_id=1, source_target_pairs={{0,1},{1,0},{2,3},{3,2},{4,5},{5,4},{6,7},{7,6},{8,9},{9,8},{10,11... | collective-permute-start | bytes 1474568 | tf_op jit(solution)/shard_map/ppermute | solution.py:486
  5.9 0.9 copy.28
  8.2 1.6 %collective-permute-start.3 = (bf16[1,4,480,128]{3,2,1,0:T(8,128)(2,1)S(1)}, bf16[1,4,480,128]{3,2,1,0:T(8,128)(2,1)S(1)}, u32[]{:S(2)}, u32[]{:S(2)}) collective-permute-start(bf16[1,4,480,128]{3,2,1,0:T(8,128)(2,1)S(1)} %collective-permute-done.2), channel_id=1, source_target_pairs={{0,8},{8,16},{16,24},{24,28},{28,20},{20,12},{12,4},{4,0},{2,6},{1... | collective-permute-start | bytes 1474568 | tf_op jit(solution)/shard_map/ppermute | solution.py:495
  10.5 0.7 collective-permute-done.refs_0_
  11.2 2.1 %collective-permute-start.1 = (bf16[1,4,480,128]{3,2,1,0:T(8,128)(2,1)S(1)}, bf16[1,4,480,128]{3,2,1,0:T(8,128)(2,1)S(1)}, u32[]{:S(2)}, u32[]{:S(2)}) collective-permute-start(bf16[1,4,480,128]{3,2,1,0:T(8,128)(2,1)S(1)} %collective-permute-done.refs_0_), channel_id=1, source_target_pairs={{0,8},{8,16},{16,24},{24,28},{28,20},{20,12},{12,4},{4,0},{2,6},{1... | collective-permute-start | bytes 1474568 | tf_op jit(solution)/shard_map/ppermute | solution.py:495
  13.2 5.1 %collective-permute-done.7.refs_1_ = bf16[1,4,480,128]{3,2,1,0:T(8,128)(2,1)S(1)} collective-permute-done((bf16[1,4,480,128]{3,2,1,0:T(8,128)(2,1)S(1)}, bf16[1,4,480,128]{3,2,1,0:T(8,128)(2,1)S(1)}, u32[]{:S(2)}, u32[]{:S(2)}) %collective-permute-start.7) | collective-permute-done | bytes 491552 | tf_op jit(solution)/shard_map/ppermute | solution.py:486
  18.7 0.8 extra.12
  19.5 1.5 %collective-permute-start.11 = (bf16[2,600,128]{2,1,0:T(8,128)(2,1)S(1)}, bf16[2,600,128]{2,1,0:T(8,128)(2,1)S(1)}, u32[]{:S(2)}, u32[]{:S(2)}) collective-permute-start(bf16[2,600,128]{2,1,0:T(8,128)(2,1)S(1)} %get-tuple-element.48), channel_id=1, source_target_pairs={{0,1},{1,0},{2,3},{3,2},{4,5},{5,4},{6,7},{7,6},{8,9},{9,8},{10,11... | collective-permute-start | bytes 921608 | tf_op jit(solution)/shard_map/ppermute | solution.py:521
  21.2 1.6 %collective-permute-start.9 = (bf16[2,4,480,128]{3,2,1,0:T(8,128)(2,1)S(1)}, bf16[2,4,480,128]{3,2,1,0:T(8,128)(2,1)S(1)}, u32[]{:S(2)}, u32[]{:S(2)}) collective-permute-start(bf16[2,4,480,128]{3,2,1,0:T(8,128)(2,1)S(1)} %pad_maximum_fusion.1), channel_id=1, source_target_pairs={{0,8},{8,16},{16,24},{24,28},{28,20},{20,12},{12,4},{4,0},{2,6},{1... | collective-permute-start | bytes 2949128 | tf_op jit(solution)/shard_map/ppermute | solution.py:495
  22.9 6.2 %collective-permute-done.11.refs_3_.refs_4_ = bf16[2,600,128]{2,1,0:T(8,128)(2,1)S(1)} collective-permute-done((bf16[2,600,128]{2,1,0:T(8,128)(2,1)S(1)}, bf16[2,600,128]{2,1,0:T(8,128)(2,1)S(1)}, u32[]{:S(2)}, u32[]{:S(2)}) %collective-permute-start.11) | collective-permute-done | bytes 307232 | tf_op jit(solution)/shard_map/ppermute | solution.py:521
  29.0 0.8 extra.13
  29.8 1.3 %collective-permute-start.12 = (bf16[2,600,128]{2,1,0:T(8,128)(2,1)S(1)}, bf16[2,600,128]{2,1,0:T(8,128)(2,1)S(1)}, u32[]{:S(2)}, u32[]{:S(2)}) collective-permute-start(bf16[2,600,128]{2,1,0:T(8,128)(2,1)S(1)} %get-tuple-element.50), channel_id=1, source_target_pairs={{0,1},{1,0},{2,3},{3,2},{4,5},{5,4},{6,7},{7,6},{8,9},{9,8},{10,11... | collective-permute-start | bytes 921608 | tf_op jit(solution)/shard_map/ppermute | solution.py:521
  31.1 0.8 collective-permute-start.16
  32.0 1.6 %collective-permute-start.5 = (bf16[2,4,480,128]{3,2,1,0:T(8,128)(2,1)S(1)}, bf16[2,4,480,128]{3,2,1,0:T(8,128)(2,1)S(1)}, u32[]{:S(2)}, u32[]{:S(2)}) collective-permute-start(bf16[2,4,480,128]{3,2,1,0:T(8,128)(2,1)S(1)} %pad_maximum_fusion), channel_id=1, source_target_pairs={{0,8},{8,16},{16,24},{24,28},{28,20},{20,12},{12,4},{4,0},{2,6},{1... | collective-permute-start | bytes 2949128 | tf_op jit(solution)/shard_map/ppermute | solution.py:495
  33.7 6.4 %collective-permute-done.12.refs_2_.refs_4_ = bf16[2,600,128]{2,1,0:T(8,128)(2,1)S(1)} collective-permute-done((bf16[2,600,128]{2,1,0:T(8,128)(2,1)S(1)}, bf16[2,600,128]{2,1,0:T(8,128)(2,1)S(1)}, u32[]{:S(2)}, u32[]{:S(2)}) %collective-permute-start.12) | collective-permute-done | bytes 307232 | tf_op jit(solution)/shard_map/ppermute | solution.py:521
  40.1 0.8 extra.14
  40.9 1.1 %collective-permute-start.13 = (bf16[2,600,128]{2,1,0:T(8,128)(2,1)S(1)}, bf16[2,600,128]{2,1,0:T(8,128)(2,1)S(1)}, u32[]{:S(2)}, u32[]{:S(2)}) collective-permute-start(bf16[2,600,128]{2,1,0:T(8,128)(2,1)S(1)} %get-tuple-element.51), channel_id=1, source_target_pairs={{0,1},{1,0},{2,3},{3,2},{4,5},{5,4},{6,7},{7,6},{8,9},{9,8},{10,11... | collective-permute-start | bytes 921608 | tf_op jit(solution)/shard_map/ppermute | solution.py:521
  42.0 0.8 collective-permute-done.16.refs_3_
  42.8 2.5 %correlate.3 = (bf16[16,2520,256]{2,1,0:T(8,128)(2,1)}, bf16[1,2520,256]{2,1,0:T(8,128)(2,1)S(1)}) custom-call(s32[21]{0:T(128)S(1)} %concatenate.15.meta, bf16[1,4,480,128]{3,2,1,0:T(8,128)(2,1)S(1)} %get-tuple-element.88.refs_0_, bf16[1,4,480,128]{3,2,1,0:T(8,128)(2,1)S(1)} %collective-permute-done.7.refs_1_, ...), custom_call_target="tpu_custom_call", output_to_operand_aliasing={{0}: (6, {})} | custom-call | flops 10000001024 | bytes 1000 | tf_op jit(solution)/shard_map/correlate/pallas_call | solution.py:400
  45.3 1.2 %collective-permute-start.10 = (bf16[2,4,480,128]{3,2,1,0:T(8,128)(2,1)S(1)}, bf16[2,4,480,128]{3,2,1,0:T(8,128)(2,1)S(1)}, u32[]{:S(2)}, u32[]{:S(2)}) collective-permute-start(bf16[2,4,480,128]{3,2,1,0:T(8,128)(2,1)S(1)} %collective-permute-done.9.refs_0_.refs_2_), channel_id=1, source_target_pairs={{0,8},{8,16},{16,24},{24,28},{28,20},{20,12},{12,4},{4,0},{2,6},{1... | collective-permute-start | bytes 2949128 | tf_op jit(solution)/shard_map/ppermute | solution.py:495
  46.5 1.9 %collective-permute-done.13.refs_2_.refs_3_ = bf16[2,600,128]{2,1,0:T(8,128)(2,1)S(1)} collective-permute-done((bf16[2,600,128]{2,1,0:T(8,128)(2,1)S(1)}, bf16[2,600,128]{2,1,0:T(8,128)(2,1)S(1)}, u32[]{:S(2)}, u32[]{:S(2)}) %collective-permute-start.13) | collective-permute-done | bytes 307232 | tf_op jit(solution)/shard_map/ppermute | solution.py:521
  48.7 0.8 extra.15
  49.5 1.3 %collective-permute-start.17 = (bf16[2,600,128]{2,1,0:T(8,128)(2,1)S(1)}, bf16[2,600,128]{2,1,0:T(8,128)(2,1)S(1)}, u32[]{:S(2)}, u32[]{:S(2)}) collective-permute-start(bf16[2,600,128]{2,1,0:T(8,128)(2,1)S(1)} %get-tuple-element.58), channel_id=1, source_target_pairs={{0,1},{1,0},{2,3},{3,2},{4,5},{5,4},{6,7},{7,6},{8,9},{9,8},{10,11... | collective-permute-start | bytes 921608 | tf_op jit(solution)/shard_map/ppermute | solution.py:521
  50.8 1.6 %collective-permute-start.6 = (bf16[1,4,480,128]{3,2,1,0:T(8,128)(2,1)S(1)}, bf16[1,4,480,128]{3,2,1,0:T(8,128)(2,1)S(1)}, u32[]{:S(2)}, u32[]{:S(2)}) collective-permute-start(bf16[1,4,480,128]{3,2,1,0:T(8,128)(2,1)S(1)} %slice.12), channel_id=1, source_target_pairs={{0,8},{8,16},{16,24},{24,28},{28,20},{20,12},{12,4},{4,0},{2,6},{1... | collective-permute-start | bytes 1474568 | tf_op jit(solution)/shard_map/ppermute | solution.py:495
  52.5 3.3 %correlate.4 = (bf16[16,2520,256]{2,1,0:T(8,128)(2,1)}, bf16[2,2520,256]{2,1,0:T(8,128)(2,1)S(1)}) custom-call(s32[21]{0:T(128)S(1)} %concatenate.15.meta, bf16[1,4,480,128]{3,2,1,0:T(8,128)(2,1)S(1)} %collective-permute-done.refs_0_, bf16[1,4,480,128]{3,2,1,0:T(8,128)(2,1)S(1)} %collective-permute-done.3.refs_1_, ...), custom_call_target="tpu_custom_call", output_to_operand_aliasing={{0}: (7, {})} | custom-call | flops 10000001024 | bytes 1000 | tf_op jit(solution)/shard_map/correlate/pallas_call | solution.py:400
  55.9 2.1 %collective-permute-done.17.refs_2_.refs_1_ = bf16[2,600,128]{2,1,0:T(8,128)(2,1)S(1)} collective-permute-done((bf16[2,600,128]{2,1,0:T(8,128)(2,1)S(1)}, bf16[2,600,128]{2,1,0:T(8,128)(2,1)S(1)}, u32[]{:S(2)}, u32[]{:S(2)}) %collective-permute-start.17) | collective-permute-done | bytes 307232 | tf_op jit(solution)/shard_map/ppermute | solution.py:521
  58.0 1.5 %collective-permute-done.10.refs_0_.refs_2_ = bf16[2,4,480,128]{3,2,1,0:T(8,128)(2,1)S(1)} collective-permute-done((bf16[2,4,480,128]{3,2,1,0:T(8,128)(2,1)S(1)}, bf16[2,4,480,128]{3,2,1,0:T(8,128)(2,1)S(1)}, u32[]{:S(2)}, u32[]{:S(2)}) %collective-permute-start.10) | collective-permute-done | bytes 983072 | tf_op jit(solution)/shard_map/ppermute | solution.py:495
  59.5 0.8 extra.16
  60.2 1.1 %collective-permute-start.23 = (bf16[2,600,128]{2,1,0:T(8,128)(2,1)S(1)}, bf16[2,600,128]{2,1,0:T(8,128)(2,1)S(1)}, u32[]{:S(2)}, u32[]{:S(2)}) collective-permute-start(bf16[2,600,128]{2,1,0:T(8,128)(2,1)S(1)} %get-tuple-element.62), channel_id=1, source_target_pairs={{0,1},{1,0},{2,3},{3,2},{4,5},{5,4},{6,7},{7,6},{8,9},{9,8},{10,11... | collective-permute-start | bytes 921608 | tf_op jit(solution)/shard_map/ppermute | solution.py:521
  61.4 1.6 %collective-permute-start.19 = (bf16[1,4,480,128]{3,2,1,0:T(8,128)(2,1)S(1)}, bf16[1,4,480,128]{3,2,1,0:T(8,128)(2,1)S(1)}, u32[]{:S(2)}, u32[]{:S(2)}) collective-permute-start(bf16[1,4,480,128]{3,2,1,0:T(8,128)(2,1)S(1)} %get-tuple-element.86), channel_id=1, source_target_pairs={{0,8},{8,16},{16,24},{24,28},{28,20},{20,12},{12,4},{4,0},{2,6},{1... | collective-permute-start | bytes 1474568 | tf_op jit(solution)/shard_map/ppermute | solution.py:495
  63.0 1.7 %collective-permute-done.6.refs_0_ = bf16[1,4,480,128]{3,2,1,0:T(8,128)(2,1)S(1)} collective-permute-done((bf16[1,4,480,128]{3,2,1,0:T(8,128)(2,1)S(1)}, bf16[1,4,480,128]{3,2,1,0:T(8,128)(2,1)S(1)}, u32[]{:S(2)}, u32[]{:S(2)}) %collective-permute-start.6) | collective-permute-done | bytes 491552 | tf_op jit(solution)/shard_map/ppermute | solution.py:495
  64.7 1.4 %collective-permute-start.21 = (bf16[1,4,480,128]{3,2,1,0:T(8,128)(2,1)S(1)}, bf16[1,4,480,128]{3,2,1,0:T(8,128)(2,1)S(1)}, u32[]{:S(2)}, u32[]{:S(2)}) collective-permute-start(bf16[1,4,480,128]{3,2,1,0:T(8,128)(2,1)S(1)} %get-tuple-element.85), channel_id=1, source_target_pairs={{0,8},{8,16},{16,24},{24,28},{28,20},{20,12},{12,4},{4,0},{2,6},{1... | collective-permute-start | bytes 1474568 | tf_op jit(solution)/shard_map/ppermute | solution.py:495
  66.8 2.3 %collective-permute-done.23.refs_3_ = bf16[2,600,128]{2,1,0:T(8,128)(2,1)S(1)} collective-permute-done((bf16[2,600,128]{2,1,0:T(8,128)(2,1)S(1)}, bf16[2,600,128]{2,1,0:T(8,128)(2,1)S(1)}, u32[]{:S(2)}, u32[]{:S(2)}) %collective-permute-start.23) | collective-permute-done | bytes 307232 | tf_op jit(solution)/shard_map/ppermute | solution.py:521
  69.1 0.9 collective-permute-start.25
  70.3 1.6 %collective-permute-start.20 = (bf16[1,4,480,128]{3,2,1,0:T(8,128)(2,1)S(1)}, bf16[1,4,480,128]{3,2,1,0:T(8,128)(2,1)S(1)}, u32[]{:S(2)}, u32[]{:S(2)}) collective-permute-start(bf16[1,4,480,128]{3,2,1,0:T(8,128)(2,1)S(1)} %collective-permute-done.19.refs_0_.refs_1_), channel_id=1, source_target_pairs={{0,8},{8,16},{16,24},{24,28},{28,20},{20,12},{12,4},{4,0},{2,6},{1... | collective-permute-start | bytes 1474568 | tf_op jit(solution)/shard_map/ppermute | solution.py:495
  71.9 3.5 %correlate.5 = (bf16[16,2520,256]{2,1,0:T(8,128)(2,1)}, bf16[2,2520,256]{2,1,0:T(8,128)(2,1)S(1)}) custom-call(s32[21]{0:T(128)S(1)} %concatenate.15.meta, bf16[1,4,480,128]{3,2,1,0:T(8,128)(2,1)S(1)} %collective-permute-done.1.refs_0_, bf16[1,4,480,128]{3,2,1,0:T(8,128)(2,1)S(1)} %collective-permute-done.4.refs_1_, ...), custom_call_target="tpu_custom_call", output_to_operand_aliasing={{0}: (8, {})} | custom-call | flops 3000001024 | bytes 1000 | tf_op jit(solution)/shard_map/correlate/pallas_call | solution.py:400
  76.0 0.8 extra.18
  76.8 1.1 %collective-permute-start.27 = (bf16[2,600,128]{2,1,0:T(8,128)(2,1)S(1)}, bf16[2,600,128]{2,1,0:T(8,128)(2,1)S(1)}, u32[]{:S(2)}, u32[]{:S(2)}) collective-permute-start(bf16[2,600,128]{2,1,0:T(8,128)(2,1)S(1)} %get-tuple-element.70), channel_id=1, source_target_pairs={{0,1},{1,0},{2,3},{3,2},{4,5},{5,4},{6,7},{7,6},{8,9},{9,8},{10,11... | collective-permute-start | bytes 921608 | tf_op jit(solution)/shard_map/ppermute | solution.py:578
  77.9 2.8 %raw_rows.2 = (bf16[16,2520,256]{2,1,0:T(8,128)(2,1)}, bf16[2,2520,256]{2,1,0:T(8,128)(2,1)S(1)}, bf16[2,2520,256]{2,1,0:T(8,128)(2,1)S(1)}) custom-call(s32[21]{0:T(128)S(1)} %concatenate.15.meta, bf16[2,4,480,128]{3,2,1,0:T(8,128)(2,1)S(1)} %collective-permute-done.5.refs_0_, ...), custom_call_target="tpu_custom_call", output_to_operand_aliasing={{0}: (6, {})} | custom-call | flops 1000 | bytes 1000 | tf_op jit(solution)/shard_map/raw_rows/pallas_call | solution.py:426
  82.0 1.3 %collective-permute-start.30 = (bf16[1,600,128]{2,1,0:T(8,128)(2,1)S(1)}, bf16[1,600,128]{2,1,0:T(8,128)(2,1)S(1)}, u32[]{:S(2)}, u32[]{:S(2)}) collective-permute-start(bf16[1,600,128]{2,1,0:T(8,128)(2,1)S(1)} %get-tuple-element.78), channel_id=1, source_target_pairs={{0,1},{1,0},{2,3},{3,2},{4,5},{5,4},{6,7},{7,6},{8,9},{9,8},{10,11... | collective-permute-start | bytes 460808 | tf_op jit(solution)/shard_map/ppermute | solution.py:559
  83.2 2.0 %land.1.refs_3_ = bf16[16,2520,256]{2,1,0:T(8,128)(2,1)} custom-call(s32[21]{0:T(128)S(1)} %concatenate.15.meta, bf16[2,2520,256]{2,1,0:T(8,128)(2,1)S(1)} %collective-permute-done.28.strips, bf16[16,2520,256]{2,1,0:T(8,128)(2,1)} %get-tuple-element.72._), custom_call_target="tpu_custom_call", output_to_operand_aliasing={{}: (2, {})} | custom-call | flops 1000 | bytes 1000 | tf_op jit(solution)/shard_map/land/pallas_call | solution.py:587
  85.3 1.7 %collective-permute-done.27.refs_0_ = bf16[2,600,128]{2,1,0:T(8,128)(2,1)S(1)} collective-permute-done((bf16[2,600,128]{2,1,0:T(8,128)(2,1)S(1)}, bf16[2,600,128]{2,1,0:T(8,128)(2,1)S(1)}, u32[]{:S(2)}, u32[]{:S(2)}) %collective-permute-start.27) | collective-permute-done | bytes 307232 | tf_op jit(solution)/shard_map/ppermute | solution.py:578
  87.0 1.3 %came_rows.2 = (bf16[16,2520,256]{2,1,0:T(8,128)(2,1)}, bf16[2,2520,256]{2,1,0:T(8,128)(2,1)S(1)}, bf16[2,600,256]{2,1,0:T(8,128)(2,1)S(1)}) custom-call(s32[21]{0:T(128)S(1)} %concatenate.15.meta, bf16[2,600,128]{2,1,0:T(8,128)(2,1)S(1)} %collective-permute-done.27.refs_0_, ...), custom_call_target="tpu_custom_call", output_to_operand_aliasing={{0}: (4, {}), {1}: (5, {})} | custom-call | flops 22000001024 | bytes 1000 | tf_op jit(solution)/shard_map/came_rows/pallas_call | solution.py:448
  88.3 2.5 %raw_rows.3 = (bf16[16,2520,256]{2,1,0:T(8,128)(2,1)}, bf16[2,2520,256]{2,1,0:T(8,128)(2,1)S(1)}) custom-call(s32[21]{0:T(128)S(1)} %concatenate.15.meta, bf16[1,4,480,128]{3,2,1,0:T(8,128)(2,1)S(1)} %get-tuple-element.60.refs_0_, bf16[1,4,480,128]{3,2,1,0:T(8,128)(2,1)S(1)} %collective-permute-done.18.refs_5_.refs_1_, ...), custom_call_target="tpu_custom_call", output_to_operand_aliasing={{0}: (8, {})} | custom-call | flops 10000001024 | bytes 1000 | tf_op jit(solution)/shard_map/raw_rows/pallas_call | solution.py:426
  91.5 0.9 collective-permute-done.31.refs_1_
  92.8 2.2 %came_rows.3 = (bf16[16,2520,256]{2,1,0:T(8,128)(2,1)}, bf16[2,2520,256]{2,1,0:T(8,128)(2,1)S(1)}, bf16[2,2520,256]{2,1,0:T(8,128)(2,1)S(1)}) custom-call(s32[21]{0:T(128)S(1)} %concatenate.15.meta, bf16[1,600,128]{2,1,0:T(8,128)(2,1)S(1)} %get-tuple-element.79.refs_0_, ...), custom_call_target="tpu_custom_call", output_to_operand_aliasing={{0}: (7, {}), {1}: (8, {}), {2}: (9, {})} | custom-call | flops 1000 | bytes 1000 | tf_op jit(solution)/shard_map/came_rows/pallas_call | solution.py:448
  (50 shorter events, 7.6 us)
Async XLA Ops:
  1.2 7.0 %collective-permute-start.2 = (bf16[1,4,480,128]{3,2,1,0:T(8,128)(2,1)S(1)}, bf16[1,4,480,128]{3,2,1,0:T(8,128)(2,1)S(1)}, u32[]{:S(2)}, u32[]{:S(2)}) collective-permute-start(bf16[1,4,480,128]{3,2,1,0:T(8,128)(2,1)S(1)} %get-tuple-element.88.refs_0_), channel_id=1, source_target_pairs={{0,2},{2,0},{4,6},{6,4},{8,10},{10,8},{12,14},{14,12},{16,18},{18,... | collective-permute-start | bytes 1474568 | tf_op jit(solution)/shard_map/ppermute | solution.py:495
  1.8 9.4 %collective-permute-start = (bf16[1,4,480,128]{3,2,1,0:T(8,128)(2,1)S(1)}, bf16[1,4,480,128]{3,2,1,0:T(8,128)(2,1)S(1)}, u32[]{:S(2)}, u32[]{:S(2)}) collective-permute-start(bf16[1,4,480,128]{3,2,1,0:T(8,128)(2,1)S(1)} %get-tuple-element.88.refs_0_), channel_id=1, source_target_pairs={{0,8},{8,16},{16,24},{24,28},{28,20},{20,12},{12,4},{4,0},{2,6},{1... | collective-permute-start | bytes 1474568 | tf_op jit(solution)/shard_map/ppermute | solution.py:495
  4.4 13.9 %collective-permute-start.7 = (bf16[1,4,480,128]{3,2,1,0:T(8,128)(2,1)S(1)}, bf16[1,4,480,128]{3,2,1,0:T(8,128)(2,1)S(1)}, u32[]{:S(2)}, u32[]{:S(2)}) collective-permute-start(bf16[1,4,480,128]{3,2,1,0:T(8,128)(2,1)S(1)} %get-tuple-element.87.refs_0_), channel_id=1, source_target_pairs={{0,1},{1,0},{2,3},{3,2},{4,5},{5,4},{6,7},{7,6},{8,9},{9,8},{10,11... | collective-permute-start | bytes 1474568 | tf_op jit(solution)/shard_map/ppermute | solution.py:486
  6.8 14.2 %collective-permute-start.14 = (bf16[256,128]{0,1:T(8,128)(2,1)S(1)}, bf16[256,128]{0,1:T(8,128)(2,1)S(1)}, u32[]{:S(2)}, u32[]{:S(2)}) collective-permute-start(bf16[256,128]{0,1:T(8,128)(2,1)S(1)} %copy.28), channel_id=1, source_target_pairs={{0,1},{1,0},{2,3},{3,2},{4,5},{5,4},{6,7},{7,6},{8,9},{9,8},{10,11... | collective-permute-start | bytes 196616 | tf_op jit(solution)/shard_map/ppermute | solution.py:487
  8.2 10.1 %collective-permute-start.3 = (bf16[1,4,480,128]{3,2,1,0:T(8,128)(2,1)S(1)}, bf16[1,4,480,128]{3,2,1,0:T(8,128)(2,1)S(1)}, u32[]{:S(2)}, u32[]{:S(2)}) collective-permute-start(bf16[1,4,480,128]{3,2,1,0:T(8,128)(2,1)S(1)} %collective-permute-done.2), channel_id=1, source_target_pairs={{0,8},{8,16},{16,24},{24,28},{28,20},{20,12},{12,4},{4,0},{2,6},{1... | collective-permute-start | bytes 1474568 | tf_op jit(solution)/shard_map/ppermute | solution.py:495
  11.2 11.7 %collective-permute-start.1 = (bf16[1,4,480,128]{3,2,1,0:T(8,128)(2,1)S(1)}, bf16[1,4,480,128]{3,2,1,0:T(8,128)(2,1)S(1)}, u32[]{:S(2)}, u32[]{:S(2)}) collective-permute-start(bf16[1,4,480,128]{3,2,1,0:T(8,128)(2,1)S(1)} %collective-permute-done.refs_0_), channel_id=1, source_target_pairs={{0,8},{8,16},{16,24},{24,28},{28,20},{20,12},{12,4},{4,0},{2,6},{1... | collective-permute-start | bytes 1474568 | tf_op jit(solution)/shard_map/ppermute | solution.py:495
  18.3 2.8 %collective-permute-start.8 = (bf16[1,4,480,128]{3,2,1,0:T(8,128)(2,1)S(1)}, bf16[1,4,480,128]{3,2,1,0:T(8,128)(2,1)S(1)}, u32[]{:S(2)}, u32[]{:S(2)}) collective-permute-start(bf16[1,4,480,128]{3,2,1,0:T(8,128)(2,1)S(1)} %collective-permute-done.7.refs_1_), channel_id=1, source_target_pairs={{0,2},{2,0},{4,6},{6,4},{8,10},{10,8},{12,14},{14,12},{16,18},{18,... | collective-permute-start | bytes 1474568 | tf_op jit(solution)/shard_map/ppermute | solution.py:495
  18.3 10.7 %collective-permute-start.4 = (bf16[1,4,480,128]{3,2,1,0:T(8,128)(2,1)S(1)}, bf16[1,4,480,128]{3,2,1,0:T(8,128)(2,1)S(1)}, u32[]{:S(2)}, u32[]{:S(2)}) collective-permute-start(bf16[1,4,480,128]{3,2,1,0:T(8,128)(2,1)S(1)} %collective-permute-done.3.refs_1_), channel_id=1, source_target_pairs={{0,8},{8,16},{16,24},{24,28},{28,20},{20,12},{12,4},{4,0},{2,6},{1... | collective-permute-start | bytes 1474568 | tf_op jit(solution)/shard_map/ppermute | solution.py:495
  19.5 9.6 %collective-permute-start.11 = (bf16[2,600,128]{2,1,0:T(8,128)(2,1)S(1)}, bf16[2,600,128]{2,1,0:T(8,128)(2,1)S(1)}, u32[]{:S(2)}, u32[]{:S(2)}) collective-permute-start(bf16[2,600,128]{2,1,0:T(8,128)(2,1)S(1)} %get-tuple-element.48), channel_id=1, source_target_pairs={{0,1},{1,0},{2,3},{3,2},{4,5},{5,4},{6,7},{7,6},{8,9},{9,8},{10,11... | collective-permute-start | bytes 921608 | tf_op jit(solution)/shard_map/ppermute | solution.py:521
  21.0 10.9 %collective-permute-start.15 = (bf16[256,256]{1,0:T(8,128)(2,1)S(1)}, bf16[256,256]{1,0:T(8,128)(2,1)S(1)}, u32[]{:S(2)}, u32[]{:S(2)}) collective-permute-start(bf16[256,256]{1,0:T(8,128)(2,1)S(1)} %pad_maximum_fusion.3.refs_4_), channel_id=1, source_target_pairs={{0,2},{2,0},{4,6},{6,4},{8,10},{10,8},{12,14},{14,12},{16,18},{18,... | collective-permute-start | bytes 393224 | tf_op jit(solution)/shard_map/ppermute | solution.py:490
  21.2 18.9 %collective-permute-start.9 = (bf16[2,4,480,128]{3,2,1,0:T(8,128)(2,1)S(1)}, bf16[2,4,480,128]{3,2,1,0:T(8,128)(2,1)S(1)}, u32[]{:S(2)}, u32[]{:S(2)}) collective-permute-start(bf16[2,4,480,128]{3,2,1,0:T(8,128)(2,1)S(1)} %pad_maximum_fusion.1), channel_id=1, source_target_pairs={{0,8},{8,16},{16,24},{24,28},{28,20},{20,12},{12,4},{4,0},{2,6},{1... | collective-permute-start | bytes 2949128 | tf_op jit(solution)/shard_map/ppermute | solution.py:495
  29.8 10.3 %collective-permute-start.12 = (bf16[2,600,128]{2,1,0:T(8,128)(2,1)S(1)}, bf16[2,600,128]{2,1,0:T(8,128)(2,1)S(1)}, u32[]{:S(2)}, u32[]{:S(2)}) collective-permute-start(bf16[2,600,128]{2,1,0:T(8,128)(2,1)S(1)} %get-tuple-element.50), channel_id=1, source_target_pairs={{0,1},{1,0},{2,3},{3,2},{4,5},{5,4},{6,7},{7,6},{8,9},{9,8},{10,11... | collective-permute-start | bytes 921608 | tf_op jit(solution)/shard_map/ppermute | solution.py:521
  31.1 11.7 %collective-permute-start.16 = (bf16[1,600,128]{2,1,0:T(8,128)(2,1)S(1)}, bf16[1,600,128]{2,1,0:T(8,128)(2,1)S(1)}, u32[]{:S(2)}, u32[]{:S(2)}) collective-permute-start(bf16[1,600,128]{2,1,0:T(8,128)(2,1)S(1)} %get-tuple-element.53), channel_id=1, source_target_pairs={{0,1},{1,0},{2,3},{3,2},{4,5},{5,4},{6,7},{7,6},{8,9},{9,8},{10,11... | collective-permute-start | bytes 460808 | tf_op jit(solution)/shard_map/ppermute | solution.py:521
  32.0 16.7 %collective-permute-start.5 = (bf16[2,4,480,128]{3,2,1,0:T(8,128)(2,1)S(1)}, bf16[2,4,480,128]{3,2,1,0:T(8,128)(2,1)S(1)}, u32[]{:S(2)}, u32[]{:S(2)}) collective-permute-start(bf16[2,4,480,128]{3,2,1,0:T(8,128)(2,1)S(1)} %pad_maximum_fusion), channel_id=1, source_target_pairs={{0,8},{8,16},{16,24},{24,28},{28,20},{20,12},{12,4},{4,0},{2,6},{1... | collective-permute-start | bytes 2949128 | tf_op jit(solution)/shard_map/ppermute | solution.py:495
  40.9 7.6 %collective-permute-start.13 = (bf16[2,600,128]{2,1,0:T(8,128)(2,1)S(1)}, bf16[2,600,128]{2,1,0:T(8,128)(2,1)S(1)}, u32[]{:S(2)}, u32[]{:S(2)}) collective-permute-start(bf16[2,600,128]{2,1,0:T(8,128)(2,1)S(1)} %get-tuple-element.51), channel_id=1, source_target_pairs={{0,1},{1,0},{2,3},{3,2},{4,5},{5,4},{6,7},{7,6},{8,9},{9,8},{10,11... | collective-permute-start | bytes 921608 | tf_op jit(solution)/shard_map/ppermute | solution.py:521
  45.2 26.6 %collective-permute-start.24 = (bf16[1,2520,256]{2,1,0:T(8,128)(2,1)S(1)}, bf16[1,2520,256]{2,1,0:T(8,128)(2,1)S(1)}, u32[]{:S(2)}, u32[]{:S(2)}) collective-permute-start(bf16[1,2520,256]{2,1,0:T(8,128)(2,1)S(1)} %get-tuple-element.63), channel_id=1, source_target_pairs={{0,2},{2,0},{4,6},{6,4},{8,10},{10,8},{12,14},{14,12},{16,18},{18,... | collective-permute-start | bytes 3870728 | tf_op jit(solution)/shard_map/ppermute | solution.py:495
  45.3 14.1 %collective-permute-start.10 = (bf16[2,4,480,128]{3,2,1,0:T(8,128)(2,1)S(1)}, bf16[2,4,480,128]{3,2,1,0:T(8,128)(2,1)S(1)}, u32[]{:S(2)}, u32[]{:S(2)}) collective-permute-start(bf16[2,4,480,128]{3,2,1,0:T(8,128)(2,1)S(1)} %collective-permute-done.9.refs_0_.refs_2_), channel_id=1, source_target_pairs={{0,8},{8,16},{16,24},{24,28},{28,20},{20,12},{12,4},{4,0},{2,6},{1... | collective-permute-start | bytes 2949128 | tf_op jit(solution)/shard_map/ppermute | solution.py:495
  49.5 8.5 %collective-permute-start.17 = (bf16[2,600,128]{2,1,0:T(8,128)(2,1)S(1)}, bf16[2,600,128]{2,1,0:T(8,128)(2,1)S(1)}, u32[]{:S(2)}, u32[]{:S(2)}) collective-permute-start(bf16[2,600,128]{2,1,0:T(8,128)(2,1)S(1)} %get-tuple-element.58), channel_id=1, source_target_pairs={{0,1},{1,0},{2,3},{3,2},{4,5},{5,4},{6,7},{7,6},{8,9},{9,8},{10,11... | collective-permute-start | bytes 921608 | tf_op jit(solution)/shard_map/ppermute | solution.py:521
  50.8 13.9 %collective-permute-start.6 = (bf16[1,4,480,128]{3,2,1,0:T(8,128)(2,1)S(1)}, bf16[1,4,480,128]{3,2,1,0:T(8,128)(2,1)S(1)}, u32[]{:S(2)}, u32[]{:S(2)}) collective-permute-start(bf16[1,4,480,128]{3,2,1,0:T(8,128)(2,1)S(1)} %slice.12), channel_id=1, source_target_pairs={{0,8},{8,16},{16,24},{24,28},{28,20},{20,12},{12,4},{4,0},{2,6},{1... | collective-permute-start | bytes 1474568 | tf_op jit(solution)/shard_map/ppermute | solution.py:495
  55.8 22.1 %collective-permute-start.22 = (bf16[2,2520,256]{2,1,0:T(8,128)(2,1)S(1)}, bf16[2,2520,256]{2,1,0:T(8,128)(2,1)S(1)}, u32[]{:S(2)}, u32[]{:S(2)}) collective-permute-start(bf16[2,2520,256]{2,1,0:T(8,128)(2,1)S(1)} %get-tuple-element.61), channel_id=1, source_target_pairs={{0,2},{2,0},{4,6},{6,4},{8,10},{10,8},{12,14},{14,12},{16,18},{18,... | collective-permute-start | bytes 7741448 | tf_op jit(solution)/shard_map/ppermute | solution.py:495
  60.2 8.8 %collective-permute-start.23 = (bf16[2,600,128]{2,1,0:T(8,128)(2,1)S(1)}, bf16[2,600,128]{2,1,0:T(8,128)(2,1)S(1)}, u32[]{:S(2)}, u32[]{:S(2)}) collective-permute-start(bf16[2,600,128]{2,1,0:T(8,128)(2,1)S(1)} %get-tuple-element.62), channel_id=1, source_target_pairs={{0,1},{1,0},{2,3},{3,2},{4,5},{5,4},{6,7},{7,6},{8,9},{9,8},{10,11... | collective-permute-start | bytes 921608 | tf_op jit(solution)/shard_map/ppermute | solution.py:521
  61.4 8.9 %collective-permute-start.19 = (bf16[1,4,480,128]{3,2,1,0:T(8,128)(2,1)S(1)}, bf16[1,4,480,128]{3,2,1,0:T(8,128)(2,1)S(1)}, u32[]{:S(2)}, u32[]{:S(2)}) collective-permute-start(bf16[1,4,480,128]{3,2,1,0:T(8,128)(2,1)S(1)} %get-tuple-element.86), channel_id=1, source_target_pairs={{0,8},{8,16},{16,24},{24,28},{28,20},{20,12},{12,4},{4,0},{2,6},{1... | collective-permute-start | bytes 1474568 | tf_op jit(solution)/shard_map/ppermute | solution.py:495
  64.7 11.2 %collective-permute-start.21 = (bf16[1,4,480,128]{3,2,1,0:T(8,128)(2,1)S(1)}, bf16[1,4,480,128]{3,2,1,0:T(8,128)(2,1)S(1)}, u32[]{:S(2)}, u32[]{:S(2)}) collective-permute-start(bf16[1,4,480,128]{3,2,1,0:T(8,128)(2,1)S(1)} %get-tuple-element.85), channel_id=1, source_target_pairs={{0,8},{8,16},{16,24},{24,28},{28,20},{20,12},{12,4},{4,0},{2,6},{1... | collective-permute-start | bytes 1474568 | tf_op jit(solution)/shard_map/ppermute | solution.py:495
  69.1 6.4 %collective-permute-start.25 = (bf16[1,600,128]{2,1,0:T(8,128)(2,1)S(1)}, bf16[1,600,128]{2,1,0:T(8,128)(2,1)S(1)}, u32[]{:S(2)}, u32[]{:S(2)}) collective-permute-start(bf16[1,600,128]{2,1,0:T(8,128)(2,1)S(1)} %get-tuple-element.66), channel_id=1, source_target_pairs={{0,1},{1,0},{2,3},{3,2},{4,5},{5,4},{6,7},{7,6},{8,9},{9,8},{10,11... | collective-permute-start | bytes 460808 | tf_op jit(solution)/shard_map/ppermute | solution.py:559
  70.3 10.5 %collective-permute-start.20 = (bf16[1,4,480,128]{3,2,1,0:T(8,128)(2,1)S(1)}, bf16[1,4,480,128]{3,2,1,0:T(8,128)(2,1)S(1)}, u32[]{:S(2)}, u32[]{:S(2)}) collective-permute-start(bf16[1,4,480,128]{3,2,1,0:T(8,128)(2,1)S(1)} %collective-permute-done.19.refs_0_.refs_1_), channel_id=1, source_target_pairs={{0,8},{8,16},{16,24},{24,28},{28,20},{20,12},{12,4},{4,0},{2,6},{1... | collective-permute-start | bytes 1474568 | tf_op jit(solution)/shard_map/ppermute | solution.py:495
  75.4 6.6 %collective-permute-start.28 = (bf16[2,2520,256]{2,1,0:T(8,128)(2,1)S(1)}, bf16[2,2520,256]{2,1,0:T(8,128)(2,1)S(1)}, u32[]{:S(2)}, u32[]{:S(2)}) collective-permute-start(bf16[2,2520,256]{2,1,0:T(8,128)(2,1)S(1)} %get-tuple-element.71), channel_id=1, source_target_pairs={{0,2},{2,0},{4,6},{6,4},{8,10},{10,8},{12,14},{14,12},{16,18},{18,... | collective-permute-start | bytes 7741448 | tf_op jit(solution)/shard_map/ppermute | solution.py:495
  75.5 9.8 %collective-permute-start.18 = (bf16[1,4,480,128]{3,2,1,0:T(8,128)(2,1)S(1)}, bf16[1,4,480,128]{3,2,1,0:T(8,128)(2,1)S(1)}, u32[]{:S(2)}, u32[]{:S(2)}) collective-permute-start(bf16[1,4,480,128]{3,2,1,0:T(8,128)(2,1)S(1)} %get-tuple-element.60.refs_0_), channel_id=1, source_target_pairs={{0,2},{2,0},{4,6},{6,4},{8,10},{10,8},{12,14},{14,12},{16,18},{18,... | collective-permute-start | bytes 1474568 | tf_op jit(solution)/shard_map/ppermute | solution.py:495
  76.8 10.2 %collective-permute-start.27 = (bf16[2,600,128]{2,1,0:T(8,128)(2,1)S(1)}, bf16[2,600,128]{2,1,0:T(8,128)(2,1)S(1)}, u32[]{:S(2)}, u32[]{:S(2)}) collective-permute-start(bf16[2,600,128]{2,1,0:T(8,128)(2,1)S(1)} %get-tuple-element.70), channel_id=1, source_target_pairs={{0,1},{1,0},{2,3},{3,2},{4,5},{5,4},{6,7},{7,6},{8,9},{9,8},{10,11... | collective-permute-start | bytes 921608 | tf_op jit(solution)/shard_map/ppermute | solution.py:578
  80.7 7.7 %collective-permute-start.29 = (bf16[2,2520,256]{2,1,0:T(8,128)(2,1)S(1)}, bf16[2,2520,256]{2,1,0:T(8,128)(2,1)S(1)}, u32[]{:S(2)}, u32[]{:S(2)}) collective-permute-start(bf16[2,2520,256]{2,1,0:T(8,128)(2,1)S(1)} %get-tuple-element.75), channel_id=1, source_target_pairs={{0,2},{2,0},{4,6},{6,4},{8,10},{10,8},{12,14},{14,12},{16,18},{18,... | collective-permute-start | bytes 7741448 | tf_op jit(solution)/shard_map/ppermute | solution.py:495
  81.5 6.8 %collective-permute-start.26 = (bf16[1,4,480,128]{3,2,1,0:T(8,128)(2,1)S(1)}, bf16[1,4,480,128]{3,2,1,0:T(8,128)(2,1)S(1)}, u32[]{:S(2)}, u32[]{:S(2)}) collective-permute-start(bf16[1,4,480,128]{3,2,1,0:T(8,128)(2,1)S(1)} %get-tuple-element.69.refs_2_), channel_id=1, source_target_pairs={{0,2},{2,0},{4,6},{6,4},{8,10},{10,8},{12,14},{14,12},{16,18},{18,... | collective-permute-start | bytes 1474568 | tf_op jit(solution)/shard_map/ppermute | solution.py:495
  82.0 8.9 %collective-permute-start.30 = (bf16[1,600,128]{2,1,0:T(8,128)(2,1)S(1)}, bf16[1,600,128]{2,1,0:T(8,128)(2,1)S(1)}, u32[]{:S(2)}, u32[]{:S(2)}) collective-permute-start(bf16[1,600,128]{2,1,0:T(8,128)(2,1)S(1)} %get-tuple-element.78), channel_id=1, source_target_pairs={{0,1},{1,0},{2,3},{3,2},{4,5},{5,4},{6,7},{7,6},{8,9},{9,8},{10,11... | collective-permute-start | bytes 460808 | tf_op jit(solution)/shard_map/ppermute | solution.py:559
  88.2 3.3 %collective-permute-start.33 = (bf16[2,600,256]{2,1,0:T(8,128)(2,1)S(1)}, bf16[2,600,256]{2,1,0:T(8,128)(2,1)S(1)}, u32[]{:S(2)}, u32[]{:S(2)}) collective-permute-start(bf16[2,600,256]{2,1,0:T(8,128)(2,1)S(1)} %get-tuple-element.81), channel_id=1, source_target_pairs={{0,2},{2,0},{4,6},{6,4},{8,10},{10,8},{12,14},{14,12},{16,18},{18,... | collective-permute-start | bytes 1843208 | tf_op jit(solution)/shard_map/ppermute | solution.py:495
  90.9 1.6 %collective-permute-start.31 = (bf16[1,600,128]{2,1,0:T(8,128)(2,1)S(1)}, bf16[1,600,128]{2,1,0:T(8,128)(2,1)S(1)}, u32[]{:S(2)}, u32[]{:S(2)}) collective-permute-start(bf16[1,600,128]{2,1,0:T(8,128)(2,1)S(1)} %get-tuple-element.79.refs_0_), channel_id=1, source_target_pairs={{0,2},{2,0},{4,6},{6,4},{8,10},{10,8},{12,14},{14,12},{16,18},{18,... | collective-permute-start | bytes 460808 | tf_op jit(solution)/shard_map/ppermute | solution.py:495
  91.4 1.4 %collective-permute-start.32 = (bf16[1,600,128]{2,1,0:T(8,128)(2,1)S(1)}, bf16[1,600,128]{2,1,0:T(8,128)(2,1)S(1)}, u32[]{:S(2)}, u32[]{:S(2)}) collective-permute-start(bf16[1,600,128]{2,1,0:T(8,128)(2,1)S(1)} %get-tuple-element.80.refs_2_), channel_id=1, source_target_pairs={{0,2},{2,0},{4,6},{6,4},{8,10},{10,8},{12,14},{14,12},{16,18},{18,... | collective-permute-start | bytes 460808 | tf_op jit(solution)/shard_map/ppermute | solution.py:495

commit v6 on v5

--- a/solution.py
+++ b/solution.py
@@ -8,7 +8,7 @@
 from jax.sharding import PartitionSpec as P
 
 LANES = 128
-PARAMS = {'LAG': 2, 'F0': 10, 'F1': 0, 'PS0': 2, 'JA': 3, 'JB': 1, 'C0POS': 2, 'GATE': 30, 'F3': 0, 'F2': 22, 'NL': 1, 'PE4': 0, 'P4': 0, 'P3': 1, 'CPOS': 1, 'LC': 1, 'BSPL': 1, 'ONEX': 1, 'EL': 1, 'WH': 0, 'X00': 10, 'X01': 10, 'C0': 10, 'X10': 10, 'X11': 10, 'C1': 10, 'X20': 10, 'X21': 10, 'C2': 3, 'X30': 10, 'X31': 3, 'C3': 10, 'X40': 10, 'X41': 24, 'C4': 10}
+PARAMS = {'LAG': 2, 'F0': 10, 'F1': 0, 'PS0': 2, 'JA': 3, 'JB': 1, 'C0POS': 2, 'GATE': 30, 'F3': 0, 'F2': 22, 'NL': 0, 'PE4': 0, 'P4': 0, 'P3': 1, 'CPOS': 1, 'LC': 1, 'BSPL': 1, 'ONEX': 1, 'EL': 1, 'WH': 0, 'X00': 10, 'X01': 10, 'C0': 10, 'X10': 10, 'X11': 10, 'C1': 10, 'X20': 10, 'X21': 10, 'C2': 3, 'X30': 10, 'X31': 3, 'C3': 10, 'X40': 10, 'X41': 24, 'C4': 10}
 
 
 def G(name):

time: 95.4 us -> 95.4 us (level)
  no operation moved by 1% of the time
where the time goes in v6:
time: 95.4 us; the launch traced here: 95.3 us
  starting transfers between devices  32.4 us (34%)
  waiting for transfers between devices  32.4 us (34%)
  Pallas kernels  27.4 us (29%)
  local copies, waits for them, and re-layouts  2.36 us (2%)
    ppermute x22, starting transfers between devices, permute_rows(): return [lax.ppermute(piece, 'rows', pairs) for piece in pieces]  19.8 us
    ppermute x6, waiting for transfers between devices, do_extra(): across_came[d, 1 - part].append(lax.ppermute(extra, 'chan', across))  19.7 us
    pallas_call x3, Pallas kernels, correlate(): pl.pallas_call(functools.partial(corr_kernel, factor, tuple((len(part) fo...  9.29 us
    pallas_call x10, Pallas kernels, make_extra(): pl.pallas_call(functools.partial(extra_kernel, len(halves), 2 + len(carri...  7.18 us
    ppermute x6, starting transfers between devices, do_extra(): across_came[d, 1 - part].append(lax.ppermute(extra, 'chan', across))  7.11 us
    ppermute x22, waiting for transfers between devices, permute_rows(): return [lax.ppermute(piece, 'rows', pairs) for piece in pieces]  5.91 us
    ppermute x1, waiting for transfers between devices, ring_local(): partner = lax.ppermute(theirs, 'chan', across)  5.11 us
    pallas_call x2, Pallas kernels, raw_rows(): pl.pallas_call(functools.partial(raw_kernel, factor, (len(own), len(other...  5.08 us
  transfers between devices with their start and end apart: 34, of which 16 were waited for; matrix products, arithmetic and copies ran while one was open for 1% of the time, Pallas kernels for 26%

profile of v6, /device:TPU:0, one launch (start us, length us, event | category | flops | bytes accessed | tf_op | source)
XLA Modules:
  0.0 95.3 jit_solution(1389650129139995910)
XLA Ops:
  0.0 1.2 %dynamic-slice_bitcast_fusion = (bf16[1,4,480,128]{3,2,1,0:T(8,128)(2,1)S(1)}, bf16[1,4,480,128]{3,2,1,0:T(8,128)(2,1)S(1)}) fusion(bf16[8,480,128]{2,1,0:T(8,128)(2,1)} %param.3, s32[]{:T(128)S(6)} %select_n.72, s32[]{:T(128)S(6)} %select_n.71), kind=kLoop, calls=%fused_computation.2 | loop fusion | bytes 1966088 | tf_op jit(solution)/shard_map/broadcast_in_dim | solution.py:478
  1.8 2.6 %collective-permute-start = (bf16[1,4,480,128]{3,2,1,0:T(8,128)(2,1)S(1)}, bf16[1,4,480,128]{3,2,1,0:T(8,128)(2,1)S(1)}, u32[]{:S(2)}, u32[]{:S(2)}) collective-permute-start(bf16[1,4,480,128]{3,2,1,0:T(8,128)(2,1)S(1)} %get-tuple-element.88.refs_0_), channel_id=1, source_target_pairs={{0,8},{8,16},{16,24},{24,28},{28,20},{20,12},{12,4},{4,0},{2,6},{1... | collective-permute-start | bytes 1474568 | tf_op jit(solution)/shard_map/ppermute | solution.py:495
  4.4 1.5 %collective-permute-start.7 = (bf16[1,4,480,128]{3,2,1,0:T(8,128)(2,1)S(1)}, bf16[1,4,480,128]{3,2,1,0:T(8,128)(2,1)S(1)}, u32[]{:S(2)}, u32[]{:S(2)}) collective-permute-start(bf16[1,4,480,128]{3,2,1,0:T(8,128)(2,1)S(1)} %get-tuple-element.87.refs_0_), channel_id=1, source_target_pairs={{0,1},{1,0},{2,3},{3,2},{4,5},{5,4},{6,7},{7,6},{8,9},{9,8},{10,11... | collective-permute-start | bytes 1474568 | tf_op jit(solution)/shard_map/ppermute | solution.py:486
  5.9 0.9 copy.28
  8.2 1.6 %collective-permute-start.3 = (bf16[1,4,480,128]{3,2,1,0:T(8,128)(2,1)S(1)}, bf16[1,4,480,128]{3,2,1,0:T(8,128)(2,1)S(1)}, u32[]{:S(2)}, u32[]{:S(2)}) collective-permute-start(bf16[1,4,480,128]{3,2,1,0:T(8,128)(2,1)S(1)} %collective-permute-done.2), channel_id=1, source_target_pairs={{0,8},{8,16},{16,24},{24,28},{28,20},{20,12},{12,4},{4,0},{2,6},{1... | collective-permute-start | bytes 1474568 | tf_op jit(solution)/shard_map/ppermute | solution.py:495
  10.5 0.7 collective-permute-done.refs_0_
  11.2 2.1 %collective-permute-start.1 = (bf16[1,4,480,128]{3,2,1,0:T(8,128)(2,1)S(1)}, bf16[1,4,480,128]{3,2,1,0:T(8,128)(2,1)S(1)}, u32[]{:S(2)}, u32[]{:S(2)}) collective-permute-start(bf16[1,4,480,128]{3,2,1,0:T(8,128)(2,1)S(1)} %collective-permute-done.refs_0_), channel_id=1, source_target_pairs={{0,8},{8,16},{16,24},{24,28},{28,20},{20,12},{12,4},{4,0},{2,6},{1... | collective-permute-start | bytes 1474568 | tf_op jit(solution)/shard_map/ppermute | solution.py:495
  13.2 5.1 %collective-permute-done.7.refs_1_ = bf16[1,4,480,128]{3,2,1,0:T(8,128)(2,1)S(1)} collective-permute-done((bf16[1,4,480,128]{3,2,1,0:T(8,128)(2,1)S(1)}, bf16[1,4,480,128]{3,2,1,0:T(8,128)(2,1)S(1)}, u32[]{:S(2)}, u32[]{:S(2)}) %collective-permute-start.7) | collective-permute-done | bytes 491552 | tf_op jit(solution)/shard_map/ppermute | solution.py:486
  18.7 0.8 extra.12
  19.5 1.5 %collective-permute-start.11 = (bf16[2,600,128]{2,1,0:T(8,128)(2,1)S(1)}, bf16[2,600,128]{2,1,0:T(8,128)(2,1)S(1)}, u32[]{:S(2)}, u32[]{:S(2)}) collective-permute-start(bf16[2,600,128]{2,1,0:T(8,128)(2,1)S(1)} %get-tuple-element.48), channel_id=1, source_target_pairs={{0,1},{1,0},{2,3},{3,2},{4,5},{5,4},{6,7},{7,6},{8,9},{9,8},{10,11... | collective-permute-start | bytes 921608 | tf_op jit(solution)/shard_map/ppermute | solution.py:521
  21.2 1.6 %collective-permute-start.9 = (bf16[2,4,480,128]{3,2,1,0:T(8,128)(2,1)S(1)}, bf16[2,4,480,128]{3,2,1,0:T(8,128)(2,1)S(1)}, u32[]{:S(2)}, u32[]{:S(2)}) collective-permute-start(bf16[2,4,480,128]{3,2,1,0:T(8,128)(2,1)S(1)} %pad_maximum_fusion.1), channel_id=1, source_target_pairs={{0,8},{8,16},{16,24},{24,28},{28,20},{20,12},{12,4},{4,0},{2,6},{1... | collective-permute-start | bytes 2949128 | tf_op jit(solution)/shard_map/ppermute | solution.py:495
  22.9 6.2 %collective-permute-done.11.refs_3_.refs_4_ = bf16[2,600,128]{2,1,0:T(8,128)(2,1)S(1)} collective-permute-done((bf16[2,600,128]{2,1,0:T(8,128)(2,1)S(1)}, bf16[2,600,128]{2,1,0:T(8,128)(2,1)S(1)}, u32[]{:S(2)}, u32[]{:S(2)}) %collective-permute-start.11) | collective-permute-done | bytes 307232 | tf_op jit(solution)/shard_map/ppermute | solution.py:521
  29.0 0.8 extra.13
  29.8 1.3 %collective-permute-start.12 = (bf16[2,600,128]{2,1,0:T(8,128)(2,1)S(1)}, bf16[2,600,128]{2,1,0:T(8,128)(2,1)S(1)}, u32[]{:S(2)}, u32[]{:S(2)}) collective-permute-start(bf16[2,600,128]{2,1,0:T(8,128)(2,1)S(1)} %get-tuple-element.50), channel_id=1, source_target_pairs={{0,1},{1,0},{2,3},{3,2},{4,5},{5,4},{6,7},{7,6},{8,9},{9,8},{10,11... | collective-permute-start | bytes 921608 | tf_op jit(solution)/shard_map/ppermute | solution.py:521
  31.1 0.8 collective-permute-start.16
  32.0 1.6 %collective-permute-start.5 = (bf16[2,4,480,128]{3,2,1,0:T(8,128)(2,1)S(1)}, bf16[2,4,480,128]{3,2,1,0:T(8,128)(2,1)S(1)}, u32[]{:S(2)}, u32[]{:S(2)}) collective-permute-start(bf16[2,4,480,128]{3,2,1,0:T(8,128)(2,1)S(1)} %pad_maximum_fusion), channel_id=1, source_target_pairs={{0,8},{8,16},{16,24},{24,28},{28,20},{20,12},{12,4},{4,0},{2,6},{1... | collective-permute-start | bytes 2949128 | tf_op jit(solution)/shard_map/ppermute | solution.py:495
  33.7 6.4 %collective-permute-done.12.refs_2_.refs_4_ = bf16[2,600,128]{2,1,0:T(8,128)(2,1)S(1)} collective-permute-done((bf16[2,600,128]{2,1,0:T(8,128)(2,1)S(1)}, bf16[2,600,128]{2,1,0:T(8,128)(2,1)S(1)}, u32[]{:S(2)}, u32[]{:S(2)}) %collective-permute-start.12) | collective-permute-done | bytes 307232 | tf_op jit(solution)/shard_map/ppermute | solution.py:521
  40.1 0.8 extra.14
  40.9 1.1 %collective-permute-start.13 = (bf16[2,600,128]{2,1,0:T(8,128)(2,1)S(1)}, bf16[2,600,128]{2,1,0:T(8,128)(2,1)S(1)}, u32[]{:S(2)}, u32[]{:S(2)}) collective-permute-start(bf16[2,600,128]{2,1,0:T(8,128)(2,1)S(1)} %get-tuple-element.51), channel_id=1, source_target_pairs={{0,1},{1,0},{2,3},{3,2},{4,5},{5,4},{6,7},{7,6},{8,9},{9,8},{10,11... | collective-permute-start | bytes 921608 | tf_op jit(solution)/shard_map/ppermute | solution.py:521
  42.0 0.8 collective-permute-done.16.refs_3_
  42.8 2.5 %correlate.3 = (bf16[16,2520,256]{2,1,0:T(8,128)(2,1)}, bf16[1,2520,256]{2,1,0:T(8,128)(2,1)S(1)}) custom-call(s32[21]{0:T(128)S(1)} %concatenate.15.meta, bf16[1,4,480,128]{3,2,1,0:T(8,128)(2,1)S(1)} %get-tuple-element.88.refs_0_, bf16[1,4,480,128]{3,2,1,0:T(8,128)(2,1)S(1)} %collective-permute-done.7.refs_1_, ...), custom_call_target="tpu_custom_call", output_to_operand_aliasing={{0}: (6, {})} | custom-call | flops 10000001024 | bytes 1000 | tf_op jit(solution)/shard_map/correlate/pallas_call | solution.py:400
  45.3 1.2 %collective-permute-start.10 = (bf16[2,4,480,128]{3,2,1,0:T(8,128)(2,1)S(1)}, bf16[2,4,480,128]{3,2,1,0:T(8,128)(2,1)S(1)}, u32[]{:S(2)}, u32[]{:S(2)}) collective-permute-start(bf16[2,4,480,128]{3,2,1,0:T(8,128)(2,1)S(1)} %collective-permute-done.9.refs_0_.refs_2_), channel_id=1, source_target_pairs={{0,8},{8,16},{16,24},{24,28},{28,20},{20,12},{12,4},{4,0},{2,6},{1... | collective-permute-start | bytes 2949128 | tf_op jit(solution)/shard_map/ppermute | solution.py:495
  46.5 1.9 %collective-permute-done.13.refs_2_.refs_3_ = bf16[2,600,128]{2,1,0:T(8,128)(2,1)S(1)} collective-permute-done((bf16[2,600,128]{2,1,0:T(8,128)(2,1)S(1)}, bf16[2,600,128]{2,1,0:T(8,128)(2,1)S(1)}, u32[]{:S(2)}, u32[]{:S(2)}) %collective-permute-start.13) | collective-permute-done | bytes 307232 | tf_op jit(solution)/shard_map/ppermute | solution.py:521
  48.7 0.8 extra.15
  49.5 1.3 %collective-permute-start.17 = (bf16[2,600,128]{2,1,0:T(8,128)(2,1)S(1)}, bf16[2,600,128]{2,1,0:T(8,128)(2,1)S(1)}, u32[]{:S(2)}, u32[]{:S(2)}) collective-permute-start(bf16[2,600,128]{2,1,0:T(8,128)(2,1)S(1)} %get-tuple-element.58), channel_id=1, source_target_pairs={{0,1},{1,0},{2,3},{3,2},{4,5},{5,4},{6,7},{7,6},{8,9},{9,8},{10,11... | collective-permute-start | bytes 921608 | tf_op jit(solution)/shard_map/ppermute | solution.py:521
  50.8 1.6 %collective-permute-start.6 = (bf16[1,4,480,128]{3,2,1,0:T(8,128)(2,1)S(1)}, bf16[1,4,480,128]{3,2,1,0:T(8,128)(2,1)S(1)}, u32[]{:S(2)}, u32[]{:S(2)}) collective-permute-start(bf16[1,4,480,128]{3,2,1,0:T(8,128)(2,1)S(1)} %slice.12), channel_id=1, source_target_pairs={{0,8},{8,16},{16,24},{24,28},{28,20},{20,12},{12,4},{4,0},{2,6},{1... | collective-permute-start | bytes 1474568 | tf_op jit(solution)/shard_map/ppermute | solution.py:495
  52.5 3.3 %correlate.4 = (bf16[16,2520,256]{2,1,0:T(8,128)(2,1)}, bf16[2,2520,256]{2,1,0:T(8,128)(2,1)S(1)}) custom-call(s32[21]{0:T(128)S(1)} %concatenate.15.meta, bf16[1,4,480,128]{3,2,1,0:T(8,128)(2,1)S(1)} %collective-permute-done.refs_0_, bf16[1,4,480,128]{3,2,1,0:T(8,128)(2,1)S(1)} %collective-permute-done.3.refs_1_, ...), custom_call_target="tpu_custom_call", output_to_operand_aliasing={{0}: (7, {})} | custom-call | flops 10000001024 | bytes 1000 | tf_op jit(solution)/shard_map/correlate/pallas_call | solution.py:400
  55.9 2.1 %collective-permute-done.17.refs_2_.refs_1_ = bf16[2,600,128]{2,1,0:T(8,128)(2,1)S(1)} collective-permute-done((bf16[2,600,128]{2,1,0:T(8,128)(2,1)S(1)}, bf16[2,600,128]{2,1,0:T(8,128)(2,1)S(1)}, u32[]{:S(2)}, u32[]{:S(2)}) %collective-permute-start.17) | collective-permute-done | bytes 307232 | tf_op jit(solution)/shard_map/ppermute | solution.py:521
  58.0 1.5 %collective-permute-done.10.refs_0_.refs_2_ = bf16[2,4,480,128]{3,2,1,0:T(8,128)(2,1)S(1)} collective-permute-done((bf16[2,4,480,128]{3,2,1,0:T(8,128)(2,1)S(1)}, bf16[2,4,480,128]{3,2,1,0:T(8,128)(2,1)S(1)}, u32[]{:S(2)}, u32[]{:S(2)}) %collective-permute-start.10) | collective-permute-done | bytes 983072 | tf_op jit(solution)/shard_map/ppermute | solution.py:495
  59.5 0.8 extra.16
  60.2 1.1 %collective-permute-start.23 = (bf16[2,600,128]{2,1,0:T(8,128)(2,1)S(1)}, bf16[2,600,128]{2,1,0:T(8,128)(2,1)S(1)}, u32[]{:S(2)}, u32[]{:S(2)}) collective-permute-start(bf16[2,600,128]{2,1,0:T(8,128)(2,1)S(1)} %get-tuple-element.62), channel_id=1, source_target_pairs={{0,1},{1,0},{2,3},{3,2},{4,5},{5,4},{6,7},{7,6},{8,9},{9,8},{10,11... | collective-permute-start | bytes 921608 | tf_op jit(solution)/shard_map/ppermute | solution.py:521
  61.4 1.6 %collective-permute-start.19 = (bf16[1,4,480,128]{3,2,1,0:T(8,128)(2,1)S(1)}, bf16[1,4,480,128]{3,2,1,0:T(8,128)(2,1)S(1)}, u32[]{:S(2)}, u32[]{:S(2)}) collective-permute-start(bf16[1,4,480,128]{3,2,1,0:T(8,128)(2,1)S(1)} %get-tuple-element.86), channel_id=1, source_target_pairs={{0,8},{8,16},{16,24},{24,28},{28,20},{20,12},{12,4},{4,0},{2,6},{1... | collective-permute-start | bytes 1474568 | tf_op jit(solution)/shard_map/ppermute | solution.py:495
  63.0 1.7 %collective-permute-done.6.refs_0_ = bf16[1,4,480,128]{3,2,1,0:T(8,128)(2,1)S(1)} collective-permute-done((bf16[1,4,480,128]{3,2,1,0:T(8,128)(2,1)S(1)}, bf16[1,4,480,128]{3,2,1,0:T(8,128)(2,1)S(1)}, u32[]{:S(2)}, u32[]{:S(2)}) %collective-permute-start.6) | collective-permute-done | bytes 491552 | tf_op jit(solution)/shard_map/ppermute | solution.py:495
  64.7 1.4 %collective-permute-start.21 = (bf16[1,4,480,128]{3,2,1,0:T(8,128)(2,1)S(1)}, bf16[1,4,480,128]{3,2,1,0:T(8,128)(2,1)S(1)}, u32[]{:S(2)}, u32[]{:S(2)}) collective-permute-start(bf16[1,4,480,128]{3,2,1,0:T(8,128)(2,1)S(1)} %get-tuple-element.85), channel_id=1, source_target_pairs={{0,8},{8,16},{16,24},{24,28},{28,20},{20,12},{12,4},{4,0},{2,6},{1... | collective-permute-start | bytes 1474568 | tf_op jit(solution)/shard_map/ppermute | solution.py:495
  66.8 2.3 %collective-permute-done.23.refs_3_ = bf16[2,600,128]{2,1,0:T(8,128)(2,1)S(1)} collective-permute-done((bf16[2,600,128]{2,1,0:T(8,128)(2,1)S(1)}, bf16[2,600,128]{2,1,0:T(8,128)(2,1)S(1)}, u32[]{:S(2)}, u32[]{:S(2)}) %collective-permute-start.23) | collective-permute-done | bytes 307232 | tf_op jit(solution)/shard_map/ppermute | solution.py:521
  69.1 0.9 collective-permute-start.25
  70.3 1.6 %collective-permute-start.20 = (bf16[1,4,480,128]{3,2,1,0:T(8,128)(2,1)S(1)}, bf16[1,4,480,128]{3,2,1,0:T(8,128)(2,1)S(1)}, u32[]{:S(2)}, u32[]{:S(2)}) collective-permute-start(bf16[1,4,480,128]{3,2,1,0:T(8,128)(2,1)S(1)} %collective-permute-done.19.refs_0_.refs_1_), channel_id=1, source_target_pairs={{0,8},{8,16},{16,24},{24,28},{28,20},{20,12},{12,4},{4,0},{2,6},{1... | collective-permute-start | bytes 1474568 | tf_op jit(solution)/shard_map/ppermute | solution.py:495
  71.9 3.5 %correlate.5 = (bf16[16,2520,256]{2,1,0:T(8,128)(2,1)}, bf16[2,2520,256]{2,1,0:T(8,128)(2,1)S(1)}) custom-call(s32[21]{0:T(128)S(1)} %concatenate.15.meta, bf16[1,4,480,128]{3,2,1,0:T(8,128)(2,1)S(1)} %collective-permute-done.1.refs_0_, bf16[1,4,480,128]{3,2,1,0:T(8,128)(2,1)S(1)} %collective-permute-done.4.refs_1_, ...), custom_call_target="tpu_custom_call", output_to_operand_aliasing={{0}: (8, {})} | custom-call | flops 3000001024 | bytes 1000 | tf_op jit(solution)/shard_map/correlate/pallas_call | solution.py:400
  76.0 0.8 extra.18
  76.8 1.1 %collective-permute-start.27 = (bf16[2,600,128]{2,1,0:T(8,128)(2,1)S(1)}, bf16[2,600,128]{2,1,0:T(8,128)(2,1)S(1)}, u32[]{:S(2)}, u32[]{:S(2)}) collective-permute-start(bf16[2,600,128]{2,1,0:T(8,128)(2,1)S(1)} %get-tuple-element.70), channel_id=1, source_target_pairs={{0,1},{1,0},{2,3},{3,2},{4,5},{5,4},{6,7},{7,6},{8,9},{9,8},{10,11... | collective-permute-start | bytes 921608 | tf_op jit(solution)/shard_map/ppermute | solution.py:578
  77.9 2.8 %raw_rows.2 = (bf16[16,2520,256]{2,1,0:T(8,128)(2,1)}, bf16[2,2520,256]{2,1,0:T(8,128)(2,1)S(1)}, bf16[2,2520,256]{2,1,0:T(8,128)(2,1)S(1)}) custom-call(s32[21]{0:T(128)S(1)} %concatenate.15.meta, bf16[2,4,480,128]{3,2,1,0:T(8,128)(2,1)S(1)} %collective-permute-done.5.refs_0_, ...), custom_call_target="tpu_custom_call", output_to_operand_aliasing={{0}: (6, {})} | custom-call | flops 1000 | bytes 1000 | tf_op jit(solution)/shard_map/raw_rows/pallas_call | solution.py:426
  82.0 1.3 %collective-permute-start.30 = (bf16[1,600,128]{2,1,0:T(8,128)(2,1)S(1)}, bf16[1,600,128]{2,1,0:T(8,128)(2,1)S(1)}, u32[]{:S(2)}, u32[]{:S(2)}) collective-permute-start(bf16[1,600,128]{2,1,0:T(8,128)(2,1)S(1)} %get-tuple-element.78), channel_id=1, source_target_pairs={{0,1},{1,0},{2,3},{3,2},{4,5},{5,4},{6,7},{7,6},{8,9},{9,8},{10,11... | collective-permute-start | bytes 460808 | tf_op jit(solution)/shard_map/ppermute | solution.py:559
  83.2 2.0 %land.1.refs_3_ = bf16[16,2520,256]{2,1,0:T(8,128)(2,1)} custom-call(s32[21]{0:T(128)S(1)} %concatenate.15.meta, bf16[2,2520,256]{2,1,0:T(8,128)(2,1)S(1)} %collective-permute-done.28.strips, bf16[16,2520,256]{2,1,0:T(8,128)(2,1)} %get-tuple-element.72._), custom_call_target="tpu_custom_call", output_to_operand_aliasing={{}: (2, {})} | custom-call | flops 1000 | bytes 1000 | tf_op jit(solution)/shard_map/land/pallas_call | solution.py:587
  85.3 1.7 %collective-permute-done.27.refs_0_ = bf16[2,600,128]{2,1,0:T(8,128)(2,1)S(1)} collective-permute-done((bf16[2,600,128]{2,1,0:T(8,128)(2,1)S(1)}, bf16[2,600,128]{2,1,0:T(8,128)(2,1)S(1)}, u32[]{:S(2)}, u32[]{:S(2)}) %collective-permute-start.27) | collective-permute-done | bytes 307232 | tf_op jit(solution)/shard_map/ppermute | solution.py:578
  87.0 1.3 %came_rows.2 = (bf16[16,2520,256]{2,1,0:T(8,128)(2,1)}, bf16[2,2520,256]{2,1,0:T(8,128)(2,1)S(1)}, bf16[2,600,256]{2,1,0:T(8,128)(2,1)S(1)}) custom-call(s32[21]{0:T(128)S(1)} %concatenate.15.meta, bf16[2,600,128]{2,1,0:T(8,128)(2,1)S(1)} %collective-permute-done.27.refs_0_, ...), custom_call_target="tpu_custom_call", output_to_operand_aliasing={{0}: (4, {}), {1}: (5, {})} | custom-call | flops 22000001024 | bytes 1000 | tf_op jit(solution)/shard_map/came_rows/pallas_call | solution.py:448
  88.3 2.3 %raw_rows.3 = (bf16[16,2520,256]{2,1,0:T(8,128)(2,1)}, bf16[2,2520,256]{2,1,0:T(8,128)(2,1)S(1)}) custom-call(s32[21]{0:T(128)S(1)} %concatenate.15.meta, bf16[1,4,480,128]{3,2,1,0:T(8,128)(2,1)S(1)} %get-tuple-element.60.refs_0_, bf16[1,4,480,128]{3,2,1,0:T(8,128)(2,1)S(1)} %collective-permute-done.18.refs_5_.refs_1_, ...), custom_call_target="tpu_custom_call", output_to_operand_aliasing={{0}: (8, {})} | custom-call | flops 10000001024 | bytes 1000 | tf_op jit(solution)/shard_map/raw_rows/pallas_call | solution.py:426
  91.3 0.9 collective-permute-done.31.refs_1_
  92.6 2.5 %came_rows.3 = (bf16[16,2520,256]{2,1,0:T(8,128)(2,1)}, bf16[2,2520,256]{2,1,0:T(8,128)(2,1)S(1)}, bf16[2,2520,256]{2,1,0:T(8,128)(2,1)S(1)}) custom-call(s32[21]{0:T(128)S(1)} %concatenate.15.meta, bf16[1,600,128]{2,1,0:T(8,128)(2,1)S(1)} %get-tuple-element.79.refs_0_, ...), custom_call_target="tpu_custom_call", output_to_operand_aliasing={{0}: (7, {}), {1}: (8, {}), {2}: (9, {})} | custom-call | flops 1000 | bytes 1000 | tf_op jit(solution)/shard_map/came_rows/pallas_call | solution.py:448
  (50 shorter events, 7.6 us)
Async XLA Ops:
  1.2 7.0 %collective-permute-start.2 = (bf16[1,4,480,128]{3,2,1,0:T(8,128)(2,1)S(1)}, bf16[1,4,480,128]{3,2,1,0:T(8,128)(2,1)S(1)}, u32[]{:S(2)}, u32[]{:S(2)}) collective-permute-start(bf16[1,4,480,128]{3,2,1,0:T(8,128)(2,1)S(1)} %get-tuple-element.88.refs_0_), channel_id=1, source_target_pairs={{0,2},{2,0},{4,6},{6,4},{8,10},{10,8},{12,14},{14,12},{16,18},{18,... | collective-permute-start | bytes 1474568 | tf_op jit(solution)/shard_map/ppermute | solution.py:495
  1.8 9.4 %collective-permute-start = (bf16[1,4,480,128]{3,2,1,0:T(8,128)(2,1)S(1)}, bf16[1,4,480,128]{3,2,1,0:T(8,128)(2,1)S(1)}, u32[]{:S(2)}, u32[]{:S(2)}) collective-permute-start(bf16[1,4,480,128]{3,2,1,0:T(8,128)(2,1)S(1)} %get-tuple-element.88.refs_0_), channel_id=1, source_target_pairs={{0,8},{8,16},{16,24},{24,28},{28,20},{20,12},{12,4},{4,0},{2,6},{1... | collective-permute-start | bytes 1474568 | tf_op jit(solution)/shard_map/ppermute | solution.py:495
  4.4 13.9 %collective-permute-start.7 = (bf16[1,4,480,128]{3,2,1,0:T(8,128)(2,1)S(1)}, bf16[1,4,480,128]{3,2,1,0:T(8,128)(2,1)S(1)}, u32[]{:S(2)}, u32[]{:S(2)}) collective-permute-start(bf16[1,4,480,128]{3,2,1,0:T(8,128)(2,1)S(1)} %get-tuple-element.87.refs_0_), channel_id=1, source_target_pairs={{0,1},{1,0},{2,3},{3,2},{4,5},{5,4},{6,7},{7,6},{8,9},{9,8},{10,11... | collective-permute-start | bytes 1474568 | tf_op jit(solution)/shard_map/ppermute | solution.py:486
  6.8 14.2 %collective-permute-start.14 = (bf16[256,128]{0,1:T(8,128)(2,1)S(1)}, bf16[256,128]{0,1:T(8,128)(2,1)S(1)}, u32[]{:S(2)}, u32[]{:S(2)}) collective-permute-start(bf16[256,128]{0,1:T(8,128)(2,1)S(1)} %copy.28), channel_id=1, source_target_pairs={{0,1},{1,0},{2,3},{3,2},{4,5},{5,4},{6,7},{7,6},{8,9},{9,8},{10,11... | collective-permute-start | bytes 196616 | tf_op jit(solution)/shard_map/ppermute | solution.py:487
  8.2 10.1 %collective-permute-start.3 = (bf16[1,4,480,128]{3,2,1,0:T(8,128)(2,1)S(1)}, bf16[1,4,480,128]{3,2,1,0:T(8,128)(2,1)S(1)}, u32[]{:S(2)}, u32[]{:S(2)}) collective-permute-start(bf16[1,4,480,128]{3,2,1,0:T(8,128)(2,1)S(1)} %collective-permute-done.2), channel_id=1, source_target_pairs={{0,8},{8,16},{16,24},{24,28},{28,20},{20,12},{12,4},{4,0},{2,6},{1... | collective-permute-start | bytes 1474568 | tf_op jit(solution)/shard_map/ppermute | solution.py:495
  11.2 11.7 %collective-permute-start.1 = (bf16[1,4,480,128]{3,2,1,0:T(8,128)(2,1)S(1)}, bf16[1,4,480,128]{3,2,1,0:T(8,128)(2,1)S(1)}, u32[]{:S(2)}, u32[]{:S(2)}) collective-permute-start(bf16[1,4,480,128]{3,2,1,0:T(8,128)(2,1)S(1)} %collective-permute-done.refs_0_), channel_id=1, source_target_pairs={{0,8},{8,16},{16,24},{24,28},{28,20},{20,12},{12,4},{4,0},{2,6},{1... | collective-permute-start | bytes 1474568 | tf_op jit(solution)/shard_map/ppermute | solution.py:495
  18.3 2.8 %collective-permute-start.8 = (bf16[1,4,480,128]{3,2,1,0:T(8,128)(2,1)S(1)}, bf16[1,4,480,128]{3,2,1,0:T(8,128)(2,1)S(1)}, u32[]{:S(2)}, u32[]{:S(2)}) collective-permute-start(bf16[1,4,480,128]{3,2,1,0:T(8,128)(2,1)S(1)} %collective-permute-done.7.refs_1_), channel_id=1, source_target_pairs={{0,2},{2,0},{4,6},{6,4},{8,10},{10,8},{12,14},{14,12},{16,18},{18,... | collective-permute-start | bytes 1474568 | tf_op jit(solution)/shard_map/ppermute | solution.py:495
  18.3 10.7 %collective-permute-start.4 = (bf16[1,4,480,128]{3,2,1,0:T(8,128)(2,1)S(1)}, bf16[1,4,480,128]{3,2,1,0:T(8,128)(2,1)S(1)}, u32[]{:S(2)}, u32[]{:S(2)}) collective-permute-start(bf16[1,4,480,128]{3,2,1,0:T(8,128)(2,1)S(1)} %collective-permute-done.3.refs_1_), channel_id=1, source_target_pairs={{0,8},{8,16},{16,24},{24,28},{28,20},{20,12},{12,4},{4,0},{2,6},{1... | collective-permute-start | bytes 1474568 | tf_op jit(solution)/shard_map/ppermute | solution.py:495
  19.5 9.6 %collective-permute-start.11 = (bf16[2,600,128]{2,1,0:T(8,128)(2,1)S(1)}, bf16[2,600,128]{2,1,0:T(8,128)(2,1)S(1)}, u32[]{:S(2)}, u32[]{:S(2)}) collective-permute-start(bf16[2,600,128]{2,1,0:T(8,128)(2,1)S(1)} %get-tuple-element.48), channel_id=1, source_target_pairs={{0,1},{1,0},{2,3},{3,2},{4,5},{5,4},{6,7},{7,6},{8,9},{9,8},{10,11... | collective-permute-start | bytes 921608 | tf_op jit(solution)/shard_map/ppermute | solution.py:521
  21.0 10.9 %collective-permute-start.15 = (bf16[256,256]{1,0:T(8,128)(2,1)S(1)}, bf16[256,256]{1,0:T(8,128)(2,1)S(1)}, u32[]{:S(2)}, u32[]{:S(2)}) collective-permute-start(bf16[256,256]{1,0:T(8,128)(2,1)S(1)} %pad_maximum_fusion.3.refs_4_), channel_id=1, source_target_pairs={{0,2},{2,0},{4,6},{6,4},{8,10},{10,8},{12,14},{14,12},{16,18},{18,... | collective-permute-start | bytes 393224 | tf_op jit(solution)/shard_map/ppermute | solution.py:490
  21.2 18.9 %collective-permute-start.9 = (bf16[2,4,480,128]{3,2,1,0:T(8,128)(2,1)S(1)}, bf16[2,4,480,128]{3,2,1,0:T(8,128)(2,1)S(1)}, u32[]{:S(2)}, u32[]{:S(2)}) collective-permute-start(bf16[2,4,480,128]{3,2,1,0:T(8,128)(2,1)S(1)} %pad_maximum_fusion.1), channel_id=1, source_target_pairs={{0,8},{8,16},{16,24},{24,28},{28,20},{20,12},{12,4},{4,0},{2,6},{1... | collective-permute-start | bytes 2949128 | tf_op jit(solution)/shard_map/ppermute | solution.py:495
  29.8 10.3 %collective-permute-start.12 = (bf16[2,600,128]{2,1,0:T(8,128)(2,1)S(1)}, bf16[2,600,128]{2,1,0:T(8,128)(2,1)S(1)}, u32[]{:S(2)}, u32[]{:S(2)}) collective-permute-start(bf16[2,600,128]{2,1,0:T(8,128)(2,1)S(1)} %get-tuple-element.50), channel_id=1, source_target_pairs={{0,1},{1,0},{2,3},{3,2},{4,5},{5,4},{6,7},{7,6},{8,9},{9,8},{10,11... | collective-permute-start | bytes 921608 | tf_op jit(solution)/shard_map/ppermute | solution.py:521
  31.1 11.7 %collective-permute-start.16 = (bf16[1,600,128]{2,1,0:T(8,128)(2,1)S(1)}, bf16[1,600,128]{2,1,0:T(8,128)(2,1)S(1)}, u32[]{:S(2)}, u32[]{:S(2)}) collective-permute-start(bf16[1,600,128]{2,1,0:T(8,128)(2,1)S(1)} %get-tuple-element.53), channel_id=1, source_target_pairs={{0,1},{1,0},{2,3},{3,2},{4,5},{5,4},{6,7},{7,6},{8,9},{9,8},{10,11... | collective-permute-start | bytes 460808 | tf_op jit(solution)/shard_map/ppermute | solution.py:521
  32.0 16.7 %collective-permute-start.5 = (bf16[2,4,480,128]{3,2,1,0:T(8,128)(2,1)S(1)}, bf16[2,4,480,128]{3,2,1,0:T(8,128)(2,1)S(1)}, u32[]{:S(2)}, u32[]{:S(2)}) collective-permute-start(bf16[2,4,480,128]{3,2,1,0:T(8,128)(2,1)S(1)} %pad_maximum_fusion), channel_id=1, source_target_pairs={{0,8},{8,16},{16,24},{24,28},{28,20},{20,12},{12,4},{4,0},{2,6},{1... | collective-permute-start | bytes 2949128 | tf_op jit(solution)/shard_map/ppermute | solution.py:495
  40.9 7.6 %collective-permute-start.13 = (bf16[2,600,128]{2,1,0:T(8,128)(2,1)S(1)}, bf16[2,600,128]{2,1,0:T(8,128)(2,1)S(1)}, u32[]{:S(2)}, u32[]{:S(2)}) collective-permute-start(bf16[2,600,128]{2,1,0:T(8,128)(2,1)S(1)} %get-tuple-element.51), channel_id=1, source_target_pairs={{0,1},{1,0},{2,3},{3,2},{4,5},{5,4},{6,7},{7,6},{8,9},{9,8},{10,11... | collective-permute-start | bytes 921608 | tf_op jit(solution)/shard_map/ppermute | solution.py:521
  45.2 26.6 %collective-permute-start.24 = (bf16[1,2520,256]{2,1,0:T(8,128)(2,1)S(1)}, bf16[1,2520,256]{2,1,0:T(8,128)(2,1)S(1)}, u32[]{:S(2)}, u32[]{:S(2)}) collective-permute-start(bf16[1,2520,256]{2,1,0:T(8,128)(2,1)S(1)} %get-tuple-element.63), channel_id=1, source_target_pairs={{0,2},{2,0},{4,6},{6,4},{8,10},{10,8},{12,14},{14,12},{16,18},{18,... | collective-permute-start | bytes 3870728 | tf_op jit(solution)/shard_map/ppermute | solution.py:495
  45.3 14.1 %collective-permute-start.10 = (bf16[2,4,480,128]{3,2,1,0:T(8,128)(2,1)S(1)}, bf16[2,4,480,128]{3,2,1,0:T(8,128)(2,1)S(1)}, u32[]{:S(2)}, u32[]{:S(2)}) collective-permute-start(bf16[2,4,480,128]{3,2,1,0:T(8,128)(2,1)S(1)} %collective-permute-done.9.refs_0_.refs_2_), channel_id=1, source_target_pairs={{0,8},{8,16},{16,24},{24,28},{28,20},{20,12},{12,4},{4,0},{2,6},{1... | collective-permute-start | bytes 2949128 | tf_op jit(solution)/shard_map/ppermute | solution.py:495
  49.5 8.5 %collective-permute-start.17 = (bf16[2,600,128]{2,1,0:T(8,128)(2,1)S(1)}, bf16[2,600,128]{2,1,0:T(8,128)(2,1)S(1)}, u32[]{:S(2)}, u32[]{:S(2)}) collective-permute-start(bf16[2,600,128]{2,1,0:T(8,128)(2,1)S(1)} %get-tuple-element.58), channel_id=1, source_target_pairs={{0,1},{1,0},{2,3},{3,2},{4,5},{5,4},{6,7},{7,6},{8,9},{9,8},{10,11... | collective-permute-start | bytes 921608 | tf_op jit(solution)/shard_map/ppermute | solution.py:521
  50.8 13.9 %collective-permute-start.6 = (bf16[1,4,480,128]{3,2,1,0:T(8,128)(2,1)S(1)}, bf16[1,4,480,128]{3,2,1,0:T(8,128)(2,1)S(1)}, u32[]{:S(2)}, u32[]{:S(2)}) collective-permute-start(bf16[1,4,480,128]{3,2,1,0:T(8,128)(2,1)S(1)} %slice.12), channel_id=1, source_target_pairs={{0,8},{8,16},{16,24},{24,28},{28,20},{20,12},{12,4},{4,0},{2,6},{1... | collective-permute-start | bytes 1474568 | tf_op jit(solution)/shard_map/ppermute | solution.py:495
  55.8 22.1 %collective-permute-start.22 = (bf16[2,2520,256]{2,1,0:T(8,128)(2,1)S(1)}, bf16[2,2520,256]{2,1,0:T(8,128)(2,1)S(1)}, u32[]{:S(2)}, u32[]{:S(2)}) collective-permute-start(bf16[2,2520,256]{2,1,0:T(8,128)(2,1)S(1)} %get-tuple-element.61), channel_id=1, source_target_pairs={{0,2},{2,0},{4,6},{6,4},{8,10},{10,8},{12,14},{14,12},{16,18},{18,... | collective-permute-start | bytes 7741448 | tf_op jit(solution)/shard_map/ppermute | solution.py:495
  60.2 8.8 %collective-permute-start.23 = (bf16[2,600,128]{2,1,0:T(8,128)(2,1)S(1)}, bf16[2,600,128]{2,1,0:T(8,128)(2,1)S(1)}, u32[]{:S(2)}, u32[]{:S(2)}) collective-permute-start(bf16[2,600,128]{2,1,0:T(8,128)(2,1)S(1)} %get-tuple-element.62), channel_id=1, source_target_pairs={{0,1},{1,0},{2,3},{3,2},{4,5},{5,4},{6,7},{7,6},{8,9},{9,8},{10,11... | collective-permute-start | bytes 921608 | tf_op jit(solution)/shard_map/ppermute | solution.py:521
  61.4 8.9 %collective-permute-start.19 = (bf16[1,4,480,128]{3,2,1,0:T(8,128)(2,1)S(1)}, bf16[1,4,480,128]{3,2,1,0:T(8,128)(2,1)S(1)}, u32[]{:S(2)}, u32[]{:S(2)}) collective-permute-start(bf16[1,4,480,128]{3,2,1,0:T(8,128)(2,1)S(1)} %get-tuple-element.86), channel_id=1, source_target_pairs={{0,8},{8,16},{16,24},{24,28},{28,20},{20,12},{12,4},{4,0},{2,6},{1... | collective-permute-start | bytes 1474568 | tf_op jit(solution)/shard_map/ppermute | solution.py:495
  64.7 11.2 %collective-permute-start.21 = (bf16[1,4,480,128]{3,2,1,0:T(8,128)(2,1)S(1)}, bf16[1,4,480,128]{3,2,1,0:T(8,128)(2,1)S(1)}, u32[]{:S(2)}, u32[]{:S(2)}) collective-permute-start(bf16[1,4,480,128]{3,2,1,0:T(8,128)(2,1)S(1)} %get-tuple-element.85), channel_id=1, source_target_pairs={{0,8},{8,16},{16,24},{24,28},{28,20},{20,12},{12,4},{4,0},{2,6},{1... | collective-permute-start | bytes 1474568 | tf_op jit(solution)/shard_map/ppermute | solution.py:495
  69.1 6.4 %collective-permute-start.25 = (bf16[1,600,128]{2,1,0:T(8,128)(2,1)S(1)}, bf16[1,600,128]{2,1,0:T(8,128)(2,1)S(1)}, u32[]{:S(2)}, u32[]{:S(2)}) collective-permute-start(bf16[1,600,128]{2,1,0:T(8,128)(2,1)S(1)} %get-tuple-element.66), channel_id=1, source_target_pairs={{0,1},{1,0},{2,3},{3,2},{4,5},{5,4},{6,7},{7,6},{8,9},{9,8},{10,11... | collective-permute-start | bytes 460808 | tf_op jit(solution)/shard_map/ppermute | solution.py:559
  70.3 10.5 %collective-permute-start.20 = (bf16[1,4,480,128]{3,2,1,0:T(8,128)(2,1)S(1)}, bf16[1,4,480,128]{3,2,1,0:T(8,128)(2,1)S(1)}, u32[]{:S(2)}, u32[]{:S(2)}) collective-permute-start(bf16[1,4,480,128]{3,2,1,0:T(8,128)(2,1)S(1)} %collective-permute-done.19.refs_0_.refs_1_), channel_id=1, source_target_pairs={{0,8},{8,16},{16,24},{24,28},{28,20},{20,12},{12,4},{4,0},{2,6},{1... | collective-permute-start | bytes 1474568 | tf_op jit(solution)/shard_map/ppermute | solution.py:495
  75.4 6.6 %collective-permute-start.28 = (bf16[2,2520,256]{2,1,0:T(8,128)(2,1)S(1)}, bf16[2,2520,256]{2,1,0:T(8,128)(2,1)S(1)}, u32[]{:S(2)}, u32[]{:S(2)}) collective-permute-start(bf16[2,2520,256]{2,1,0:T(8,128)(2,1)S(1)} %get-tuple-element.71), channel_id=1, source_target_pairs={{0,2},{2,0},{4,6},{6,4},{8,10},{10,8},{12,14},{14,12},{16,18},{18,... | collective-permute-start | bytes 7741448 | tf_op jit(solution)/shard_map/ppermute | solution.py:495
  75.5 9.8 %collective-permute-start.18 = (bf16[1,4,480,128]{3,2,1,0:T(8,128)(2,1)S(1)}, bf16[1,4,480,128]{3,2,1,0:T(8,128)(2,1)S(1)}, u32[]{:S(2)}, u32[]{:S(2)}) collective-permute-start(bf16[1,4,480,128]{3,2,1,0:T(8,128)(2,1)S(1)} %get-tuple-element.60.refs_0_), channel_id=1, source_target_pairs={{0,2},{2,0},{4,6},{6,4},{8,10},{10,8},{12,14},{14,12},{16,18},{18,... | collective-permute-start | bytes 1474568 | tf_op jit(solution)/shard_map/ppermute | solution.py:495
  76.8 10.2 %collective-permute-start.27 = (bf16[2,600,128]{2,1,0:T(8,128)(2,1)S(1)}, bf16[2,600,128]{2,1,0:T(8,128)(2,1)S(1)}, u32[]{:S(2)}, u32[]{:S(2)}) collective-permute-start(bf16[2,600,128]{2,1,0:T(8,128)(2,1)S(1)} %get-tuple-element.70), channel_id=1, source_target_pairs={{0,1},{1,0},{2,3},{3,2},{4,5},{5,4},{6,7},{7,6},{8,9},{9,8},{10,11... | collective-permute-start | bytes 921608 | tf_op jit(solution)/shard_map/ppermute | solution.py:578
  80.7 7.7 %collective-permute-start.29 = (bf16[2,2520,256]{2,1,0:T(8,128)(2,1)S(1)}, bf16[2,2520,256]{2,1,0:T(8,128)(2,1)S(1)}, u32[]{:S(2)}, u32[]{:S(2)}) collective-permute-start(bf16[2,2520,256]{2,1,0:T(8,128)(2,1)S(1)} %get-tuple-element.75), channel_id=1, source_target_pairs={{0,2},{2,0},{4,6},{6,4},{8,10},{10,8},{12,14},{14,12},{16,18},{18,... | collective-permute-start | bytes 7741448 | tf_op jit(solution)/shard_map/ppermute | solution.py:495
  81.5 6.8 %collective-permute-start.26 = (bf16[1,4,480,128]{3,2,1,0:T(8,128)(2,1)S(1)}, bf16[1,4,480,128]{3,2,1,0:T(8,128)(2,1)S(1)}, u32[]{:S(2)}, u32[]{:S(2)}) collective-permute-start(bf16[1,4,480,128]{3,2,1,0:T(8,128)(2,1)S(1)} %get-tuple-element.69.refs_2_), channel_id=1, source_target_pairs={{0,2},{2,0},{4,6},{6,4},{8,10},{10,8},{12,14},{14,12},{16,18},{18,... | collective-permute-start | bytes 1474568 | tf_op jit(solution)/shard_map/ppermute | solution.py:495
  82.0 8.7 %collective-permute-start.30 = (bf16[1,600,128]{2,1,0:T(8,128)(2,1)S(1)}, bf16[1,600,128]{2,1,0:T(8,128)(2,1)S(1)}, u32[]{:S(2)}, u32[]{:S(2)}) collective-permute-start(bf16[1,600,128]{2,1,0:T(8,128)(2,1)S(1)} %get-tuple-element.78), channel_id=1, source_target_pairs={{0,1},{1,0},{2,3},{3,2},{4,5},{5,4},{6,7},{7,6},{8,9},{9,8},{10,11... | collective-permute-start | bytes 460808 | tf_op jit(solution)/shard_map/ppermute | solution.py:559
  88.2 3.0 %collective-permute-start.33 = (bf16[2,600,256]{2,1,0:T(8,128)(2,1)S(1)}, bf16[2,600,256]{2,1,0:T(8,128)(2,1)S(1)}, u32[]{:S(2)}, u32[]{:S(2)}) collective-permute-start(bf16[2,600,256]{2,1,0:T(8,128)(2,1)S(1)} %get-tuple-element.81), channel_id=1, source_target_pairs={{0,2},{2,0},{4,6},{6,4},{8,10},{10,8},{12,14},{14,12},{16,18},{18,... | collective-permute-start | bytes 1843208 | tf_op jit(solution)/shard_map/ppermute | solution.py:495
  90.7 1.6 %collective-permute-start.31 = (bf16[1,600,128]{2,1,0:T(8,128)(2,1)S(1)}, bf16[1,600,128]{2,1,0:T(8,128)(2,1)S(1)}, u32[]{:S(2)}, u32[]{:S(2)}) collective-permute-start(bf16[1,600,128]{2,1,0:T(8,128)(2,1)S(1)} %get-tuple-element.79.refs_0_), channel_id=1, source_target_pairs={{0,2},{2,0},{4,6},{6,4},{8,10},{10,8},{12,14},{14,12},{16,18},{18,... | collective-permute-start | bytes 460808 | tf_op jit(solution)/shard_map/ppermute | solution.py:495
  91.2 1.4 %collective-permute-start.32 = (bf16[1,600,128]{2,1,0:T(8,128)(2,1)S(1)}, bf16[1,600,128]{2,1,0:T(8,128)(2,1)S(1)}, u32[]{:S(2)}, u32[]{:S(2)}) collective-permute-start(bf16[1,600,128]{2,1,0:T(8,128)(2,1)S(1)} %get-tuple-element.80.refs_2_), channel_id=1, source_target_pairs={{0,2},{2,0},{4,6},{6,4},{8,10},{10,8},{12,14},{14,12},{16,18},{18,... | collective-permute-start | bytes 460808 | tf_op jit(solution)/shard_map/ppermute | solution.py:495
